TPU v7x, 256 devices: a whole 4x4x8 slice. The times are simulated.
256 devices in a mesh: date: 4 (over x_lo, core), az: 16 (over z, x_hi), rg: 4 (over y).
Axes of the slice: x: 4 (x_hi: 2, x_lo: 2; x = x_hi * 2 + x_lo), y: 4, z: 8, core: 2. Of those that a mesh axis runs over, the one named last changes fastest.
Arguments:
- reference_slab: bfloat16 [2, 1024, 4, 512], P(None, 'az', 'rg', 'date'), may hold values from -6 to 6
- secondary: bfloat16 [4, 2, 1024, 2048], P('date', None, 'az', 'rg'), may hold values from -6 to 6
- az_shift: int32 [4, 1024], P('date', 'az'), may hold values from -12 to 12
- az_fraction: float32 [4, 1024], P('date', 'az'), as said below
- rg_shift: int32 [4, 2048], P('date', 'rg'), may hold values from -12 to 12
- rg_fraction: float32 [4, 2048], P('date', 'rg'), as said below
Outputs:
- filtered: float32 [4, 2, 1024, 2048], P('date', None, 'az', 'rg')
Inputs may be any that keep to these rules, and one draw needn't show every extreme that they name: `az_fraction`: whole multiples of 1/64, below 1. `rg_fraction`: whole multiples of 1/64, below 1.
All inputs are finite; a program needn't handle non-finite values.
Results may differ from a plain program's by a relative error of at most 0.0031.
The roundings to bfloat16 on the way count: a program that leaves them out, or rounds other values in their place, can miss the bound.
Values may be sent and summed in bfloat16 or wider, within the bound.
No kernel may reach another device: no remote copies, remote signals or barrier semaphores. Data moves between devices by JAX's collectives and lax.ppermute only.
A program may use at most 64 MiB of HBM per device.

v0:
```python
import math

import jax
import jax.numpy as jnp
from jax import lax
from jax.sharding import PartitionSpec as P

PATCH = 64
TAPS = 8
MAXOFF = 12


def padded(shard, sides, width):
    for axis, dim in sides:
        peers, length = (lax.axis_size(axis), shard.shape[dim])
        up = [(i, (i + 1) % peers) for i in range(peers - 1)]
        down = [(j, i) for i, j in up]
        last = lax.slice_in_dim(shard, length - width, length, axis=dim)
        first = lax.slice_in_dim(shard, 0, width, axis=dim)
        before = lax.ppermute(last, axis, up)
        after = lax.ppermute(first, axis, down)
        shard = jnp.concatenate([before, shard, after], axis=dim)
    return shard


def sinc_weights(fraction):
    tap_offset = (jnp.arange(TAPS) - (TAPS // 2 - 1)).astype(fraction.dtype)
    distance = fraction[..., None] - tap_offset
    taper = 0.5 + 0.5 * jnp.cos(jnp.pi * distance / (TAPS // 2))
    return (jnp.sinc(distance) * taper).astype(jnp.bfloat16)


def gather_reference(reference_slab):
    gathered = lax.all_gather(reference_slab, "date", axis=3, tiled=True)
    return gathered.reshape(2, gathered.shape[1], gathered.shape[3])


def band_matrix(weights, shifts, positions, margin, width):
    tap_offset = jnp.arange(TAPS, dtype=jnp.int32) - (TAPS // 2 - 1)
    target = positions[None, :, None] + shifts[:, :, None] + margin + tap_offset
    column = jnp.arange(width, dtype=jnp.int32)
    picked = jnp.where(column == target[..., None], weights.astype(jnp.float32)[..., None], 0.0)
    return jnp.sum(picked, axis=2).astype(jnp.bfloat16)


def resample(extended, az_shift, az_fraction, rg_shift, rg_fraction, margin):
    date_count = extended.shape[0]
    line_count = az_shift.shape[1]
    sample_count = rg_shift.shape[1]
    line_index = jnp.arange(line_count, dtype=jnp.int32)
    az_matrix = band_matrix(
        sinc_weights(az_fraction), az_shift, line_index, margin, line_count + 2 * margin
    )
    az_rows = jnp.einsum(
        "dre,dpec->dprc", az_matrix, extended, preferred_element_type=jnp.float32
    ).astype(jnp.bfloat16)
    block_width = math.gcd(sample_count, 128)
    block_count = sample_count // block_width
    heads = az_rows[..., :sample_count].reshape(date_count, 2, line_count, block_count, block_width)
    tails = jnp.concatenate(
        [heads[:, :, :, 1:, : 2 * margin], az_rows[:, :, :, None, sample_count:]], axis=3
    )
    windows = jnp.concatenate([heads, tails], axis=4)
    sample_index = jnp.arange(sample_count, dtype=jnp.int32) % block_width
    rg_matrix = band_matrix(
        sinc_weights(rg_fraction), rg_shift, sample_index, margin, block_width + 2 * margin
    )
    rg_matrix = rg_matrix.reshape(date_count, block_count, block_width, block_width + 2 * margin)
    resampled = jnp.einsum(
        "dprbc,dbjc->dprbj", windows, rg_matrix, preferred_element_type=jnp.float32
    )
    return resampled.reshape(date_count, 2, line_count, sample_count)


def transform_table(sign):
    integer = jnp.arange(PATCH, dtype=jnp.int32)
    phase = (integer[:, None] * integer[None, :] % PATCH).astype(jnp.float32) * (
        2.0 * jnp.pi / PATCH
    )
    cos_table = jnp.cos(phase)
    sin_table = jnp.sin(phase)
    upper = jnp.concatenate([cos_table, -sign * sin_table], axis=1)
    lower = jnp.concatenate([sign * sin_table, cos_table], axis=1)
    return jnp.concatenate([upper, lower], axis=0)


def along_samples(packed, table):
    return jnp.einsum("damcq,qw->damcw", packed, table, precision=lax.Precision.HIGHEST)


def along_lines(packed, table):
    shape = packed.shape
    split = packed.reshape(shape[0], shape[1], shape[2], shape[3], 2, PATCH)
    lines_table = jnp.transpose(table.reshape(2, PATCH, 2, PATCH), (3, 2, 1, 0))
    moved = jnp.einsum("uymq,damcqn->daucyn", lines_table, split, precision=lax.Precision.HIGHEST)
    return moved.reshape(shape)


def goldstein(extended):
    date_count = extended.shape[0]
    half_size = PATCH // 2
    row_blocks = extended.shape[2] // half_size
    col_blocks = extended.shape[3] // half_size
    pieces = extended.reshape(date_count, 2, row_blocks, half_size, extended.shape[3])
    pieces = jnp.concatenate([pieces[:, :, :-1], pieces[:, :, 1:]], axis=3)
    pieces = pieces.reshape(date_count, 2, row_blocks - 1, PATCH, col_blocks, half_size)
    pieces = jnp.concatenate([pieces[:, :, :, :, :-1], pieces[:, :, :, :, 1:]], axis=5)
    packed = jnp.concatenate([pieces[:, 0], pieces[:, 1]], axis=4)
    forward = transform_table(1.0)
    inverse = transform_table(-1.0)
    packed = along_lines(along_samples(packed, forward), forward)
    real_part = packed[..., :PATCH]
    imag_part = packed[..., PATCH:]
    magnitude = jnp.sqrt(real_part * real_part + imag_part * imag_part)
    smooth = magnitude + jnp.roll(magnitude, 1, axis=4) + jnp.roll(magnitude, -1, axis=4)
    smooth = smooth + jnp.roll(smooth, 1, axis=2) + jnp.roll(smooth, -1, axis=2)
    response = jnp.sqrt(smooth / 9.0)
    gain = response / (jnp.mean(response, axis=(2, 4), keepdims=True) + 1e-06)
    packed = packed * jnp.concatenate([gain, gain], axis=4)
    packed = along_lines(along_samples(packed, inverse), inverse)
    position = jnp.arange(PATCH).astype(jnp.float32)
    taper = jnp.minimum(position + 0.5, PATCH - 0.5 - position) / half_size
    weight_grid = taper[:, None, None] * taper[None, None, :] / (PATCH * PATCH)
    outputs = []
    for values in (packed[..., :PATCH] * weight_grid, packed[..., PATCH:] * weight_grid):
        across = values[:, :, :, 1:, :half_size] + values[:, :, :, :-1, half_size:]
        across = across.reshape(date_count, row_blocks - 1, PATCH, (col_blocks - 2) * half_size)
        down = across[:, 1:, :half_size] + across[:, :-1, half_size:]
        outputs.append(
            down.reshape(date_count, (row_blocks - 2) * half_size, (col_blocks - 2) * half_size)
        )
    return jnp.stack(outputs, axis=1)


def cross_product(master, resampled):
    real_part = master[0] * resampled[:, 0] + master[1] * resampled[:, 1]
    imag_part = master[1] * resampled[:, 0] - master[0] * resampled[:, 1]
    return jnp.stack([real_part, imag_part], axis=1)


def on_device(reference_slab, secondary, az_shift, az_fraction, rg_shift, rg_fraction):
    margin = MAXOFF + 4
    half_size = PATCH // 2
    master_tile = gather_reference(reference_slab)
    extended = padded(secondary, (("az", 2), ("rg", 3)), margin)
    resampled = resample(extended, az_shift, az_fraction, rg_shift, rg_fraction, margin)
    interferogram = cross_product(master_tile.astype(jnp.float32), resampled)
    bordered = padded(interferogram, (("az", 2), ("rg", 3)), half_size)
    return goldstein(bordered)


def solution(mesh):
    in_specs = (
        P(None, "az", "rg", "date"),
        P("date", None, "az", "rg"),
        P("date", "az"),
        P("date", "az"),
        P("date", "rg"),
        P("date", "rg"),
    )
    out_specs = P("date", None, "az", "rg")
    return jax.shard_map(
        on_device, mesh=mesh, in_specs=in_specs, out_specs=out_specs, check_vma=False
    )
```

profile of v0, /device:TPU:110, one launch (start us, length us, event | category | flops | bytes accessed | tf_op | source)
XLA Modules:
  0.0 99.9 jit_solution(15344309040009659886)
XLA Ops:
  0.0 0.8 fusion.119
  0.8 5.9 %collective-permute-start = (bf16[1,2,16,512]{3,2,1,0:T(8,128)(2,1)S(1)}, bf16[1,2,16,512]{3,2,1,0:T(8,128)(2,1)S(1)}, u32[]{:S(2)}, u32[]{:S(2)}) collective-permute-start(bf16[1,2,16,512]{3,2,1,0:T(8,128)(2,1)S(1)} %get-tuple-element.36), channel_id=1, source_target_pairs={{0,4},{4,8},{8,12},{12,16},{16,20},{20,24},{24,28},{28,32},{32,36}... | collective-permute-start | bytes 98312 | tf_op jit(solution)/shard_map/ppermute | solution.py:20
  6.7 1.9 %collective-permute-start.1 = (bf16[1,2,16,512]{3,2,1,0:T(8,128)(2,1)S(1)}, bf16[1,2,16,512]{3,2,1,0:T(8,128)(2,1)S(1)}, u32[]{:S(2)}, u32[]{:S(2)}) collective-permute-start(bf16[1,2,16,512]{3,2,1,0:T(8,128)(2,1)S(1)} %get-tuple-element.35), channel_id=1, source_target_pairs={{4,0},{8,4},{12,8},{16,12},{20,16},{24,20},{28,24},{32,28},{36,32}... | collective-permute-start | bytes 98312 | tf_op jit(solution)/shard_map/ppermute | solution.py:21
  8.6 0.8 fusion.98
  9.5 0.7 fusion.104
  10.1 0.7 fusion.100
  11.0 0.8 fusion.72
  11.8 0.7 multiply_multiply_fusion
  12.5 0.3 select_reduce_fusion
  12.8 0.2 select_reduce_fusion.1
  13.0 0.8 copy.48
  13.9 0.9 constant_dynamic-update-slice_fusion.1
  14.8 1.3 %collective-permute-done.1 = bf16[1,2,16,512]{3,2,1,0:T(8,128)(2,1)S(1)} collective-permute-done((bf16[1,2,16,512]{3,2,1,0:T(8,128)(2,1)S(1)}, bf16[1,2,16,512]{3,2,1,0:T(8,128)(2,1)S(1)}, u32[]{:S(2)}, u32[]{:S(2)}) %collective-permute-start.1) | collective-permute-done | bytes 32800 | tf_op jit(solution)/shard_map/ppermute | solution.py:21
  16.2 3.5 %collective-permute-start.2 = (bf16[1,2,96,16]{3,2,1,0:T(8,128)(2,1)S(1)}, bf16[1,2,96,16]{3,2,1,0:T(8,128)(2,1)S(1)}, u32[]{:S(2)}, u32[]{:S(2)}) collective-permute-start(bf16[1,2,96,16]{3,2,1,0:T(8,128)(2,1)S(1)} %get-tuple-element.33), channel_id=1, source_target_pairs={{0,1},{1,2},{2,3},{4,5},{5,6},{6,7},{8,9},{9,10},{10,11},{12,13},{... | collective-permute-start | bytes 18440 | tf_op jit(solution)/shard_map/ppermute | solution.py:20
  19.7 2.4 %collective-permute-start.3 = (bf16[1,2,96,16]{3,2,1,0:T(8,128)(2,1)S(1)}, bf16[1,2,96,16]{3,2,1,0:T(8,128)(2,1)S(1)}, u32[]{:S(2)}, u32[]{:S(2)}) collective-permute-start(bf16[1,2,96,16]{3,2,1,0:T(8,128)(2,1)S(1)} %get-tuple-element.34), channel_id=1, source_target_pairs={{1,0},{2,1},{3,2},{5,4},{6,5},{7,6},{9,8},{10,9},{11,10},{13,12},{... | collective-permute-start | bytes 18440 | tf_op jit(solution)/shard_map/ppermute | solution.py:21
  22.0 5.5 %all_gather.3 = bf16[2,64,1,512]{3,0,2,1:T(2,128)(2,1)S(1)} all-gather(bf16[2,64,1,128]{3,0,2,1:T(2,128)(2,1)S(1)} %copy.48), channel_id=1, replica_groups=mesh['date'=4,'az'=16,'rg'=4] {'date'}, dimensions={3}, use_global_device_ids=true | all-gather | bytes 163840 | tf_op jit(solution)/shard_map/all_gather | solution.py:34
  27.6 0.3 fusion.16
  28.0 0.2 fusion.21
  28.2 0.2 copy.53
  28.4 0.3 add_bitcast_fusion
  28.7 0.2 fusion.24
  29.0 6.3 %collective-permute-start.4 = (f32[1,2,32,512]{3,0,2,1:T(1,128)S(1)}, f32[1,2,32,512]{3,0,2,1:T(1,128)S(1)}, u32[]{:S(2)}, u32[]{:S(2)}) collective-permute-start(f32[1,2,32,512]{3,0,2,1:T(1,128)S(1)} %get-tuple-element.31), channel_id=1, source_target_pairs={{0,4},{4,8},{8,12},{12,16},{16,20},{20,24},{24,28},{28,32},{32,36}... | collective-permute-start | bytes 393224 | tf_op jit(solution)/shard_map/ppermute | solution.py:20
  35.2 1.9 %collective-permute-start.5 = (f32[1,2,32,512]{3,0,2,1:T(1,128)S(1)}, f32[1,2,32,512]{3,0,2,1:T(1,128)S(1)}, u32[]{:S(2)}, u32[]{:S(2)}) collective-permute-start(f32[1,2,32,512]{3,0,2,1:T(1,128)S(1)} %get-tuple-element.32), channel_id=1, source_target_pairs={{4,0},{8,4},{12,8},{16,12},{20,16},{24,20},{28,24},{32,28},{36,32}... | collective-permute-start | bytes 393224 | tf_op jit(solution)/shard_map/ppermute | solution.py:21
  37.1 0.1 fusion.66
  37.3 0.1 broadcast_multiply_fusion
  37.4 1.1 %collective-permute-done.4 = f32[1,2,32,512]{3,0,2,1:T(1,128)S(1)} collective-permute-done((f32[1,2,32,512]{3,0,2,1:T(1,128)S(1)}, f32[1,2,32,512]{3,0,2,1:T(1,128)S(1)}, u32[]{:S(2)}, u32[]{:S(2)}) %collective-permute-start.4) | collective-permute-done | bytes 131104 | tf_op jit(solution)/shard_map/ppermute | solution.py:20
  38.5 7.7 %collective-permute-done.5 = f32[1,2,32,512]{3,0,2,1:T(1,128)S(1)} collective-permute-done((f32[1,2,32,512]{3,0,2,1:T(1,128)S(1)}, f32[1,2,32,512]{3,0,2,1:T(1,128)S(1)}, u32[]{:S(2)}, u32[]{:S(2)}) %collective-permute-start.5) | collective-permute-done | bytes 131104 | tf_op jit(solution)/shard_map/ppermute | solution.py:21
  46.2 0.4 pad_maximum_fusion.7
  46.6 3.5 %collective-permute-start.6 = (f32[1,2,128,32]{3,0,2,1:T(1,128)S(1)}, f32[1,2,128,32]{3,0,2,1:T(1,128)S(1)}, u32[]{:S(2)}, u32[]{:S(2)}) collective-permute-start(f32[1,2,128,32]{3,0,2,1:T(1,128)S(1)} %get-tuple-element.27), channel_id=1, source_target_pairs={{0,1},{1,2},{2,3},{4,5},{5,6},{6,7},{8,9},{9,10},{10,11},{12,13},{... | collective-permute-start | bytes 98312 | tf_op jit(solution)/shard_map/ppermute | solution.py:20
  50.1 2.4 %collective-permute-start.7 = (f32[1,2,128,32]{3,0,2,1:T(1,128)S(1)}, f32[1,2,128,32]{3,0,2,1:T(1,128)S(1)}, u32[]{:S(2)}, u32[]{:S(2)}) collective-permute-start(f32[1,2,128,32]{3,0,2,1:T(1,128)S(1)} %get-tuple-element.28), channel_id=1, source_target_pairs={{1,0},{2,1},{3,2},{5,4},{6,5},{7,6},{9,8},{10,9},{11,10},{13,12},{... | collective-permute-start | bytes 98312 | tf_op jit(solution)/shard_map/ppermute | solution.py:21
  52.6 0.8 reshape.597
  53.4 0.8 reshape.598
  54.1 2.8 %collective-permute-done.7 = f32[1,2,128,32]{3,0,2,1:T(1,128)S(1)} collective-permute-done((f32[1,2,128,32]{3,0,2,1:T(1,128)S(1)}, f32[1,2,128,32]{3,0,2,1:T(1,128)S(1)}, u32[]{:S(2)}, u32[]{:S(2)}) %collective-permute-start.7) | collective-permute-done | bytes 32800 | tf_op jit(solution)/shard_map/ppermute | solution.py:21
  56.9 4.7 %pad_maximum_fusion.2 = f32[1,2,128,576]{3,0,2,1:T(1,128)S(1)} fusion(f32[1,2,128,32]{3,0,2,1:T(1,128)S(1)} %collective-permute-done.7, f32[1,2,32,512]{3,0,2,1:T(1,128)S(1)} %collective-permute-done.5, f32[1,1,64,512]{3,0,2,1:T(1,128)S(1)} %get-tuple-element.30, f32[1,1,64,512]{3,0,2,1:T(1,128)S(1)} %get-tuple-element.29, ...), kind=kLoop, calls=%fused_computation.35 | loop fusion | flops 737280 | bytes 1179648 | tf_op jit(solution)/shard_map/concatenate | solution.py:22
  61.7 1.6 %fusion.117 = (f32[1,2,3,32,576]{4,0,3,2,1:T(1,128)S(1)}, f32[1,2,3,32,576]{4,0,3,2,1:T(1,128)}) fusion(f32[1,2,4,32,576]{4,0,3,2,1:T(1,128)S(1)} %bitcast.163), kind=kLoop, calls=%fused_computation.193 | loop fusion | bytes 1769472 | tf_op jit(solution)/shard_map/slice | solution.py:105
  63.2 0.7 copy.87
  63.9 1.6 %copy.88 = f32[1,2,3,32,576]{3,4,2,1,0:T(8,128)S(1)} copy(f32[1,2,3,32,576]{4,0,3,2,1:T(1,128)} %get-tuple-element.26) | data formatting | bytes 884736
  65.5 0.5 pad_maximum_fusion
  66.1 2.2 %fusion.110 = (f32[1,2,3,64,17,32]{3,5,4,2,1,0:T(8,128)}, f32[1,2,3,64,17,32]{3,5,4,2,1,0:T(8,128)}) fusion(f32[1,2,3,64,18,32]{3,5,4,2,1,0:T(8,128)S(1)} %bitcast.158), kind=kLoop, calls=%fused_computation.186 | loop fusion | bytes 3342336 | tf_op jit(solution)/shard_map/slice | solution.py:107
  68.2 2.2 %copy.89 = f32[1,2,3,64,17,32]{5,3,4,2,1,0:T(8,128)S(1)} copy(f32[1,2,3,64,17,32]{3,5,4,2,1,0:T(8,128)} %get-tuple-element.11) | data formatting | bytes 1671168
  70.5 3.4 %copy.90 = f32[1,2,3,64,17,32]{5,3,4,2,1,0:T(8,128)} copy(f32[1,2,3,64,17,32]{3,5,4,2,1,0:T(8,128)} %get-tuple-element.12) | data formatting | bytes 1671168
  73.8 2.9 %fusion.5 = (f32[1,3,64,17,64]{4,2,3,1,0:T(8,128)S(1)}, f32[1,3,64,17,64]{4,2,3,1,0:T(8,128)S(1)}) fusion(f32[1,2,3,64,17,32]{5,3,4,2,1,0:T(8,128)S(1)} %copy.89, f32[1,2,3,64,17,32]{5,3,4,2,1,0:T(8,128)} %copy.90), kind=kLoop, calls=%fused_computation.11 | loop fusion | flops 417792 | bytes 3342336 | tf_op jit(solution)/shard_map/squeeze | solution.py:108
  76.8 4.6 %fusion.9 = f32[3,64,17,2,64]{1,4,3,2,0:T(8,128)S(1)} fusion(f32[2,64,128,1,1]{2,1,0,4,3:T(8,128)S(1)} %bitcast.168, f32[1,3,64,17,64]{4,2,3,1,0:T(8,128)S(1)} %get-tuple-element.8, f32[1,3,64,17,64]{4,2,3,1,0:T(8,128)S(1)} %get-tuple-element.7), kind=kOutput, calls=%fused_computation.21 | convolution fusion | flops 642146304 | bytes 3407872 | tf_op jit(solution)/shard_map/damcq,qw->damcw/dot_general | solution.py:88
  81.4 2.9 %fusion.2 = f32[3,17,64,64,2,1]{3,2,5,4,1,0:T(8,128)S(1)} fusion(f32[3,64,17,2,64]{1,4,3,2,0:T(8,128)S(1)} %fusion.9, f32[2,64,2,64]{1,0,3,2:T(2,128)S(1)} %copy-done.5), kind=kOutput, calls=%fused_computation.5 | convolution fusion | flops 641728512 | bytes 3407872 | tf_op jit(solution)/shard_map/uymq,damcqn->daucyn/dot_general | solution.py:95
  84.4 0.6 fusion.7
  85.0 0.5 fusion.113
  85.5 1.0 fusion.12
  86.5 0.6 fusion.111
  87.1 0.6 fusion.112
  87.7 2.1 %fusion.108 = (f32[3,17]{1,0:T(4,128)S(1)}, f32[1,3,64,17,64]{2,4,3,1,0:T(8,128)S(1)}) fusion(f32[1,3,1,17,64]{2,4,3,1,0:T(8,128)S(1)} %get-tuple-element.14, f32[1,3,63,17,64]{2,4,3,1,0:T(8,128)S(1)} %get-tuple-element.16, f32[1,3,64,17,64]{2,4,3,1,0:T(8,128)S(1)} %fusion.12, f32[1,3,63,17,64]{2,4,3,1,0:T(8,128)S(1)} %get-tuple-element.15, ...), kind=kLoop, calls=%fused_computation.185 | loop fusion | flops 1253325 | bytes 3342540 | tf_op jit(solution)/shard_map/reduce_sum | solution.py:118
  89.8 0.2 divide_bitcast_fusion
  90.1 0.9 maximum_multiply_fusion
  91.0 3.2 %fusion.120 = f32[3,64,17,2,64]{1,4,3,2,0:T(8,128)S(1)} fusion(f32[3,64,17,128,1]{1,3,4,2,0:T(8,128)S(1)} %bitcast.160, f32[2,64,128,1,1]{2,1,0,4,3:T(8,128)S(1)} %bitcast.167), kind=kOutput, calls=%fused_computation.196 | convolution fusion | flops 641728512 | bytes 3407872 | tf_op jit(solution)/shard_map/damcq,qw->damcw/dot_general | solution.py:88
  94.2 2.9 %fusion = f32[3,17,64,64,2,1]{3,2,5,4,1,0:T(8,128)S(1)} fusion(f32[3,64,17,2,64]{1,4,3,2,0:T(8,128)S(1)} %fusion.120, f32[2,64,2,64]{1,0,3,2:T(2,128)S(1)} %copy-done.4), kind=kOutput, calls=%fused_computation.3 | convolution fusion | flops 641728512 | bytes 3407872 | tf_op jit(solution)/shard_map/uymq,damcqn->daucyn/dot_general | solution.py:95
  97.2 0.5 slice_multiply_fusion.1
  97.7 0.1 slice_add_fusion.1
  97.8 0.2 fusion.115
  98.0 0.2 copy.91
  98.2 0.2 copy.92
  98.4 0.1 slice_add_fusion
  98.5 0.2 fusion.116
  98.7 0.2 copy.93
  98.9 0.2 copy.94
  99.1 0.7 pad_maximum_fusion.3
  (37 shorter events, 0.7 us)
Async XLA Ops:
  0.8 13.1 %collective-permute-start = (bf16[1,2,16,512]{3,2,1,0:T(8,128)(2,1)S(1)}, bf16[1,2,16,512]{3,2,1,0:T(8,128)(2,1)S(1)}, u32[]{:S(2)}, u32[]{:S(2)}) collective-permute-start(bf16[1,2,16,512]{3,2,1,0:T(8,128)(2,1)S(1)} %get-tuple-element.36), channel_id=1, source_target_pairs={{0,4},{4,8},{8,12},{12,16},{16,20},{20,24},{24,28},{28,32},{32,36}... | collective-permute-start | bytes 98312 | tf_op jit(solution)/shard_map/ppermute | solution.py:20
  6.7 9.4 %collective-permute-start.1 = (bf16[1,2,16,512]{3,2,1,0:T(8,128)(2,1)S(1)}, bf16[1,2,16,512]{3,2,1,0:T(8,128)(2,1)S(1)}, u32[]{:S(2)}, u32[]{:S(2)}) collective-permute-start(bf16[1,2,16,512]{3,2,1,0:T(8,128)(2,1)S(1)} %get-tuple-element.35), channel_id=1, source_target_pairs={{4,0},{8,4},{12,8},{16,12},{20,16},{24,20},{28,24},{32,28},{36,32}... | collective-permute-start | bytes 98312 | tf_op jit(solution)/shard_map/ppermute | solution.py:21
  16.2 11.4 %collective-permute-start.2 = (bf16[1,2,96,16]{3,2,1,0:T(8,128)(2,1)S(1)}, bf16[1,2,96,16]{3,2,1,0:T(8,128)(2,1)S(1)}, u32[]{:S(2)}, u32[]{:S(2)}) collective-permute-start(bf16[1,2,96,16]{3,2,1,0:T(8,128)(2,1)S(1)} %get-tuple-element.33), channel_id=1, source_target_pairs={{0,1},{1,2},{2,3},{4,5},{5,6},{6,7},{8,9},{9,10},{10,11},{12,13},{... | collective-permute-start | bytes 18440 | tf_op jit(solution)/shard_map/ppermute | solution.py:20
  19.7 7.9 %collective-permute-start.3 = (bf16[1,2,96,16]{3,2,1,0:T(8,128)(2,1)S(1)}, bf16[1,2,96,16]{3,2,1,0:T(8,128)(2,1)S(1)}, u32[]{:S(2)}, u32[]{:S(2)}) collective-permute-start(bf16[1,2,96,16]{3,2,1,0:T(8,128)(2,1)S(1)} %get-tuple-element.34), channel_id=1, source_target_pairs={{1,0},{2,1},{3,2},{5,4},{6,5},{7,6},{9,8},{10,9},{11,10},{13,12},{... | collective-permute-start | bytes 18440 | tf_op jit(solution)/shard_map/ppermute | solution.py:21
  29.0 9.6 %collective-permute-start.4 = (f32[1,2,32,512]{3,0,2,1:T(1,128)S(1)}, f32[1,2,32,512]{3,0,2,1:T(1,128)S(1)}, u32[]{:S(2)}, u32[]{:S(2)}) collective-permute-start(f32[1,2,32,512]{3,0,2,1:T(1,128)S(1)} %get-tuple-element.31), channel_id=1, source_target_pairs={{0,4},{4,8},{8,12},{12,16},{16,20},{20,24},{24,28},{28,32},{32,36}... | collective-permute-start | bytes 393224 | tf_op jit(solution)/shard_map/ppermute | solution.py:20
  35.2 11.0 %collective-permute-start.5 = (f32[1,2,32,512]{3,0,2,1:T(1,128)S(1)}, f32[1,2,32,512]{3,0,2,1:T(1,128)S(1)}, u32[]{:S(2)}, u32[]{:S(2)}) collective-permute-start(f32[1,2,32,512]{3,0,2,1:T(1,128)S(1)} %get-tuple-element.32), channel_id=1, source_target_pairs={{4,0},{8,4},{12,8},{16,12},{20,16},{24,20},{28,24},{32,28},{36,32}... | collective-permute-start | bytes 393224 | tf_op jit(solution)/shard_map/ppermute | solution.py:21
  46.6 7.6 %collective-permute-start.6 = (f32[1,2,128,32]{3,0,2,1:T(1,128)S(1)}, f32[1,2,128,32]{3,0,2,1:T(1,128)S(1)}, u32[]{:S(2)}, u32[]{:S(2)}) collective-permute-start(f32[1,2,128,32]{3,0,2,1:T(1,128)S(1)} %get-tuple-element.27), channel_id=1, source_target_pairs={{0,1},{1,2},{2,3},{4,5},{5,6},{6,7},{8,9},{9,10},{10,11},{12,13},{... | collective-permute-start | bytes 98312 | tf_op jit(solution)/shard_map/ppermute | solution.py:20
  50.1 6.9 %collective-permute-start.7 = (f32[1,2,128,32]{3,0,2,1:T(1,128)S(1)}, f32[1,2,128,32]{3,0,2,1:T(1,128)S(1)}, u32[]{:S(2)}, u32[]{:S(2)}) collective-permute-start(f32[1,2,128,32]{3,0,2,1:T(1,128)S(1)} %get-tuple-element.28), channel_id=1, source_target_pairs={{1,0},{2,1},{3,2},{5,4},{6,5},{7,6},{9,8},{10,9},{11,10},{13,12},{... | collective-permute-start | bytes 98312 | tf_op jit(solution)/shard_map/ppermute | solution.py:21
  52.6 10.7 %copy-start = (f32[128,128]{0,1:T(8,128)}, f32[128,128]{0,1:T(8,128)S(1)}, u32[]{:S(2)}) copy-start(f32[128,128]{0,1:T(8,128)S(1)} %get-tuple-element.37) | copy-start | bytes 196612
  52.6 10.7 %copy-start.2 = (f32[128,128]{0,1:T(8,128)}, f32[128,128]{0,1:T(8,128)S(1)}, u32[]{:S(2)}) copy-start(f32[128,128]{0,1:T(8,128)S(1)} %get-tuple-element.38) | copy-start | bytes 196612
  73.8 2.9 %copy-start.3 = (f32[128,128]{0,1:T(8,128)S(1)}, f32[128,128]{0,1:T(8,128)}, u32[]{:S(2)}) copy-start(f32[128,128]{0,1:T(8,128)} %copy-done.2) | copy-start | bytes 196612
  76.8 4.7 %copy-start.5 = (f32[2,64,2,64]{1,0,3,2:T(2,128)S(1)}, f32[2,64,2,64]{1,0,3,2:T(2,128)}, u32[]{:S(2)}) copy-start(f32[2,64,2,64]{1,0,3,2:T(2,128)} %reshape.597) | copy-start | bytes 196612
  90.1 0.9 copy-start.1
  91.0 3.3 %copy-start.4 = (f32[2,64,2,64]{1,0,3,2:T(2,128)S(1)}, f32[2,64,2,64]{1,0,3,2:T(2,128)}, u32[]{:S(2)}) copy-start(f32[2,64,2,64]{1,0,3,2:T(2,128)} %reshape.598) | copy-start | bytes 196612
  94.2 3.0 %copy-start.6 = (f32[64,64]{0,1:T(8,128)S(1)}, f32[64,64]{0,1:T(8,128)}, u32[]{:S(2)}) copy-start(f32[64,64]{0,1:T(8,128)} %multiply_multiply_fusion) | copy-start | bytes 49156
where the time goes:
time: 100 us; the launch traced here: 99.9 us
  starting transfers between devices  27.7 us (28%)
  other arithmetic  20.2 us (20%)
  local copies, waits for them, and re-layouts  19 us (19%)
  matrix products  14.2 us (14%)
  waiting for transfers between devices  12.9 us (13%)
  blocking collectives  5.46 us (5%)
    ppermute x4, starting transfers between devices, padded(): before = lax.ppermute(last, axis, up)  19.1 us
    ppermute x4, waiting for transfers between devices, padded(): after = lax.ppermute(first, axis, down)  11.8 us
    unnamed x25, local copies, waits for them, and re-layouts  10.3 us
    ppermute x4, starting transfers between devices, padded(): after = lax.ppermute(first, axis, down)  8.56 us
    dot_general x2, matrix products, along_samples(): jnp.einsum('damcq,qw->damcw', packed, table, precision=lax.Precision.HIGH...  7.87 us
    dot_general x2, matrix products, along_lines(): jnp.einsum('uymq,damcqn->daucyn', lines_table, split, precision=lax.Preci...  5.87 us
    all_gather x1, blocking collectives, gather_reference(): gathered = lax.all_gather(reference_slab, 'date', axis=3, tiled=True)  5.46 us
    concatenate x1, other arithmetic, padded(): shard = jnp.concatenate([before, shard, after], axis=dim)  4.71 us
  transfers between devices with their start and end apart: 8, of which 4 were waited for; matrix products, arithmetic and copies ran while one was open for 8% of the time, Pallas kernels for 0%

commit v1 on v0

v1 whole, which is shorter than its diff:
```python
import functools

import jax
import jax.numpy as jnp
import ml_dtypes
import numpy as np
from jax import lax
from jax.experimental import pallas as pl
from jax.experimental.pallas import tpu as pltpu
from jax.sharding import PartitionSpec as P

PATCH = 64
HALF = 32
TAPS = 8
MARGIN = 48
LINES_DEV = 64
SAMPLES_DEV = 512
BF = jnp.bfloat16
F32 = jnp.float32
VMEM_LIMIT = 32 * 1024 * 1024


def split_table(table):
    high = table.astype(ml_dtypes.bfloat16)
    low = (table - high.astype(np.float64)).astype(ml_dtypes.bfloat16)
    return high, low


def hann(position):
    return np.minimum(position + 0.5, PATCH - 0.5 - position) / HALF


def sample_forward():
    table = np.zeros((2, 128, 2, 64, 2))
    v = np.arange(64)
    for p in range(2):
        for m in range(64):
            angle = 2 * np.pi * ((v * m) % 64) / 64
            n = m + 32 * p
            table[0, n, 0, :, p] = np.cos(angle)
            table[1, n, 0, :, p] = np.sin(angle)
            table[0, n, 1, :, p] = -np.sin(angle)
            table[1, n, 1, :, p] = np.cos(angle)
    return table.reshape(256, 256)


def line_forward():
    table = np.zeros((3, 2, 64, 2, 128))
    u = np.arange(64)
    for band in range(3):
        for m in range(64):
            angle = 2 * np.pi * ((u * m) % 64) / 64
            i = m + 32 * band
            table[band, 0, :, 0, i] = np.cos(angle)
            table[band, 0, :, 1, i] = np.sin(angle)
            table[band, 1, :, 0, i] = -np.sin(angle)
            table[band, 1, :, 1, i] = np.cos(angle)
    return table.reshape(384, 256)


def line_inverse():
    table = np.zeros((2, 64, 3, 2, 64))
    u = np.arange(64)
    for band in range(3):
        for y in range(64):
            m = y + 32 - 32 * band
            if 0 <= m < 64:
                angle = 2 * np.pi * ((u * m) % 64) / 64
                weight = hann(m) / 64
                table[0, y, band, 0, :] = weight * np.cos(angle)
                table[0, y, band, 1, :] = -weight * np.sin(angle)
                table[1, y, band, 0, :] = weight * np.sin(angle)
                table[1, y, band, 1, :] = weight * np.cos(angle)
    return table.reshape(128, 384)


def sample_inverse(start):
    table = np.zeros((2, 64, 2, 2, 128))
    v = np.arange(64)
    for p in range(2):
        for y in range(128):
            n = 32 + y - start - 32 * p
            if 0 <= n < 64:
                angle = 2 * np.pi * ((v * n) % 64) / 64
                weight = hann(n) / 64
                table[0, :, p, 0, y] = weight * np.cos(angle)
                table[1, :, p, 0, y] = -weight * np.sin(angle)
                table[0, :, p, 1, y] = weight * np.sin(angle)
                table[1, :, p, 1, y] = weight * np.cos(angle)
    return table.reshape(256, 256)


def filter_tables():
    inverse = np.stack([sample_inverse(start) for start in (0, 64, 128, 96)])
    tables = []
    for table in (sample_forward(), line_forward(), line_inverse(), inverse):
        tables.extend(split_table(table))
    return tables


def sinc_rows(fraction):
    tap = lax.broadcasted_iota(jnp.int32, (TAPS, fraction.shape[1]), 0)
    distance = fraction - (tap - (TAPS // 2 - 1)).astype(F32)
    centre = distance == 0.0
    sign = jnp.where(tap % 2 == 1, 1.0, -1.0)
    wave = sign * jnp.sin(np.float32(np.pi) * fraction)
    sinc = wave / jnp.where(centre, 1.0, np.float32(np.pi) * distance)
    sinc = jnp.where(centre, 1.0, sinc)
    taper = 0.5 + 0.5 * jnp.cos(np.float32(np.pi) * distance / (TAPS // 2))
    return (sinc * taper).astype(BF).astype(F32)


def kernel_rows(shift, fraction):
    weights = sinc_rows(fraction)
    row = lax.broadcasted_iota(jnp.int32, weights.shape, 0)
    shifts = jnp.where(row == 0, shift.astype(F32), 0.0)
    return jnp.concatenate([weights, shifts], axis=0)


def band_matrix(rows, depth):
    width = rows.shape[1]
    shift = rows[TAPS : TAPS + 1].astype(jnp.int32)
    source = lax.broadcasted_iota(jnp.int32, (depth, width), 0)
    target = lax.broadcasted_iota(jnp.int32, (depth, width), 1)
    step = source - (target + 13 + shift)
    matrix = jnp.zeros((depth, width), F32)
    for k in range(TAPS):
        matrix = jnp.where(step == k, rows[k : k + 1], matrix)
    return matrix


def split(values):
    high = values.astype(BF)
    return high, (values - high.astype(F32)).astype(BF)


def dot(left, right):
    return jnp.dot(left, right, preferred_element_type=F32)


def dot_table(values, high, low):
    values_high, values_low = split(values)
    return dot(values_high, high) + dot(values_low, high) + dot(values_high, low)


def table_dot(high, low, values):
    values_high, values_low = split(values)
    return dot(high, values_high) + dot(high, values_low) + dot(low, values_high)


def pack_body(secondary, own, peer1, peer2, peer3, shift, fraction, first, second, reference, line_rows):
    date = lax.axis_index("date")
    odd = lax.axis_index("az") % 2 == 1
    pieces = (own, peer1, peer2, peer3)
    for value in range(4):

        @pl.when(date == value)
        def _():
            for offset in range(4):
                place = value ^ offset
                reference[:, :, place * 128 : place * 128 + 128] = pieces[offset][...]

    row_shift = jnp.concatenate([shift[...], shift[...]], axis=1)
    row_fraction = jnp.concatenate([fraction[...], fraction[...]], axis=1)
    rows = kernel_rows(pltpu.roll(row_shift, 32, 1), pltpu.roll(row_fraction, 32, 1))
    line_rows[...] = rows
    rows = rows.astype(BF)

    def fill(message, sec_start, ref_start):
        for part in range(2):
            message[part * 48 : part * 48 + 48] = secondary[0, part, sec_start : sec_start + 48]
            message[96 + part * 32 : 128 + part * 32] = reference[part, ref_start : ref_start + 32]
        message[160:176, 0:128] = rows
        message[160:176, 128:512] = jnp.zeros((16, 384), BF)

    @pl.when(odd)
    def _():
        fill(first, 0, 0)
        fill(second, 16, 32)

    @pl.when(jnp.logical_not(odd))
    def _():
        fill(first, 16, 32)
        fill(second, 0, 0)


def lines_body(secondary, reference, line_rows, first, second, shift, fraction,
               rows_out, master, sample_rows, send_first, send_second, extended, halo_rows):
    az = lax.axis_index("az")
    odd = az % 2 == 1
    has_top = az > 0
    has_bottom = az < lax.axis_size("az") - 1

    def place(top, bottom):
        for part in range(2):
            extended[part, 0:48] = top[part * 48 : part * 48 + 48]
            extended[part, 112:160] = bottom[part * 48 : part * 48 + 48]
            master[part * 128 : part * 128 + 32] = top[96 + part * 32 : 128 + part * 32]
            master[part * 128 + 96 : part * 128 + 128] = bottom[96 + part * 32 : 128 + part * 32]
        halo_rows[0] = top[160:176, 0:128].astype(F32)
        halo_rows[1] = bottom[160:176, 0:128].astype(F32)

    @pl.when(odd)
    def _():
        place(first, second)

    @pl.when(jnp.logical_not(odd))
    def _():
        place(second, first)

    for part in range(2):
        extended[part, 48:112] = secondary[0, part]
        master[part * 128 + 32 : part * 128 + 96] = reference[part]

    @pl.when(jnp.logical_not(has_top))
    def _():
        for part in range(2):
            master[part * 128 : part * 128 + 32] = jnp.zeros((32, 512), BF)
            extended[part, 0:48] = jnp.zeros((48, 512), BF)

    @pl.when(jnp.logical_not(has_bottom))
    def _():
        for part in range(2):
            master[part * 128 + 96 : part * 128 + 128] = jnp.zeros((32, 512), BF)
            extended[part, 112:160] = jnp.zeros((48, 512), BF)

    lane = lax.broadcasted_iota(jnp.int32, (16, 128), 1)
    rows = jnp.where(
        lane < 32,
        pltpu.roll(halo_rows[0], 64, 1),
        jnp.where(lane < 96, line_rows[...], pltpu.roll(halo_rows[1], 64, 1)),
    )
    matrix = band_matrix(rows, 160).astype(BF)
    for part in range(2):
        values = lax.dot_general(
            matrix, extended[part], (((0,), (0,)), ((), ())), preferred_element_type=F32
        )
        rows_out[part * 128 : part * 128 + 128] = values.astype(BF)

    samples = kernel_rows(shift[...], fraction[...])
    sample_rows[...] = samples
    lane = lax.broadcasted_iota(jnp.int32, (256, 128), 1)
    to_right = jnp.where(
        lane < 48,
        pltpu.roll(rows_out[:, 384:512].astype(F32), 48, 1),
        master[:, 384:512].astype(F32),
    ).astype(BF)
    to_left = jnp.where(
        lane >= 80,
        pltpu.roll(rows_out[:, 0:128].astype(F32), 80, 1),
        master[:, 0:128].astype(F32),
    ).astype(BF)
    right_rows = samples[:, 384:512].astype(BF)
    left_rows = samples[:, 0:128].astype(BF)
    rg_odd = lax.axis_index("rg") % 2 == 1

    @pl.when(rg_odd)
    def _():
        send_first[0:256] = to_left
        send_first[256:272] = left_rows
        send_second[0:256] = to_right
        send_second[256:272] = right_rows

    @pl.when(jnp.logical_not(rg_odd))
    def _():
        send_first[0:256] = to_right
        send_first[256:272] = right_rows
        send_second[0:256] = to_left
        send_second[256:272] = left_rows


def shifted(tiles, start):
    index, offset = start // 128, start % 128
    here = pltpu.roll(tiles[index], 128 - offset, 1)
    after = pltpu.roll(tiles[min(index + 1, 3)], 128 - offset, 1)
    lane = lax.broadcasted_iota(jnp.int32, here.shape, 1)
    return jnp.where(lane < 128 - offset, here, after)


def lane_sum(values):
    for step in (2, 4, 8, 16, 32, 64):
        values = values + pltpu.roll(values, step, 1)
    return values


def block_spectrum(window, master, rows, forward):
    matrix = band_matrix(rows, 128).astype(BF)
    resampled = dot(window.astype(BF), matrix)
    real, imag = resampled[:128], resampled[128:]
    product = jnp.concatenate(
        [master[:128] * real + master[128:] * imag, master[128:] * real - master[:128] * imag],
        axis=1,
    )
    columns = dot_table(product, forward[0][...], forward[1][...])
    return jnp.concatenate([columns[:, :128], columns[:, 128:]], axis=0)


def filter_spectrum(spectrum, single):
    parts = []
    for band in range(3):
        real = spectrum[band * 128 : band * 128 + 64]
        imag = spectrum[band * 128 + 64 : band * 128 + 128]
        smooth = jnp.sqrt(real * real + imag * imag)
        smooth = smooth + pltpu.roll(smooth, 2, 1) + pltpu.roll(smooth, 126, 1)
        smooth = smooth + pltpu.roll(smooth, 1, 0) + pltpu.roll(smooth, 63, 0)
        response = jnp.sqrt(smooth * np.float32(1 / 9))
        mean = lane_sum(jnp.sum(response, axis=0, keepdims=True)) * np.float32(1 / 4096)
        scale = 1.0 / (mean + 1e-06)
        if single:
            lane = lax.broadcasted_iota(jnp.int32, scale.shape, 1)
            scale = jnp.where(lane % 2 == 0, scale, 0.0)
        gain = response * scale
        parts.extend([real * gain, imag * gain])
    return jnp.concatenate(parts, axis=0)


def filter_blocks(columns, singles, lines, inverse):
    spectrum = table_dot(lines[0][...], lines[1][...], jnp.concatenate(columns, axis=1))
    gained = jnp.concatenate(
        [
            filter_spectrum(spectrum[:, at * 128 : at * 128 + 128], single)
            for at, single in enumerate(singles)
        ],
        axis=1,
    )
    back = table_dot(inverse[0][...], inverse[1][...], gained)
    result = []
    for at in range(len(singles)):
        tile = back[:, at * 128 : at * 128 + 128]
        result.append(jnp.concatenate([tile[:64], tile[64:]], axis=1))
    return result


def filter_body(rows_in, master, sample_rows, first, second, *refs):
    forward, lines, inverse, samples = refs[0:2], refs[2:4], refs[4:6], refs[6:8]
    out = refs[8]
    rg = lax.axis_index("rg")
    odd = rg % 2 == 1
    left_scale = jnp.where(rg > 0, 1.0, 0.0).astype(F32)
    right_scale = jnp.where(rg < lax.axis_size("rg") - 1, 1.0, 0.0).astype(F32)

    row_tiles = [rows_in[:, t * 128 : t * 128 + 128].astype(F32) for t in range(4)]
    master_tiles = [master[:, t * 128 : t * 128 + 128].astype(F32) for t in range(4)]
    sample_tiles = [sample_rows[:, t * 128 : t * 128 + 128] for t in range(4)]

    def interior(j):
        return block_spectrum(
            shifted(row_tiles, 64 * j - 48),
            shifted(master_tiles, 64 * j - 32),
            shifted(sample_tiles, 64 * j - 32),
            forward,
        )

    def contribute(values, block, which):
        return dot_table(values, samples[0][which], samples[1][which])

    totals = [None] * 4

    def add(block, which, values):
        part = contribute(values, block, which)
        totals[block] = part if totals[block] is None else totals[block] + part

    for group in ((1, 2), (3, 4), (5, 6), (7,)):
        columns = [interior(j) for j in group]
        results = filter_blocks(columns, [j == 7 for j in group], lines, inverse)
        for j, values in zip(group, results):
            if j % 2 == 1:
                add(j // 2, 1, values)
            else:
                add(j // 2, 0, values)
                add(j // 2 - 1, 2, values)

    first_f = first[...].astype(F32)
    second_f = second[...].astype(F32)
    from_left = jnp.where(odd, first_f, second_f)
    from_right = jnp.where(odd, second_f, first_f)

    def mixed(lane_count, halo, own, reverse):
        lane = lax.broadcasted_iota(jnp.int32, own.shape, 1)
        return jnp.where(lane >= lane_count if reverse else lane < lane_count, halo, own)

    left = block_spectrum(
        mixed(48, from_left[:256] * left_scale, pltpu.roll(row_tiles[0], 48, 1), False),
        mixed(32, pltpu.roll(from_left[:256], 32, 1) * left_scale, pltpu.roll(master_tiles[0], 32, 1), False),
        mixed(32, pltpu.roll(from_left[256:], 32, 1), pltpu.roll(sample_tiles[0], 32, 1), False),
        forward,
    )
    right = block_spectrum(
        mixed(80, from_right[:256] * right_scale, pltpu.roll(row_tiles[3], 80, 1), True),
        mixed(64, pltpu.roll(from_right[:256], 64, 1) * right_scale, pltpu.roll(master_tiles[3], 64, 1), True),
        mixed(64, pltpu.roll(from_right[256:], 64, 1), pltpu.roll(sample_tiles[3], 64, 1), True),
        forward,
    )
    results = filter_blocks([left, right], [False, False], lines, inverse)
    add(0, 0, results[0])
    add(3, 3, results[1])
    for block in range(4):
        out[0, 0, :, block * 128 : block * 128 + 128] = totals[block][:, :128]
        out[0, 1, :, block * 128 : block * 128 + 128] = totals[block][:, 128:]


def call(body, outputs, scratch=()):
    vmem = pl.BlockSpec(memory_space=pltpu.VMEM)
    return lambda *args: pl.pallas_call(
        body,
        out_shape=[jax.ShapeDtypeStruct(shape, kind) for shape, kind in outputs],
        in_specs=[vmem] * len(args),
        out_specs=[vmem] * len(outputs),
        scratch_shapes=list(scratch),
        compiler_params=pltpu.CompilerParams(vmem_limit_bytes=VMEM_LIMIT),
    )(*args)


def swaps(size):
    first = [(i, i ^ 1) for i in range(size)]
    second = [(i, (i + 1) % size if i % 2 == 1 else (i - 1) % size) for i in range(size)]
    return first, second


def exchange(first, second, axis):
    pairs = swaps(lax.axis_size(axis))
    received_second = lax.ppermute(second, axis, pairs[1])
    received_first = lax.ppermute(first, axis, pairs[0])
    return received_first, received_second


def on_device(reference_slab, secondary, az_shift, az_fraction, rg_shift, rg_fraction):
    own = reference_slab.reshape(2, LINES_DEV, 128)
    peers = [lax.ppermute(own, "date", [(i, i ^ k) for i in range(4)]) for k in (1, 2, 3)]
    first, second, reference, line_rows = call(
        pack_body,
        [((176, 512), BF), ((176, 512), BF), ((2, LINES_DEV, 512), BF), ((16, 128), F32)],
    )(secondary, own, *peers, az_shift, az_fraction)
    first, second = exchange(first, second, "az")
    rows, master, sample_rows, first, second = call(
        lines_body,
        [((256, 512), BF), ((256, 512), BF), ((16, 512), F32), ((272, 128), BF), ((272, 128), BF)],
        [pltpu.VMEM((2, 160, 512), BF), pltpu.VMEM((2, 16, 128), F32)],
    )(secondary, reference, line_rows, first, second, rg_shift, rg_fraction)
    first, second = exchange(first, second, "rg")
    tables = [jnp.asarray(table) for table in filter_tables()]
    return call(filter_body, [((1, 2, LINES_DEV, SAMPLES_DEV), F32)])(
        rows, master, sample_rows, first, second, *tables
    )[0]


def solution(mesh):
    in_specs = (
        P(None, "az", "rg", "date"),
        P("date", None, "az", "rg"),
        P("date", "az"),
        P("date", "az"),
        P("date", "rg"),
        P("date", "rg"),
    )
    out_specs = P("date", None, "az", "rg")
    return jax.shard_map(
        on_device, mesh=mesh, in_specs=in_specs, out_specs=out_specs, check_vma=False
    )
```

time: 100 us -> 44.5 us (0.45)
  the two profiles are of different devices: /device:TPU:110 before, /device:TPU:2 now
where the time goes in v1:
time: 44.5 us; the launch traced here: 44.1 us
  starting transfers between devices  15 us (34%)
  Pallas kernels  11.1 us (25%)
  waiting for transfers between devices  10.2 us (23%)
  local copies, waits for them, and re-layouts  7.69 us (17%)
    pallas_call x3, Pallas kernels, call(): pl.pallas_call(body, out_shape=[jax.ShapeDtypeStruct(shape, kind) for sha...  11.1 us
    ppermute x2, starting transfers between devices, exchange(): received_second = lax.ppermute(second, axis, pairs[1])  8.89 us
    unnamed x28, local copies, waits for them, and re-layouts  7.69 us
    ppermute x2, waiting for transfers between devices, exchange(): received_second = lax.ppermute(second, axis, pairs[1])  6.21 us
    ppermute x2, starting transfers between devices, exchange(): received_first = lax.ppermute(first, axis, pairs[0])  3.74 us
    ppermute x3, starting transfers between devices, on_device(): lax.ppermute(own, 'date', [(i, i ^ k) for i in range(4)])  2.38 us
    ppermute x3, waiting for transfers between devices, on_device(): lax.ppermute(own, 'date', [(i, i ^ k) for i in range(4)])  2.34 us
    ppermute x2, waiting for transfers between devices, exchange(): received_first = lax.ppermute(first, axis, pairs[0])  1.66 us
  transfers between devices with their start and end apart: 7, of which 6 were waited for; matrix products, arithmetic and copies ran while one was open for 0% of the time, Pallas kernels for 0%

profile of v1, /device:TPU:2, one launch (start us, length us, event | category | flops | bytes accessed | tf_op | source)
XLA Modules:
  0.0 44.1 jit_solution(8822780191337187301)
XLA Ops:
  0.0 0.0 copy-start.13
  0.0 0.0 copy-start.12
  0.0 0.0 collective-permute-start.2
  0.0 2.3 %collective-permute-start.1 = (bf16[2,64,128]{2,1,0:T(8,128)(2,1)}, bf16[2,64,128]{2,1,0:T(8,128)(2,1)S(1)}, u32[]{:S(2)}, u32[]{:S(2)}) collective-permute-start(bf16[2,64,128]{2,1,0:T(8,128)(2,1)} %bitcast.2), channel_id=1, source_target_pairs={{0,128},{64,192},{128,0},{192,64},{1,129},{65,193},{129,1},{193,65... | collective-permute-start | bytes 98312 | tf_op jit(solution)/shard_map/ppermute | solution.py:429
  2.3 0.1 collective-permute-start
  2.4 1.2 %collective-permute-done.2.peer3 = bf16[2,64,128]{2,1,0:T(8,128)(2,1)S(1)} collective-permute-done((bf16[2,64,128]{2,1,0:T(8,128)(2,1)}, bf16[2,64,128]{2,1,0:T(8,128)(2,1)S(1)}, u32[]{:S(2)}, u32[]{:S(2)}) %collective-permute-start.2) | collective-permute-done | bytes 32800 | tf_op jit(solution)/shard_map/ppermute | solution.py:429
  3.6 1.2 %collective-permute-done.1.peer2 = bf16[2,64,128]{2,1,0:T(8,128)(2,1)S(1)} collective-permute-done((bf16[2,64,128]{2,1,0:T(8,128)(2,1)}, bf16[2,64,128]{2,1,0:T(8,128)(2,1)S(1)}, u32[]{:S(2)}, u32[]{:S(2)}) %collective-permute-start.1) | collective-permute-done | bytes 32800 | tf_op jit(solution)/shard_map/ppermute | solution.py:429
  4.7 0.0 collective-permute-done.peer1
  4.7 0.0 copy-done.13
  4.7 0.0 copy-done.12
  4.7 0.0 copy-start
  4.8 0.9 %copy-done = bf16[1,2,64,512]{3,2,1,0:T(8,128)(2,1)S(1)} copy-done((bf16[1,2,64,512]{3,2,1,0:T(8,128)(2,1)S(1)}, bf16[1,2,64,512]{3,2,1,0:T(8,128)(2,1)}, u32[]{:S(2)}) %copy-start) | copy-done | bytes 131096
  5.6 0.0 copy-start.9
  5.6 0.8 %copy-done.9 = bf16[2,64,1,128]{3,1,2,0:T(8,128)(2,1)S(1)} copy-done((bf16[2,64,1,128]{3,1,2,0:T(8,128)(2,1)S(1)}, bf16[2,64,1,128]{3,1,2,0:T(8,128)(2,1)}, u32[]{:S(2)}) %copy-start.9) | copy-done | bytes 32792
  6.4 0.0 copy-start.1
  6.4 0.2 shard_map.136
  6.6 2.1 %collective-permute-start.3 = (bf16[176,512]{1,0:T(8,128)(2,1)S(1)}, bf16[176,512]{1,0:T(8,128)(2,1)S(1)}, u32[]{:S(2)}, u32[]{:S(2)}) collective-permute-start(bf16[176,512]{1,0:T(8,128)(2,1)S(1)} %get-tuple-element.16), channel_id=1, source_target_pairs={{0,4},{4,0},{8,12},{12,8},{16,20},{20,16},{24,28},{28,24},{32,36},... | collective-permute-start | bytes 540680 | tf_op jit(solution)/shard_map/ppermute | solution.py:423
  8.7 6.7 %collective-permute-start.4 = (bf16[176,512]{1,0:T(8,128)(2,1)S(1)}, bf16[176,512]{1,0:T(8,128)(2,1)S(1)}, u32[]{:S(2)}, u32[]{:S(2)}) collective-permute-start(bf16[176,512]{1,0:T(8,128)(2,1)S(1)} %get-tuple-element.17), channel_id=1, source_target_pairs={{0,60},{4,8},{8,4},{12,16},{16,12},{20,24},{24,20},{28,32},{32,28}... | collective-permute-start | bytes 540680 | tf_op jit(solution)/shard_map/ppermute | solution.py:422
  15.4 1.1 %collective-permute-done.3.first = bf16[176,512]{1,0:T(8,128)(2,1)S(1)} collective-permute-done((bf16[176,512]{1,0:T(8,128)(2,1)S(1)}, bf16[176,512]{1,0:T(8,128)(2,1)S(1)}, u32[]{:S(2)}, u32[]{:S(2)}) %collective-permute-start.3) | collective-permute-done | bytes 180256 | tf_op jit(solution)/shard_map/ppermute | solution.py:423
  16.6 3.4 %collective-permute-done.4.second = bf16[176,512]{1,0:T(8,128)(2,1)S(1)} collective-permute-done((bf16[176,512]{1,0:T(8,128)(2,1)S(1)}, bf16[176,512]{1,0:T(8,128)(2,1)S(1)}, u32[]{:S(2)}, u32[]{:S(2)}) %collective-permute-start.4) | collective-permute-done | bytes 180256 | tf_op jit(solution)/shard_map/ppermute | solution.py:422
  20.0 0.0 copy-start.10
  20.0 0.7 %copy-done.10 = s32[1,512]{1,0:T(1,128)S(1)} copy-done((s32[1,512]{1,0:T(1,128)S(1)}, s32[1,512]{1,0:T(1,128)}, u32[]{:S(2)}) %copy-start.10) | copy-done | bytes 2072
  20.7 0.0 copy-start.11
  20.7 0.7 %copy-done.11 = f32[1,512]{1,0:T(1,128)S(1)} copy-done((f32[1,512]{1,0:T(1,128)S(1)}, f32[1,512]{1,0:T(1,128)}, u32[]{:S(2)}) %copy-start.11) | copy-done | bytes 2072
  21.3 0.0 copy-start.3
  21.3 0.0 copy-start.5
  21.3 0.5 %shard_map.137 = (bf16[256,512]{1,0:T(8,128)(2,1)S(1)}, bf16[256,512]{1,0:T(8,128)(2,1)S(1)}, f32[16,512]{1,0:T(8,128)S(1)}, bf16[272,128]{1,0:T(8,128)(2,1)S(1)}, bf16[272,128]{1,0:T(8,128)(2,1)S(1)}) custom-call(bf16[1,2,64,512]{3,2,1,0:T(8,128)(2,1)S(1)} %copy-done, bf16[2,64,512]{2,1,0:T(8,128)(2,1)S(1)} %get-tuple-element.14.reference, ...), custom_call_target="tpu_custom_call" | custom-call | tf_op jit(solution)/shard_map/pallas_call | solution.py:404
  21.9 1.7 %collective-permute-start.5 = (bf16[272,128]{1,0:T(8,128)(2,1)S(1)}, bf16[272,128]{1,0:T(8,128)(2,1)S(1)}, u32[]{:S(2)}, u32[]{:S(2)}) collective-permute-start(bf16[272,128]{1,0:T(8,128)(2,1)S(1)} %get-tuple-element.21), channel_id=1, source_target_pairs={{0,1},{1,0},{2,3},{3,2},{4,5},{5,4},{6,7},{7,6},{8,9},{9,8},{10,11... | collective-permute-start | bytes 208904 | tf_op jit(solution)/shard_map/ppermute | solution.py:423
  23.5 2.2 %collective-permute-start.6 = (bf16[272,128]{1,0:T(8,128)(2,1)S(1)}, bf16[272,128]{1,0:T(8,128)(2,1)S(1)}, u32[]{:S(2)}, u32[]{:S(2)}) collective-permute-start(bf16[272,128]{1,0:T(8,128)(2,1)S(1)} %get-tuple-element.22), channel_id=1, source_target_pairs={{0,3},{1,2},{2,1},{3,0},{4,7},{5,6},{6,5},{7,4},{8,11},{9,10},{10,... | collective-permute-start | bytes 208904 | tf_op jit(solution)/shard_map/ppermute | solution.py:422
  25.7 0.6 %collective-permute-done.5.first = bf16[272,128]{1,0:T(8,128)(2,1)S(1)} collective-permute-done((bf16[272,128]{1,0:T(8,128)(2,1)S(1)}, bf16[272,128]{1,0:T(8,128)(2,1)S(1)}, u32[]{:S(2)}, u32[]{:S(2)}) %collective-permute-start.5) | collective-permute-done | bytes 69664 | tf_op jit(solution)/shard_map/ppermute | solution.py:423
  26.3 2.8 %collective-permute-done.6.second = bf16[272,128]{1,0:T(8,128)(2,1)S(1)} collective-permute-done((bf16[272,128]{1,0:T(8,128)(2,1)S(1)}, bf16[272,128]{1,0:T(8,128)(2,1)S(1)}, u32[]{:S(2)}, u32[]{:S(2)}) %collective-permute-start.6) | collective-permute-done | bytes 69664 | tf_op jit(solution)/shard_map/ppermute | solution.py:422
  29.1 0.0 copy-done.1
  29.1 0.0 copy-done.3
  29.1 0.0 copy-done.5
  29.1 0.0 copy-start.2
  29.1 1.0 %copy-done.2 = bf16[4,256,256]{2,1,0:T(8,128)(2,1)S(1)} copy-done((bf16[4,256,256]{2,1,0:T(8,128)(2,1)S(1)}, bf16[4,256,256]{2,1,0:T(8,128)(2,1)}, u32[]{:S(2)}) %copy-start.2) | copy-done | bytes 524312
  30.1 0.0 copy-start.4
  30.1 0.9 %copy-done.4 = bf16[384,256]{1,0:T(8,128)(2,1)S(1)} copy-done((bf16[384,256]{1,0:T(8,128)(2,1)S(1)}, bf16[384,256]{1,0:T(8,128)(2,1)}, u32[]{:S(2)}) %copy-start.4) | copy-done | bytes 196632
  31.0 0.0 copy-start.6
  31.0 0.9 %copy-done.6 = bf16[256,256]{1,0:T(8,128)(2,1)S(1)} copy-done((bf16[256,256]{1,0:T(8,128)(2,1)S(1)}, bf16[256,256]{1,0:T(8,128)(2,1)}, u32[]{:S(2)}) %copy-start.6) | copy-done | bytes 131096
  31.9 0.0 copy-start.7
  31.9 0.9 %copy-done.7 = bf16[128,384]{1,0:T(8,128)(2,1)S(1)} copy-done((bf16[128,384]{1,0:T(8,128)(2,1)S(1)}, bf16[128,384]{1,0:T(8,128)(2,1)}, u32[]{:S(2)}) %copy-start.7) | copy-done | bytes 98328
  32.8 0.0 copy-start.8
  32.8 0.9 %copy-done.8 = bf16[128,384]{1,0:T(8,128)(2,1)S(1)} copy-done((bf16[128,384]{1,0:T(8,128)(2,1)S(1)}, bf16[128,384]{1,0:T(8,128)(2,1)}, u32[]{:S(2)}) %copy-start.8) | copy-done | bytes 98328
  33.7 10.4 %shard_map.138 = f32[1,2,64,512]{3,2,1,0:T(8,128)} custom-call(bf16[256,512]{1,0:T(8,128)(2,1)S(1)} %get-tuple-element.18.rows_in, bf16[256,512]{1,0:T(8,128)(2,1)S(1)} %get-tuple-element.19.master, f32[16,512]{1,0:T(8,128)S(1)} %get-tuple-element.20.sample_rows, bf16[272,128]{1,0:T(8,128)(2,1)S(1)} %collective-permute-done.5.first, ...), custom_call_target="tpu_custom_call" | custom-call | tf_op jit(solution)/shard_map/pallas_call | solution.py:404
Async XLA Ops:
  0.0 4.7 %copy-start.13 = (f32[1,64]{1,0:T(1,128)S(1)}, f32[1,64]{1,0:T(1,128)}, u32[]{:S(2)}) copy-start(f32[1,64]{1,0:T(1,128)} %fraction.2) | copy-start | bytes 772
  0.0 4.7 %copy-start.12 = (s32[1,64]{1,0:T(1,128)S(1)}, s32[1,64]{1,0:T(1,128)}, u32[]{:S(2)}) copy-start(s32[1,64]{1,0:T(1,128)} %shift.2) | copy-start | bytes 772
  0.0 3.6 %collective-permute-start.2 = (bf16[2,64,128]{2,1,0:T(8,128)(2,1)}, bf16[2,64,128]{2,1,0:T(8,128)(2,1)S(1)}, u32[]{:S(2)}, u32[]{:S(2)}) collective-permute-start(bf16[2,64,128]{2,1,0:T(8,128)(2,1)} %bitcast.1), channel_id=1, source_target_pairs={{0,192},{64,128},{128,64},{192,0},{1,193},{65,129},{129,65},{193,1... | collective-permute-start | bytes 98312 | tf_op jit(solution)/shard_map/ppermute | solution.py:429
  0.0 4.7 %collective-permute-start.1 = (bf16[2,64,128]{2,1,0:T(8,128)(2,1)}, bf16[2,64,128]{2,1,0:T(8,128)(2,1)S(1)}, u32[]{:S(2)}, u32[]{:S(2)}) collective-permute-start(bf16[2,64,128]{2,1,0:T(8,128)(2,1)} %bitcast.2), channel_id=1, source_target_pairs={{0,128},{64,192},{128,0},{192,64},{1,129},{65,193},{129,1},{193,65... | collective-permute-start | bytes 98312 | tf_op jit(solution)/shard_map/ppermute | solution.py:429
  2.3 2.4 %collective-permute-start = (bf16[2,64,128]{2,1,0:T(8,128)(2,1)}, bf16[2,64,128]{2,1,0:T(8,128)(2,1)S(1)}, u32[]{:S(2)}, u32[]{:S(2)}) collective-permute-start(bf16[2,64,128]{2,1,0:T(8,128)(2,1)} %bitcast.3), channel_id=1, source_target_pairs={{0,64},{64,0},{128,192},{192,128},{1,65},{65,1},{129,193},{193,129... | collective-permute-start | bytes 98312 | tf_op jit(solution)/shard_map/ppermute | solution.py:429
  4.7 0.9 %copy-start = (bf16[1,2,64,512]{3,2,1,0:T(8,128)(2,1)S(1)}, bf16[1,2,64,512]{3,2,1,0:T(8,128)(2,1)}, u32[]{:S(2)}) copy-start(bf16[1,2,64,512]{3,2,1,0:T(8,128)(2,1)} %secondary.3) | copy-start | bytes 393220
  5.6 0.8 %copy-start.9 = (bf16[2,64,1,128]{3,1,2,0:T(8,128)(2,1)S(1)}, bf16[2,64,1,128]{3,1,2,0:T(8,128)(2,1)}, u32[]{:S(2)}) copy-start(bf16[2,64,1,128]{3,1,2,0:T(8,128)(2,1)} %param.14) | copy-start | bytes 98308
  6.4 22.6 %copy-start.1 = (bf16[4,256,256]{2,1,0:T(8,128)(2,1)S(1)}, bf16[4,256,256]{2,1,0:T(8,128)(2,1)}, u32[]{:S(2)}) copy-start(bf16[4,256,256]{2,1,0:T(8,128)(2,1)} %constant.23.clone.refs_7_) | copy-start | bytes 1572868
  6.6 9.9 %collective-permute-start.3 = (bf16[176,512]{1,0:T(8,128)(2,1)S(1)}, bf16[176,512]{1,0:T(8,128)(2,1)S(1)}, u32[]{:S(2)}, u32[]{:S(2)}) collective-permute-start(bf16[176,512]{1,0:T(8,128)(2,1)S(1)} %get-tuple-element.16), channel_id=1, source_target_pairs={{0,4},{4,0},{8,12},{12,8},{16,20},{20,16},{24,28},{28,24},{32,36},... | collective-permute-start | bytes 540680 | tf_op jit(solution)/shard_map/ppermute | solution.py:423
  8.7 11.2 %collective-permute-start.4 = (bf16[176,512]{1,0:T(8,128)(2,1)S(1)}, bf16[176,512]{1,0:T(8,128)(2,1)S(1)}, u32[]{:S(2)}, u32[]{:S(2)}) collective-permute-start(bf16[176,512]{1,0:T(8,128)(2,1)S(1)} %get-tuple-element.17), channel_id=1, source_target_pairs={{0,60},{4,8},{8,4},{12,16},{16,12},{20,24},{24,20},{28,32},{32,28}... | collective-permute-start | bytes 540680 | tf_op jit(solution)/shard_map/ppermute | solution.py:422
  20.0 0.7 %copy-start.10 = (s32[1,512]{1,0:T(1,128)S(1)}, s32[1,512]{1,0:T(1,128)}, u32[]{:S(2)}) copy-start(s32[1,512]{1,0:T(1,128)} %shift.3) | copy-start | bytes 6148
  20.7 0.7 %copy-start.11 = (f32[1,512]{1,0:T(1,128)S(1)}, f32[1,512]{1,0:T(1,128)}, u32[]{:S(2)}) copy-start(f32[1,512]{1,0:T(1,128)} %fraction.3) | copy-start | bytes 6148
  21.3 7.7 %copy-start.3 = (bf16[384,256]{1,0:T(8,128)(2,1)S(1)}, bf16[384,256]{1,0:T(8,128)(2,1)}, u32[]{:S(2)}) copy-start(bf16[384,256]{1,0:T(8,128)(2,1)} %constant.19.clone.refs_3_) | copy-start | bytes 589828
  21.3 7.7 %copy-start.5 = (bf16[256,256]{1,0:T(8,128)(2,1)S(1)}, bf16[256,256]{1,0:T(8,128)(2,1)}, u32[]{:S(2)}) copy-start(bf16[256,256]{1,0:T(8,128)(2,1)} %constant.17.clone.refs_1_) | copy-start | bytes 393220
  21.9 4.4 %collective-permute-start.5 = (bf16[272,128]{1,0:T(8,128)(2,1)S(1)}, bf16[272,128]{1,0:T(8,128)(2,1)S(1)}, u32[]{:S(2)}, u32[]{:S(2)}) collective-permute-start(bf16[272,128]{1,0:T(8,128)(2,1)S(1)} %get-tuple-element.21), channel_id=1, source_target_pairs={{0,1},{1,0},{2,3},{3,2},{4,5},{5,4},{6,7},{7,6},{8,9},{9,8},{10,11... | collective-permute-start | bytes 208904 | tf_op jit(solution)/shard_map/ppermute | solution.py:423
  23.5 5.5 %collective-permute-start.6 = (bf16[272,128]{1,0:T(8,128)(2,1)S(1)}, bf16[272,128]{1,0:T(8,128)(2,1)S(1)}, u32[]{:S(2)}, u32[]{:S(2)}) collective-permute-start(bf16[272,128]{1,0:T(8,128)(2,1)S(1)} %get-tuple-element.22), channel_id=1, source_target_pairs={{0,3},{1,2},{2,1},{3,0},{4,7},{5,6},{6,5},{7,4},{8,11},{9,10},{10,... | collective-permute-start | bytes 208904 | tf_op jit(solution)/shard_map/ppermute | solution.py:422
  29.1 1.0 %copy-start.2 = (bf16[4,256,256]{2,1,0:T(8,128)(2,1)S(1)}, bf16[4,256,256]{2,1,0:T(8,128)(2,1)}, u32[]{:S(2)}) copy-start(bf16[4,256,256]{2,1,0:T(8,128)(2,1)} %constant.22.clone.refs_6_) | copy-start | bytes 1572868
  30.1 0.9 %copy-start.4 = (bf16[384,256]{1,0:T(8,128)(2,1)S(1)}, bf16[384,256]{1,0:T(8,128)(2,1)}, u32[]{:S(2)}) copy-start(bf16[384,256]{1,0:T(8,128)(2,1)} %constant.18.clone.refs_2_) | copy-start | bytes 589828
  31.0 0.9 %copy-start.6 = (bf16[256,256]{1,0:T(8,128)(2,1)S(1)}, bf16[256,256]{1,0:T(8,128)(2,1)}, u32[]{:S(2)}) copy-start(bf16[256,256]{1,0:T(8,128)(2,1)} %constant.16.clone.refs_0_) | copy-start | bytes 393220
  31.9 0.9 %copy-start.7 = (bf16[128,384]{1,0:T(8,128)(2,1)S(1)}, bf16[128,384]{1,0:T(8,128)(2,1)}, u32[]{:S(2)}) copy-start(bf16[128,384]{1,0:T(8,128)(2,1)} %constant.21.clone.refs_5_) | copy-start | bytes 294916
  32.8 0.9 %copy-start.8 = (bf16[128,384]{1,0:T(8,128)(2,1)S(1)}, bf16[128,384]{1,0:T(8,128)(2,1)}, u32[]{:S(2)}) copy-start(bf16[128,384]{1,0:T(8,128)(2,1)} %constant.20.clone.refs_4_) | copy-start | bytes 294916

commit v2 on v1

v2 whole, which is shorter than its diff:
```python
import functools

import jax
import jax.numpy as jnp
import ml_dtypes
import numpy as np
from jax import lax
from jax.experimental import pallas as pl
from jax.experimental.pallas import tpu as pltpu
from jax.sharding import PartitionSpec as P

PATCH = 64
HALF = 32
TAPS = 8
MARGIN = 48
LINES_DEV = 64
SAMPLES_DEV = 512
BF = jnp.bfloat16
F32 = jnp.float32
VMEM_LIMIT = 32 * 1024 * 1024


def split_table(table):
    high = table.astype(ml_dtypes.bfloat16)
    low = (table - high.astype(np.float64)).astype(ml_dtypes.bfloat16)
    return high, low


def hann(position):
    return np.minimum(position + 0.5, PATCH - 0.5 - position) / HALF


def sample_forward():
    table = np.zeros((2, 128, 2, 64, 2))
    v = np.arange(64)
    for p in range(2):
        for m in range(64):
            angle = 2 * np.pi * ((v * m) % 64) / 64
            n = m + 32 * p
            table[0, n, 0, :, p] = np.cos(angle)
            table[1, n, 0, :, p] = np.sin(angle)
            table[0, n, 1, :, p] = -np.sin(angle)
            table[1, n, 1, :, p] = np.cos(angle)
    return table.reshape(256, 256)


def line_forward():
    table = np.zeros((3, 2, 64, 2, 128))
    u = np.arange(64)
    for band in range(3):
        for m in range(64):
            angle = 2 * np.pi * ((u * m) % 64) / 64
            i = m + 32 * band
            table[band, 0, :, 0, i] = np.cos(angle)
            table[band, 0, :, 1, i] = np.sin(angle)
            table[band, 1, :, 0, i] = -np.sin(angle)
            table[band, 1, :, 1, i] = np.cos(angle)
    return table.reshape(384, 256)


def line_inverse():
    table = np.zeros((2, 64, 3, 2, 64))
    u = np.arange(64)
    for band in range(3):
        for y in range(64):
            m = y + 32 - 32 * band
            if 0 <= m < 64:
                angle = 2 * np.pi * ((u * m) % 64) / 64
                weight = hann(m) / 64
                table[0, y, band, 0, :] = weight * np.cos(angle)
                table[0, y, band, 1, :] = -weight * np.sin(angle)
                table[1, y, band, 0, :] = weight * np.sin(angle)
                table[1, y, band, 1, :] = weight * np.cos(angle)
    return table.reshape(128, 384)


def sample_inverse(start):
    table = np.zeros((2, 64, 2, 2, 128))
    v = np.arange(64)
    for p in range(2):
        for y in range(128):
            n = 32 + y - start - 32 * p
            if 0 <= n < 64:
                angle = 2 * np.pi * ((v * n) % 64) / 64
                weight = hann(n) / 64
                table[0, :, p, 0, y] = weight * np.cos(angle)
                table[1, :, p, 0, y] = -weight * np.sin(angle)
                table[0, :, p, 1, y] = weight * np.sin(angle)
                table[1, :, p, 1, y] = weight * np.cos(angle)
    return table.reshape(256, 256)


def triple(table, axis):
    high, low = split_table(table)
    return np.concatenate([high, high, low], axis=axis)


def filter_tables():
    inverse = [sample_inverse(start) for start in (0, 64, 128, 96)]
    return [
        triple(sample_forward(), 0),
        triple(line_forward(), 1),
        triple(line_inverse(), 1),
        np.concatenate([triple(table, 0) for table in inverse], axis=0),
    ]


def sinc_rows(fraction):
    tap = lax.broadcasted_iota(jnp.int32, (TAPS, fraction.shape[1]), 0)
    distance = fraction - (tap - (TAPS // 2 - 1)).astype(F32)
    centre = distance == 0.0
    sign = jnp.where(tap % 2 == 1, 1.0, -1.0)
    wave = sign * jnp.sin(np.float32(np.pi) * fraction)
    sinc = wave / jnp.where(centre, 1.0, np.float32(np.pi) * distance)
    sinc = jnp.where(centre, 1.0, sinc)
    taper = 0.5 + 0.5 * jnp.cos(np.float32(np.pi) * distance / (TAPS // 2))
    return (sinc * taper).astype(BF).astype(F32)


def kernel_rows(shift, fraction):
    weights = sinc_rows(fraction)
    row = lax.broadcasted_iota(jnp.int32, weights.shape, 0)
    shifts = jnp.where(row == 0, shift.astype(F32), 0.0)
    return jnp.concatenate([weights, shifts], axis=0)


def band_matrix(rows, depth):
    width = rows.shape[1]
    shift = rows[TAPS : TAPS + 1].astype(jnp.int32)
    source = lax.broadcasted_iota(jnp.int32, (depth, width), 0)
    target = lax.broadcasted_iota(jnp.int32, (depth, width), 1)
    step = source - (target + 13 + shift)
    matrix = jnp.zeros((depth, width), F32)
    for k in range(TAPS):
        matrix = jnp.where(step == k, rows[k : k + 1], matrix)
    return matrix


def split(values):
    high = values.astype(BF)
    return high, (values - high.astype(F32)).astype(BF)


def dot(left, right):
    return jnp.dot(left, right, preferred_element_type=F32)


def columns_triple(values):
    high, low = split(values)
    return jnp.concatenate([high, low, high], axis=1)


def rows_triple(values):
    high, low = split(values)
    return jnp.concatenate([high, low, high], axis=0)


def shifted(tiles, start):
    index, offset = start // 128, start % 128
    here = pltpu.roll(tiles[index], 128 - offset, 1)
    after = pltpu.roll(tiles[min(index + 1, 3)], 128 - offset, 1)
    lane = lax.broadcasted_iota(jnp.int32, here.shape, 1)
    return jnp.where(lane < 128 - offset, here, after)


def tiles_of(values):
    return [values[:, t * 128 : t * 128 + 128].astype(F32) for t in range(4)]


def pack_body(secondary, own, shift, fraction, first, second, line_rows, shift_v, fraction_v, sems):
    odd = lax.axis_index("az") % 2 == 1
    small = [
        pltpu.make_async_copy(shift, shift_v, sems.at[20]),
        pltpu.make_async_copy(fraction, fraction_v, sems.at[21]),
    ]
    for copy in small:
        copy.start()
    copies = []
    for message, upper in ((first, odd), (second, jnp.logical_not(odd))):
        line = pl.multiple_of(jnp.where(upper, 0, 16), 16)
        half = pl.multiple_of(jnp.where(upper, 0, 32), 16)
        for part in range(2):
            for tile in range(4):
                copies.append(
                    pltpu.make_async_copy(
                        secondary.at[0, part, pl.ds(line, 48), pl.ds(tile * 128, 128)],
                        message.at[pl.ds((2 * tile + part) * 48, 48)],
                        sems.at[len(copies)],
                    )
                )
            copies.append(
                pltpu.make_async_copy(
                    own.at[part, pl.ds(half, 32)],
                    message.at[pl.ds(384 + part * 32, 32)],
                    sems.at[len(copies)],
                )
            )
    for copy in copies:
        copy.start()
    for copy in small:
        copy.wait()
    row_shift = jnp.concatenate([shift_v[...], shift_v[...]], axis=1)
    row_fraction = jnp.concatenate([fraction_v[...], fraction_v[...]], axis=1)
    rows = kernel_rows(pltpu.roll(row_shift, 32, 1), pltpu.roll(row_fraction, 32, 1))
    line_rows[...] = rows
    first[448:464] = rows.astype(BF)
    second[448:464] = rows.astype(BF)
    for copy in copies:
        copy.wait()


def prepare_body(secondary, own, shift, fraction, *refs):
    tables, outs = refs[0:4], refs[4:13]
    secondary_v, own_v, sample_rows, bands = outs[0:4]
    tables_v = outs[4:8]
    shift_v, fraction_v, sems = outs[8], refs[13], refs[14]
    pairs = [(shift, shift_v), (fraction, fraction_v), (own, own_v), (secondary, secondary_v)]
    pairs.extend(zip(tables, tables_v))
    copies = [
        pltpu.make_async_copy(source, target, sems.at[at]) for at, (source, target) in enumerate(pairs)
    ]
    for copy in copies:
        copy.start()
    for copy in copies[:2]:
        copy.wait()
    samples = kernel_rows(shift_v[...], fraction_v[...])
    sample_rows[...] = samples
    tiles = tiles_of(samples)
    for j in range(1, 8):
        bands[j - 1] = band_matrix(shifted(tiles, 64 * j - 32), 128).astype(BF)
    for copy in copies[2:]:
        copy.wait()


def lines_body(secondary, line_rows, first, second, bands, edges, resampled, extended, halo_rows):
    odd = lax.axis_index("az") % 2 == 1
    has_top = lax.axis_index("az") > 0
    has_bottom = lax.axis_index("az") < lax.axis_size("az") - 1

    def place(top, bottom):
        for part in range(2):
            for tile in range(4):
                rows = slice((2 * tile + part) * 48, (2 * tile + part) * 48 + 48)
                lanes = slice(tile * 128, tile * 128 + 128)
                extended[part, 0:48, lanes] = top[rows]
                extended[part, 112:160, lanes] = bottom[rows]
        halo_rows[0] = top[448:464].astype(F32)
        halo_rows[1] = bottom[448:464].astype(F32)

    @pl.when(odd)
    def _():
        place(first, second)

    @pl.when(jnp.logical_not(odd))
    def _():
        place(second, first)

    for part in range(2):
        extended[part, 48:112] = secondary[0, part]

    lane = lax.broadcasted_iota(jnp.int32, (16, 128), 1)
    rows = jnp.where(
        lane < 32,
        pltpu.roll(halo_rows[0], 64, 1),
        jnp.where(lane < 96, line_rows[...], pltpu.roll(halo_rows[1], 64, 1)),
    )
    matrix = band_matrix(rows, 160)
    line = lax.broadcasted_iota(jnp.int32, matrix.shape, 0)
    low = jnp.where(has_top, 0, 48)
    high = jnp.where(has_bottom, 160, 112)
    matrix = jnp.where((line >= low) & (line < high), matrix, 0.0).astype(BF)
    values = [
        lax.dot_general(
            matrix, extended[part], (((0,), (0,)), ((), ())), preferred_element_type=F32
        )
        for part in range(2)
    ]
    values = jnp.concatenate(values, axis=0).astype(BF)
    edges[:, 0:128] = values[:, 0:128]
    edges[:, 128:256] = values[:, 384:512]
    tiles = tiles_of(values)
    for j in range(1, 8):
        resampled[j - 1] = dot(shifted(tiles, 64 * j - 48).astype(BF), bands[j - 1])


def reference_body(own, peer1, peer2, peer3, halo, halo1, halo2, halo3, edges, sample_rows,
                   master, send_first, send_second):
    date = lax.axis_index("date")
    az = lax.axis_index("az")
    odd = az % 2 == 1
    has_top = az > 0
    has_bottom = az < lax.axis_size("az") - 1
    pieces = (own, peer1, peer2, peer3)
    halos = (halo, halo1, halo2, halo3)
    for value in range(4):

        @pl.when(date == value)
        def _():
            for offset in range(4):
                lanes = slice((value ^ offset) * 128, (value ^ offset) * 128 + 128)
                piece, around = pieces[offset], halos[offset]
                for part in range(2):
                    base = part * 128
                    master[base + 32 : base + 96, lanes] = piece[part]

                    @pl.when(odd)
                    def _():
                        master[base : base + 32, lanes] = around[part * 32 : part * 32 + 32]
                        master[base + 96 : base + 128, lanes] = around[64 + part * 32 : 96 + part * 32]

                    @pl.when(jnp.logical_not(odd))
                    def _():
                        master[base : base + 32, lanes] = around[64 + part * 32 : 96 + part * 32]
                        master[base + 96 : base + 128, lanes] = around[part * 32 : part * 32 + 32]

    @pl.when(jnp.logical_not(has_top))
    def _():
        for part in range(2):
            master[part * 128 : part * 128 + 32] = jnp.zeros((32, 512), BF)

    @pl.when(jnp.logical_not(has_bottom))
    def _():
        for part in range(2):
            master[part * 128 + 96 : part * 128 + 128] = jnp.zeros((32, 512), BF)

    lane = lax.broadcasted_iota(jnp.int32, (256, 128), 1)
    to_right = jnp.where(
        lane < 48,
        pltpu.roll(edges[:, 128:256].astype(F32), 48, 1),
        master[:, 384:512].astype(F32),
    ).astype(BF)
    to_left = jnp.where(
        lane >= 80,
        pltpu.roll(edges[:, 0:128].astype(F32), 80, 1),
        master[:, 0:128].astype(F32),
    ).astype(BF)
    right_rows = sample_rows[:, 384:512].astype(BF)
    left_rows = sample_rows[:, 0:128].astype(BF)
    rg_odd = lax.axis_index("rg") % 2 == 1

    @pl.when(rg_odd)
    def _():
        send_first[0:256] = to_left
        send_first[256:272] = left_rows
        send_second[0:256] = to_right
        send_second[256:272] = right_rows

    @pl.when(jnp.logical_not(rg_odd))
    def _():
        send_first[0:256] = to_right
        send_first[256:272] = right_rows
        send_second[0:256] = to_left
        send_second[256:272] = left_rows


def lane_sum(values):
    for step in (2, 4, 8, 16, 32, 64):
        values = values + pltpu.roll(values, step, 1)
    return values


def root(values):
    return values * lax.rsqrt(jnp.maximum(values, np.float32(1e-36)))


def block_columns(resampled, master, forward):
    real, imag = resampled[:128], resampled[128:]
    product = jnp.concatenate(
        [master[:128] * real + master[128:] * imag, master[128:] * real - master[:128] * imag],
        axis=1,
    )
    columns = dot(columns_triple(product), forward)
    return jnp.concatenate([columns[:, :128], columns[:, 128:]], axis=0)


def responses(spectrum):
    result = []
    for band in range(3):
        real = spectrum[band * 128 : band * 128 + 64]
        imag = spectrum[band * 128 + 64 : band * 128 + 128]
        smooth = root(real * real + imag * imag)
        smooth = smooth + pltpu.roll(smooth, 2, 1) + pltpu.roll(smooth, 126, 1)
        smooth = smooth + pltpu.roll(smooth, 1, 0) + pltpu.roll(smooth, 63, 0)
        result.append(root(smooth))
    return result


def gained(spectrum, response, scale):
    parts = []
    for band in range(3):
        gain = response[band] * scale[band : band + 1]
        parts.append(spectrum[band * 128 : band * 128 + 64] * gain)
        parts.append(spectrum[band * 128 + 64 : band * 128 + 128] * gain)
    return jnp.concatenate(parts, axis=0)


def filter_blocks(columns, singles, lines, inverse):
    count = len(columns)
    spectrum = dot(lines, jnp.concatenate([rows_triple(column) for column in columns], axis=1))
    spectra = [spectrum[:, at * 128 : at * 128 + 128] for at in range(count)]
    response = [responses(values) for values in spectra]
    sums = jnp.concatenate(
        [jnp.sum(values, axis=0, keepdims=True) for block in response for values in block], axis=0
    )
    scale = 1.0 / (lane_sum(sums) * np.float32(1 / 4096) + np.float32(3e-06))
    lane = lax.broadcasted_iota(jnp.int32, (3, 128), 1)
    filtered = []
    for at in range(count):
        factor = scale[3 * at : 3 * at + 3]
        if singles[at]:
            factor = jnp.where(lane % 2 == 0, factor, 0.0)
        filtered.append(rows_triple(gained(spectra[at], response[at], factor)))
    back = dot(inverse, jnp.concatenate(filtered, axis=1))
    result = []
    for at in range(count):
        tile = back[:, at * 128 : at * 128 + 128]
        result.append(columns_triple(jnp.concatenate([tile[:64], tile[64:]], axis=1)))
    return result


def interior_body(resampled, master, forward, lines, inverse, samples, out):
    tiles = tiles_of(master[...])
    columns = [
        block_columns(resampled[j - 1], shifted(tiles, 64 * j - 32), forward[...])
        for j in range(1, 8)
    ]
    parts = filter_blocks(columns, [j == 7 for j in range(1, 8)], lines[...], inverse[...])
    for block in range(4):
        used = [j for j in (2 * block, 2 * block + 1, 2 * block + 2) if 1 <= j <= 7]
        start = (used[0] - 2 * block) * 768
        values = dot(
            jnp.concatenate([parts[j - 1] for j in used], axis=1),
            samples[start : start + 768 * len(used)],
        )
        out[0, 0, :, block * 128 : block * 128 + 128] = values[:, :128]
        out[0, 1, :, block * 128 : block * 128 + 128] = values[:, 128:]


def edge_body(part, edges, master, sample_rows, first, second, forward, lines, inverse, samples, out):
    rg = lax.axis_index("rg")
    odd = rg % 2 == 1
    left_scale = jnp.where(rg > 0, 1.0, 0.0).astype(F32)
    right_scale = jnp.where(rg < lax.axis_size("rg") - 1, 1.0, 0.0).astype(F32)
    first_f = first[...].astype(F32)
    second_f = second[...].astype(F32)
    from_left = jnp.where(odd, first_f, second_f)
    from_right = jnp.where(odd, second_f, first_f)

    def mixed(lane_count, halo, own, reverse):
        lane = lax.broadcasted_iota(jnp.int32, own.shape, 1)
        return jnp.where(lane >= lane_count if reverse else lane < lane_count, halo, own)

    def edge(window, around, rows):
        matrix = band_matrix(rows, 128).astype(BF)
        return block_columns(dot(window.astype(BF), matrix), around, forward[...])

    left = edge(
        mixed(48, from_left[:256] * left_scale,
              pltpu.roll(edges[:, 0:128].astype(F32), 48, 1), False),
        mixed(32, pltpu.roll(from_left[:256], 32, 1) * left_scale,
              pltpu.roll(master[:, 0:128].astype(F32), 32, 1), False),
        mixed(32, pltpu.roll(from_left[256:], 32, 1),
              pltpu.roll(sample_rows[:, 0:128], 32, 1), False),
    )
    right = edge(
        mixed(80, from_right[:256] * right_scale,
              pltpu.roll(edges[:, 128:256].astype(F32), 80, 1), True),
        mixed(64, pltpu.roll(from_right[:256], 64, 1) * right_scale,
              pltpu.roll(master[:, 384:512].astype(F32), 64, 1), True),
        mixed(64, pltpu.roll(from_right[256:], 64, 1),
              pltpu.roll(sample_rows[:, 384:512], 64, 1), True),
    )
    parts = filter_blocks([left, right], [False, False], lines[...], inverse[...])
    for at, block in ((0, 0), (1, 3)):
        values = dot(parts[at], samples[block * 768 : block * 768 + 768])
        lanes = slice(block * 128, block * 128 + 128)
        out[0, 0, :, lanes] = part[0, 0, :, lanes] + values[:, :128]
        out[0, 1, :, lanes] = part[0, 1, :, lanes] + values[:, 128:]
    out[0, :, :, 128:384] = part[0, :, :, 128:384]


def call(name, body, outputs, scratch=(), hbm=0, cost=0):
    vmem = pl.BlockSpec(memory_space=pltpu.VMEM)
    far = pl.BlockSpec(memory_space=pltpu.HBM)
    return lambda *args: pl.pallas_call(
        body,
        name=name,
        out_shape=[jax.ShapeDtypeStruct(shape, kind) for shape, kind in outputs],
        in_specs=[far] * hbm + [vmem] * (len(args) - hbm),
        out_specs=[vmem] * len(outputs),
        scratch_shapes=list(scratch),
        compiler_params=pltpu.CompilerParams(vmem_limit_bytes=VMEM_LIMIT),
        cost_estimate=pl.CostEstimate(flops=cost, bytes_accessed=cost // 100, transcendentals=0),
    )(*args)


def swaps(size):
    first = [(i, i ^ 1) for i in range(size)]
    second = [(i, (i + 1) % size if i % 2 == 1 else (i - 1) % size) for i in range(size)]
    return first, second


def exchange(first, second, axis):
    pairs = swaps(lax.axis_size(axis))
    received_first = lax.ppermute(first, axis, pairs[0])
    received_second = lax.ppermute(second, axis, pairs[1])
    return received_first, received_second


def date_swaps(values):
    return [lax.ppermute(values, "date", [(i, i ^ k) for i in range(4)]) for k in (1, 2, 3)]


def on_device(reference_slab, secondary, az_shift, az_fraction, rg_shift, rg_fraction):
    own = reference_slab.reshape(2, LINES_DEV, 128)
    message = ((464, 128), BF)
    first, second, line_rows = call(
        "pack", pack_body, [message, message, ((16, 128), F32)],
        [pltpu.VMEM((1, 64), jnp.int32), pltpu.VMEM((1, 64), F32), pltpu.SemaphoreType.DMA((22,))],
        hbm=4, cost=10**9,
    )(secondary, own, az_shift, az_fraction)
    tables = [jnp.asarray(table) for table in filter_tables()]
    prepared = call(
        "prepare", prepare_body,
        [((1, 2, LINES_DEV, 512), BF), ((2, LINES_DEV, 128), BF), ((16, 512), F32), ((7, 128, 128), BF)]
        + [(table.shape, BF) for table in tables],
        [pltpu.VMEM((1, 512), jnp.int32), pltpu.VMEM((1, 512), F32), pltpu.SemaphoreType.DMA((8,))],
        hbm=8, cost=2 * 10**9,
    )(secondary, own, rg_shift, rg_fraction, *tables)
    secondary_v, own_v, sample_rows, bands = prepared[:4]
    tables_v = prepared[4:]
    first, second = exchange(first, second, "az")
    peers = date_swaps(own_v)
    halo = jnp.concatenate([first[384:448], second[384:448]], axis=0)
    halos = date_swaps(halo)
    edges, resampled = call(
        "lines", lines_body, [((256, 256), BF), ((7, 256, 128), F32)],
        [pltpu.VMEM((2, 160, 512), BF), pltpu.VMEM((2, 16, 128), F32)],
        cost=10**9,
    )(secondary_v, line_rows, first, second, bands)
    master, first, second = call(
        "reference", reference_body, [((256, 512), BF), ((272, 128), BF), ((272, 128), BF)],
        cost=10**8,
    )(own_v, *peers, halo, *halos, edges, sample_rows)
    first, second = exchange(first, second, "rg")
    whole = ((1, 2, LINES_DEV, SAMPLES_DEV), F32)
    part = call("interior", interior_body, [whole], cost=4 * 10**9)(resampled, master, *tables_v)[0]
    return call("edge", edge_body, [whole], cost=10**9)(
        part, edges, master, sample_rows, first, second, *tables_v
    )[0]


def solution(mesh):
    in_specs = (
        P(None, "az", "rg", "date"),
        P("date", None, "az", "rg"),
        P("date", "az"),
        P("date", "az"),
        P("date", "rg"),
        P("date", "rg"),
    )
    out_specs = P("date", None, "az", "rg")
    return jax.shard_map(
        on_device, mesh=mesh, in_specs=in_specs, out_specs=out_specs, check_vma=False
    )
```

time: 44.5 us -> 31.9 us (0.72)
  the two profiles are of different devices: /device:TPU:2 before, /device:TPU:1 now
where the time goes in v2:
time: 31.9 us; the launch traced here: 31.7 us
  starting transfers between devices  17.7 us (55%)
  Pallas kernels  8.47 us (27%)
  local copies, waits for them, and re-layouts  3 us (9%)
  waiting for transfers between devices  2.39 us (7%)
    pallas_call x6, Pallas kernels, call(): pl.pallas_call(body, name=name, out_shape=[jax.ShapeDtypeStruct(shape, ki...  8.47 us
    ppermute x2, starting transfers between devices, exchange(): received_second = lax.ppermute(second, axis, pairs[1])  7.42 us
    ppermute x6, starting transfers between devices, date_swaps(): lax.ppermute(values, 'date', [(i, i ^ k) for i in range(4)])  5.28 us
    ppermute x2, starting transfers between devices, exchange(): received_first = lax.ppermute(first, axis, pairs[0])  5.05 us
    unnamed x20, local copies, waits for them, and re-layouts  3 us
    ppermute x6, waiting for transfers between devices, date_swaps(): lax.ppermute(values, 'date', [(i, i ^ k) for i in range(4)])  2.38 us
  transfers between devices with their start and end apart: 10, of which 2 were waited for; matrix products, arithmetic and copies ran while one was open for 0% of the time, Pallas kernels for 16%

profile of v2, /device:TPU:1, one launch (start us, length us, event | category | flops | bytes accessed | tf_op | source)
XLA Modules:
  0.0 31.7 jit_solution(7883525354316878978)
XLA Ops:
  0.0 0.0 copy-start
  0.0 0.9 %copy-done = bf16[1,2,64,512]{3,2,1,0:T(8,128)(2,1)S(1)} copy-done((bf16[1,2,64,512]{3,2,1,0:T(8,128)(2,1)S(1)}, bf16[1,2,64,512]{3,2,1,0:T(8,128)(2,1)}, u32[]{:S(2)}) %copy-start) | copy-done | bytes 131096
  0.9 0.0 copy-start.1
  0.9 0.8 %copy-done.1 = bf16[2,64,1,128]{3,1,2,0:T(8,128)(2,1)S(1)} copy-done((bf16[2,64,1,128]{3,1,2,0:T(8,128)(2,1)S(1)}, bf16[2,64,1,128]{3,1,2,0:T(8,128)(2,1)}, u32[]{:S(2)}) %copy-start.1) | copy-done | bytes 32792
  1.7 0.0 copy-start.4
  1.7 0.7 %copy-done.4 = s32[1,64]{1,0:T(1,128)S(1)} copy-done((s32[1,64]{1,0:T(1,128)S(1)}, s32[1,64]{1,0:T(1,128)}, u32[]{:S(2)}) %copy-start.4) | copy-done | bytes 280
  2.3 0.0 copy-start.5
  2.3 0.7 %copy-done.5 = f32[1,64]{1,0:T(1,128)S(1)} copy-done((f32[1,64]{1,0:T(1,128)S(1)}, f32[1,64]{1,0:T(1,128)}, u32[]{:S(2)}) %copy-start.5) | copy-done | bytes 280
  3.0 0.0 copy-start.2
  3.0 0.0 copy-start.3
  3.0 0.0 copy-start.6
  3.0 0.0 copy-start.7
  3.0 0.0 copy-start.8
  3.0 0.0 copy-start.9
  3.0 0.5 %pack.1 = (bf16[464,128]{1,0:T(8,128)(2,1)S(1)}, bf16[464,128]{1,0:T(8,128)(2,1)S(1)}, f32[16,128]{1,0:T(8,128)S(1)}) custom-call(bf16[1,2,64,512]{3,2,1,0:T(8,128)(2,1)S(1)} %copy-done, bf16[2,64,128]{2,1,0:T(8,128)(2,1)S(1)} %bitcast.1, s32[1,64]{1,0:T(1,128)S(1)} %copy-done.4, f32[1,64]{1,0:T(1,128)S(1)} %copy-done.5), custom_call_target="tpu_custom_call" | custom-call | flops 1000000000 | bytes 10000000 | tf_op jit(solution)/shard_map/pack/pallas_call | solution.py:485
  3.6 3.7 %collective-permute-start = (bf16[464,128]{1,0:T(8,128)(2,1)S(1)}, bf16[464,128]{1,0:T(8,128)(2,1)S(1)}, u32[]{:S(2)}, u32[]{:S(2)}) collective-permute-start(bf16[464,128]{1,0:T(8,128)(2,1)S(1)} %get-tuple-element.23), channel_id=1, source_target_pairs={{0,4},{4,0},{8,12},{12,8},{16,20},{20,16},{24,28},{28,24},{32,36},... | collective-permute-start | bytes 356360 | tf_op jit(solution)/shard_map/ppermute | solution.py:505
  7.2 5.5 %collective-permute-start.1 = (bf16[464,128]{1,0:T(8,128)(2,1)S(1)}, bf16[464,128]{1,0:T(8,128)(2,1)S(1)}, u32[]{:S(2)}, u32[]{:S(2)}) collective-permute-start(bf16[464,128]{1,0:T(8,128)(2,1)S(1)} %get-tuple-element.24), channel_id=1, source_target_pairs={{0,60},{4,8},{8,4},{12,16},{16,12},{20,24},{24,20},{28,32},{32,28}... | collective-permute-start | bytes 356360 | tf_op jit(solution)/shard_map/ppermute | solution.py:506
  12.7 0.0 copy-done.2
  12.7 0.0 copy-done.3
  12.7 0.0 copy-done.6
  12.7 0.0 copy-done.7
  12.7 0.0 copy-done.8
  12.8 0.0 copy-done.9
  12.8 1.2 %prepare.1 = (bf16[1,2,64,512]{3,2,1,0:T(8,128)(2,1)S(1)}, bf16[2,64,128]{2,1,0:T(8,128)(2,1)S(1)}, f32[16,512]{1,0:T(8,128)S(1)}, bf16[7,128,128]{2,1,0:T(8,128...) custom-call(bf16[1,2,64,512]{3,2,1,0:T(8,128)(2,1)S(1)} %copy-done, ...), custom_call_target="tpu_custom_call" | custom-call | flops 2000000000 | bytes 20000000 | tf_op jit(solution)/shard_map/prepare/pallas_call | solution.py:485
  14.0 1.3 %collective-permute-start.2 = (bf16[2,64,128]{2,1,0:T(8,128)(2,1)S(1)}, bf16[2,64,128]{2,1,0:T(8,128)(2,1)S(1)}, u32[]{:S(2)}, u32[]{:S(2)}) collective-permute-start(bf16[2,64,128]{2,1,0:T(8,128)(2,1)S(1)} %get-tuple-element.27.own), channel_id=1, source_target_pairs={{0,64},{64,0},{128,192},{192,128},{1,65},{65,1},{129,193},{193,129... | collective-permute-start | bytes 98312 | tf_op jit(solution)/shard_map/ppermute | solution.py:511
  15.3 1.2 %collective-permute-start.3 = (bf16[2,64,128]{2,1,0:T(8,128)(2,1)S(1)}, bf16[2,64,128]{2,1,0:T(8,128)(2,1)S(1)}, u32[]{:S(2)}, u32[]{:S(2)}) collective-permute-start(bf16[2,64,128]{2,1,0:T(8,128)(2,1)S(1)} %get-tuple-element.27.own), channel_id=1, source_target_pairs={{0,128},{64,192},{128,0},{192,64},{1,129},{65,193},{129,1},{193,65... | collective-permute-start | bytes 98312 | tf_op jit(solution)/shard_map/ppermute | solution.py:511
  16.5 0.5 %collective-permute-start.4 = (bf16[2,64,128]{2,1,0:T(8,128)(2,1)S(1)}, bf16[2,64,128]{2,1,0:T(8,128)(2,1)S(1)}, u32[]{:S(2)}, u32[]{:S(2)}) collective-permute-start(bf16[2,64,128]{2,1,0:T(8,128)(2,1)S(1)} %get-tuple-element.27.own), channel_id=1, source_target_pairs={{0,192},{64,128},{128,64},{192,0},{1,193},{65,129},{129,65},{193,1... | collective-permute-start | bytes 98312 | tf_op jit(solution)/shard_map/ppermute | solution.py:511
  17.0 0.0 collective-permute-done.1.second
  17.1 0.0 collective-permute-done.first
  17.1 0.2 collective-permute-start.5
  17.3 1.2 %collective-permute-start.6 = (bf16[128,128]{1,0:T(8,128)(2,1)S(1)}, bf16[128,128]{1,0:T(8,128)(2,1)S(1)}, u32[]{:S(2)}, u32[]{:S(2)}) collective-permute-start(bf16[128,128]{1,0:T(8,128)(2,1)S(1)} %pad_maximum_fusion.halo), channel_id=1, source_target_pairs={{0,128},{64,192},{128,0},{192,64},{1,129},{65,193},{129,1},{193,65... | collective-permute-start | bytes 98312 | tf_op jit(solution)/shard_map/ppermute | solution.py:511
  18.5 0.0 collective-permute-done.2.peer1
  18.5 0.8 %collective-permute-start.7 = (bf16[128,128]{1,0:T(8,128)(2,1)S(1)}, bf16[128,128]{1,0:T(8,128)(2,1)S(1)}, u32[]{:S(2)}, u32[]{:S(2)}) collective-permute-start(bf16[128,128]{1,0:T(8,128)(2,1)S(1)} %pad_maximum_fusion.halo), channel_id=1, source_target_pairs={{0,192},{64,128},{128,64},{192,0},{1,193},{65,129},{129,65},{193,1... | collective-permute-start | bytes 98312 | tf_op jit(solution)/shard_map/ppermute | solution.py:511
  19.3 0.7 %lines.1 = (bf16[256,256]{1,0:T(8,128)(2,1)S(1)}, f32[7,256,128]{2,1,0:T(8,128)S(1)}) custom-call(bf16[1,2,64,512]{3,2,1,0:T(8,128)(2,1)S(1)} %get-tuple-element.21.secondary, f32[16,128]{1,0:T(8,128)S(1)} %get-tuple-element.22.line_rows, bf16[464,128]{1,0:T(8,128)(2,1)S(1)} %collective-permute-done.first, ...), custom_call_target="tpu_custom_call" | custom-call | flops 1000000000 | bytes 10000000 | tf_op jit(solution)/shard_map/lines/pallas_call | solution.py:485
  20.0 0.0 collective-permute-done.3.peer2
  20.0 0.0 collective-permute-done.4.peer3
  20.1 0.0 collective-permute-done.5.halo1
  20.1 0.2 collective-permute-done.6.halo2
  20.3 2.2 %collective-permute-done.7.halo3 = bf16[128,128]{1,0:T(8,128)(2,1)S(1)} collective-permute-done((bf16[128,128]{1,0:T(8,128)(2,1)S(1)}, bf16[128,128]{1,0:T(8,128)(2,1)S(1)}, u32[]{:S(2)}, u32[]{:S(2)}) %collective-permute-start.7) | collective-permute-done | bytes 32800 | tf_op jit(solution)/shard_map/ppermute | solution.py:511
  22.4 0.2 reference.1
  22.6 1.4 %collective-permute-start.8 = (bf16[272,128]{1,0:T(8,128)(2,1)S(1)}, bf16[272,128]{1,0:T(8,128)(2,1)S(1)}, u32[]{:S(2)}, u32[]{:S(2)}) collective-permute-start(bf16[272,128]{1,0:T(8,128)(2,1)S(1)} %get-tuple-element.35), channel_id=1, source_target_pairs={{0,1},{1,0},{2,3},{3,2},{4,5},{5,4},{6,7},{7,6},{8,9},{9,8},{10,11... | collective-permute-start | bytes 208904 | tf_op jit(solution)/shard_map/ppermute | solution.py:505
  24.0 1.9 %collective-permute-start.9 = (bf16[272,128]{1,0:T(8,128)(2,1)S(1)}, bf16[272,128]{1,0:T(8,128)(2,1)S(1)}, u32[]{:S(2)}, u32[]{:S(2)}) collective-permute-start(bf16[272,128]{1,0:T(8,128)(2,1)S(1)} %get-tuple-element.36), channel_id=1, source_target_pairs={{0,3},{1,2},{2,1},{3,0},{4,7},{5,6},{6,5},{7,4},{8,11},{9,10},{10,... | collective-permute-start | bytes 208904 | tf_op jit(solution)/shard_map/ppermute | solution.py:506
  25.9 3.0 %interior.1.part = f32[1,2,64,512]{3,2,1,0:T(8,128)S(1)} custom-call(f32[7,256,128]{2,1,0:T(8,128)S(1)} %get-tuple-element.26.resampled, bf16[256,512]{1,0:T(8,128)(2,1)S(1)} %get-tuple-element.30.master, bf16[768,256]{1,0:T(8,128)(2,1)S(1)} %get-tuple-element.31.forward, bf16[384,768]{1,0:T(8,128)(2,1)S(1)} %get-tuple-element.32.lines, ...), custom_call_target="tpu_custom_call" | custom-call | flops 4000000000 | bytes 40000000 | tf_op jit(solution)/shard_map/interior/pallas_call | solution.py:485
  28.9 0.0 collective-permute-done.8.first
  29.0 0.0 collective-permute-done.9.second
  29.0 2.8 %edge.1 = f32[1,2,64,512]{3,2,1,0:T(8,128)} custom-call(f32[1,2,64,512]{3,2,1,0:T(8,128)S(1)} %interior.1.part, bf16[256,256]{1,0:T(8,128)(2,1)S(1)} %get-tuple-element.28.edges, bf16[256,512]{1,0:T(8,128)(2,1)S(1)} %get-tuple-element.30.master, f32[16,512]{1,0:T(8,128)S(1)} %get-tuple-element.29.sample_rows, ...), custom_call_target="tpu_custom_call" | custom-call | flops 1000000000 | bytes 10000000 | tf_op jit(solution)/shard_map/edge/pallas_call | solution.py:485
  (3 shorter events, 0.0 us)
Async XLA Ops:
  0.0 0.9 %copy-start = (bf16[1,2,64,512]{3,2,1,0:T(8,128)(2,1)S(1)}, bf16[1,2,64,512]{3,2,1,0:T(8,128)(2,1)}, u32[]{:S(2)}) copy-start(bf16[1,2,64,512]{3,2,1,0:T(8,128)(2,1)} %secondary.3) | copy-start | bytes 393220
  0.9 0.8 %copy-start.1 = (bf16[2,64,1,128]{3,1,2,0:T(8,128)(2,1)S(1)}, bf16[2,64,1,128]{3,1,2,0:T(8,128)(2,1)}, u32[]{:S(2)}) copy-start(bf16[2,64,1,128]{3,1,2,0:T(8,128)(2,1)} %param.10) | copy-start | bytes 98308
  1.7 0.7 %copy-start.4 = (s32[1,64]{1,0:T(1,128)S(1)}, s32[1,64]{1,0:T(1,128)}, u32[]{:S(2)}) copy-start(s32[1,64]{1,0:T(1,128)} %shift.3) | copy-start | bytes 772
  2.3 0.7 %copy-start.5 = (f32[1,64]{1,0:T(1,128)S(1)}, f32[1,64]{1,0:T(1,128)}, u32[]{:S(2)}) copy-start(f32[1,64]{1,0:T(1,128)} %fraction.3) | copy-start | bytes 772
  3.0 9.8 %copy-start.2 = (s32[1,512]{1,0:T(1,128)S(1)}, s32[1,512]{1,0:T(1,128)}, u32[]{:S(2)}) copy-start(s32[1,512]{1,0:T(1,128)} %shift.2) | copy-start | bytes 6148
  3.0 9.8 %copy-start.3 = (f32[1,512]{1,0:T(1,128)S(1)}, f32[1,512]{1,0:T(1,128)}, u32[]{:S(2)}) copy-start(f32[1,512]{1,0:T(1,128)} %fraction.2) | copy-start | bytes 6148
  3.0 9.8 %copy-start.6 = (bf16[3072,256]{1,0:T(8,128)(2,1)S(1)}, bf16[3072,256]{1,0:T(8,128)(2,1)}, u32[]{:S(2)}) copy-start(bf16[3072,256]{1,0:T(8,128)(2,1)} %constant.11.clone.refs_3_) | copy-start | bytes 4718596
  3.0 9.8 %copy-start.7 = (bf16[384,768]{1,0:T(8,128)(2,1)S(1)}, bf16[384,768]{1,0:T(8,128)(2,1)}, u32[]{:S(2)}) copy-start(bf16[384,768]{1,0:T(8,128)(2,1)} %constant.9.clone.refs_1_) | copy-start | bytes 1769476
  3.0 9.8 %copy-start.8 = (bf16[768,256]{1,0:T(8,128)(2,1)S(1)}, bf16[768,256]{1,0:T(8,128)(2,1)}, u32[]{:S(2)}) copy-start(bf16[768,256]{1,0:T(8,128)(2,1)} %constant.8.clone.refs_0_) | copy-start | bytes 1179652
  3.0 9.8 %copy-start.9 = (bf16[128,1152]{1,0:T(8,128)(2,1)S(1)}, bf16[128,1152]{1,0:T(8,128)(2,1)}, u32[]{:S(2)}) copy-start(bf16[128,1152]{1,0:T(8,128)(2,1)} %constant.10.clone.refs_2_) | copy-start | bytes 884740
  3.6 13.5 %collective-permute-start = (bf16[464,128]{1,0:T(8,128)(2,1)S(1)}, bf16[464,128]{1,0:T(8,128)(2,1)S(1)}, u32[]{:S(2)}, u32[]{:S(2)}) collective-permute-start(bf16[464,128]{1,0:T(8,128)(2,1)S(1)} %get-tuple-element.23), channel_id=1, source_target_pairs={{0,4},{4,0},{8,12},{12,8},{16,20},{20,16},{24,28},{28,24},{32,36},... | collective-permute-start | bytes 356360 | tf_op jit(solution)/shard_map/ppermute | solution.py:505
  7.2 9.8 %collective-permute-start.1 = (bf16[464,128]{1,0:T(8,128)(2,1)S(1)}, bf16[464,128]{1,0:T(8,128)(2,1)S(1)}, u32[]{:S(2)}, u32[]{:S(2)}) collective-permute-start(bf16[464,128]{1,0:T(8,128)(2,1)S(1)} %get-tuple-element.24), channel_id=1, source_target_pairs={{0,60},{4,8},{8,4},{12,16},{16,12},{20,24},{24,20},{28,32},{32,28}... | collective-permute-start | bytes 356360 | tf_op jit(solution)/shard_map/ppermute | solution.py:506
  14.0 4.5 %collective-permute-start.2 = (bf16[2,64,128]{2,1,0:T(8,128)(2,1)S(1)}, bf16[2,64,128]{2,1,0:T(8,128)(2,1)S(1)}, u32[]{:S(2)}, u32[]{:S(2)}) collective-permute-start(bf16[2,64,128]{2,1,0:T(8,128)(2,1)S(1)} %get-tuple-element.27.own), channel_id=1, source_target_pairs={{0,64},{64,0},{128,192},{192,128},{1,65},{65,1},{129,193},{193,129... | collective-permute-start | bytes 98312 | tf_op jit(solution)/shard_map/ppermute | solution.py:511
  15.3 4.7 %collective-permute-start.3 = (bf16[2,64,128]{2,1,0:T(8,128)(2,1)S(1)}, bf16[2,64,128]{2,1,0:T(8,128)(2,1)S(1)}, u32[]{:S(2)}, u32[]{:S(2)}) collective-permute-start(bf16[2,64,128]{2,1,0:T(8,128)(2,1)S(1)} %get-tuple-element.27.own), channel_id=1, source_target_pairs={{0,128},{64,192},{128,0},{192,64},{1,129},{65,193},{129,1},{193,65... | collective-permute-start | bytes 98312 | tf_op jit(solution)/shard_map/ppermute | solution.py:511
  16.5 3.5 %collective-permute-start.4 = (bf16[2,64,128]{2,1,0:T(8,128)(2,1)S(1)}, bf16[2,64,128]{2,1,0:T(8,128)(2,1)S(1)}, u32[]{:S(2)}, u32[]{:S(2)}) collective-permute-start(bf16[2,64,128]{2,1,0:T(8,128)(2,1)S(1)} %get-tuple-element.27.own), channel_id=1, source_target_pairs={{0,192},{64,128},{128,64},{192,0},{1,193},{65,129},{129,65},{193,1... | collective-permute-start | bytes 98312 | tf_op jit(solution)/shard_map/ppermute | solution.py:511
  17.1 3.0 %collective-permute-start.5 = (bf16[128,128]{1,0:T(8,128)(2,1)S(1)}, bf16[128,128]{1,0:T(8,128)(2,1)S(1)}, u32[]{:S(2)}, u32[]{:S(2)}) collective-permute-start(bf16[128,128]{1,0:T(8,128)(2,1)S(1)} %pad_maximum_fusion.halo), channel_id=1, source_target_pairs={{0,64},{64,0},{128,192},{192,128},{1,65},{65,1},{129,193},{193,129... | collective-permute-start | bytes 98312 | tf_op jit(solution)/shard_map/ppermute | solution.py:511
  17.3 2.9 %collective-permute-start.6 = (bf16[128,128]{1,0:T(8,128)(2,1)S(1)}, bf16[128,128]{1,0:T(8,128)(2,1)S(1)}, u32[]{:S(2)}, u32[]{:S(2)}) collective-permute-start(bf16[128,128]{1,0:T(8,128)(2,1)S(1)} %pad_maximum_fusion.halo), channel_id=1, source_target_pairs={{0,128},{64,192},{128,0},{192,64},{1,129},{65,193},{129,1},{193,65... | collective-permute-start | bytes 98312 | tf_op jit(solution)/shard_map/ppermute | solution.py:511
  18.5 3.9 %collective-permute-start.7 = (bf16[128,128]{1,0:T(8,128)(2,1)S(1)}, bf16[128,128]{1,0:T(8,128)(2,1)S(1)}, u32[]{:S(2)}, u32[]{:S(2)}) collective-permute-start(bf16[128,128]{1,0:T(8,128)(2,1)S(1)} %pad_maximum_fusion.halo), channel_id=1, source_target_pairs={{0,192},{64,128},{128,64},{192,0},{1,193},{65,129},{129,65},{193,1... | collective-permute-start | bytes 98312 | tf_op jit(solution)/shard_map/ppermute | solution.py:511
  22.6 6.3 %collective-permute-start.8 = (bf16[272,128]{1,0:T(8,128)(2,1)S(1)}, bf16[272,128]{1,0:T(8,128)(2,1)S(1)}, u32[]{:S(2)}, u32[]{:S(2)}) collective-permute-start(bf16[272,128]{1,0:T(8,128)(2,1)S(1)} %get-tuple-element.35), channel_id=1, source_target_pairs={{0,1},{1,0},{2,3},{3,2},{4,5},{5,4},{6,7},{7,6},{8,9},{9,8},{10,11... | collective-permute-start | bytes 208904 | tf_op jit(solution)/shard_map/ppermute | solution.py:505
  24.0 4.9 %collective-permute-start.9 = (bf16[272,128]{1,0:T(8,128)(2,1)S(1)}, bf16[272,128]{1,0:T(8,128)(2,1)S(1)}, u32[]{:S(2)}, u32[]{:S(2)}) collective-permute-start(bf16[272,128]{1,0:T(8,128)(2,1)S(1)} %get-tuple-element.36), channel_id=1, source_target_pairs={{0,3},{1,2},{2,1},{3,0},{4,7},{5,6},{6,5},{7,4},{8,11},{9,10},{10,... | collective-permute-start | bytes 208904 | tf_op jit(solution)/shard_map/ppermute | solution.py:506

commit v3 on v2

--- a/solution.py
+++ b/solution.py
@@ -167,46 +167,36 @@
     return [values[:, t * 128 : t * 128 + 128].astype(F32) for t in range(4)]
 
 
-def pack_body(secondary, own, shift, fraction, first, second, line_rows, shift_v, fraction_v, sems):
+def lead_body(out):
+    out[...] = jnp.zeros_like(out)
+
+
+def pack_body(secondary, own, shift, fraction, lead, first, second, line_rows):
     odd = lax.axis_index("az") % 2 == 1
-    small = [
-        pltpu.make_async_copy(shift, shift_v, sems.at[20]),
-        pltpu.make_async_copy(fraction, fraction_v, sems.at[21]),
-    ]
-    for copy in small:
-        copy.start()
-    copies = []
-    for message, upper in ((first, odd), (second, jnp.logical_not(odd))):
-        line = pl.multiple_of(jnp.where(upper, 0, 16), 16)
-        half = pl.multiple_of(jnp.where(upper, 0, 32), 16)
+
+    def fill(message, line, half):
         for part in range(2):
             for tile in range(4):
-                copies.append(
-                    pltpu.make_async_copy(
-                        secondary.at[0, part, pl.ds(line, 48), pl.ds(tile * 128, 128)],
-                        message.at[pl.ds((2 * tile + part) * 48, 48)],
-                        sems.at[len(copies)],
-                    )
-                )
-            copies.append(
-                pltpu.make_async_copy(
-                    own.at[part, pl.ds(half, 32)],
-                    message.at[pl.ds(384 + part * 32, 32)],
-                    sems.at[len(copies)],
-                )
-            )
-    for copy in copies:
-        copy.start()
-    for copy in small:
-        copy.wait()
-    row_shift = jnp.concatenate([shift_v[...], shift_v[...]], axis=1)
-    row_fraction = jnp.concatenate([fraction_v[...], fraction_v[...]], axis=1)
-    rows = kernel_rows(pltpu.roll(row_shift, 32, 1), pltpu.roll(row_fraction, 32, 1))
+                rows = slice((2 * tile + part) * 48, (2 * tile + part) * 48 + 48)
+                message[rows] = secondary[0, part, line : line + 48, tile * 128 : tile * 128 + 128]
+            message[384 + part * 32 : 416 + part * 32] = own[part, half : half + 32]
+
+    @pl.when(odd)
+    def _():
+        fill(first, 0, 0)
+        fill(second, 16, 32)
+
+    @pl.when(jnp.logical_not(odd))
+    def _():
+        fill(first, 16, 32)
+        fill(second, 0, 0)
+
+    row_shift = jnp.concatenate([shift[...], shift[...]], axis=1)
+    row_fraction = jnp.concatenate([fraction[...], fraction[...]], axis=1)
+    rows = kernel_rows(pltpu.roll(row_shift, 32, 1), pltpu.roll(row_fraction, 32, 1)) + lead[...]
     line_rows[...] = rows
     first[448:464] = rows.astype(BF)
     second[448:464] = rows.astype(BF)
-    for copy in copies:
-        copy.wait()
 
 
 def prepare_body(secondary, own, shift, fraction, *refs):
@@ -494,16 +484,18 @@
     )(*args)
 
 
-def swaps(size):
-    first = [(i, i ^ 1) for i in range(size)]
-    second = [(i, (i + 1) % size if i % 2 == 1 else (i - 1) % size) for i in range(size)]
-    return first, second
-
-
 def exchange(first, second, axis):
-    pairs = swaps(lax.axis_size(axis))
-    received_first = lax.ppermute(first, axis, pairs[0])
-    received_second = lax.ppermute(second, axis, pairs[1])
+    size = lax.axis_size(axis)
+    dates = lax.axis_size("date")
+    pairs = []
+    for date in range(dates):
+        for i in range(size):
+            partner = (date, i + 1 if i % 2 == 1 else i - 1)
+            if i in (0, size - 1):
+                partner = (date ^ 1, i)
+            pairs.append((date * size + i, partner[0] * size + partner[1]))
+    received_first = lax.ppermute(first, axis, [(i, i ^ 1) for i in range(size)])
+    received_second = lax.ppermute(second, ("date", axis), pairs)
     return received_first, received_second
 
 
@@ -514,11 +506,11 @@
 def on_device(reference_slab, secondary, az_shift, az_fraction, rg_shift, rg_fraction):
     own = reference_slab.reshape(2, LINES_DEV, 128)
     message = ((464, 128), BF)
+    lead = call("lead", lead_body, [((16, 128), F32)], cost=2 * 10**9)()[0]
     first, second, line_rows = call(
         "pack", pack_body, [message, message, ((16, 128), F32)],
-        [pltpu.VMEM((1, 64), jnp.int32), pltpu.VMEM((1, 64), F32), pltpu.SemaphoreType.DMA((22,))],
-        hbm=4, cost=10**9,
-    )(secondary, own, az_shift, az_fraction)
+        cost=10**9,
+    )(secondary, own, az_shift, az_fraction, lead)
     tables = [jnp.asarray(table) for table in filter_tables()]
     prepared = call(
         "prepare", prepare_body,

time: 31.9 us -> 26.5 us (0.83)
  the two profiles are of different devices: /device:TPU:1 before, /device:TPU:136 now
where the time goes in v3:
time: 26.5 us; the launch traced here: 26.4 us
  starting transfers between devices  10 us (38%)
  Pallas kernels  8.19 us (31%)
  waiting for transfers between devices  7.04 us (27%)
  local copies, waits for them, and re-layouts  0.93 us (4%)
    pallas_call x7, Pallas kernels, call(): pl.pallas_call(body, name=name, out_shape=[jax.ShapeDtypeStruct(shape, ki...  8.19 us
    ppermute x2, waiting for transfers between devices, exchange(): received_second = lax.ppermute(second, ('date', axis), pairs)  5.26 us
    ppermute x6, starting transfers between devices, date_swaps(): lax.ppermute(values, 'date', [(i, i ^ k) for i in range(4)])  3.92 us
    ppermute x2, starting transfers between devices, exchange(): lax.ppermute(first, axis, [(i, i ^ 1) for i in range(size)])  3.64 us
    ppermute x2, starting transfers between devices, exchange(): received_second = lax.ppermute(second, ('date', axis), pairs)  2.46 us
    ppermute x6, waiting for transfers between devices, date_swaps(): lax.ppermute(values, 'date', [(i, i ^ k) for i in range(4)])  1.77 us
    unnamed x20, local copies, waits for them, and re-layouts  0.93 us
  transfers between devices with their start and end apart: 10, of which 3 were waited for; matrix products, arithmetic and copies ran while one was open for 0% of the time, Pallas kernels for 19%

profile of v3, /device:TPU:136, one launch (start us, length us, event | category | flops | bytes accessed | tf_op | source)
XLA Modules:
  0.0 26.4 jit_solution(400301458535146504)
XLA Ops:
  0.0 0.0 copy-start
  0.0 0.0 copy-start.1
  0.0 0.0 copy-start.4
  0.0 0.0 copy-start.5
  0.0 0.9 %copy-done = bf16[1,2,64,512]{3,2,1,0:T(8,128)(2,1)S(1)} copy-done((bf16[1,2,64,512]{3,2,1,0:T(8,128)(2,1)S(1)}, bf16[1,2,64,512]{3,2,1,0:T(8,128)(2,1)}, u32[]{:S(2)}) %copy-start) | copy-done | bytes 131096
  0.9 0.0 copy-done.1
  0.9 0.0 copy-done.4
  0.9 0.0 copy-done.5
  0.9 0.0 copy-start.2
  0.9 0.0 copy-start.3
  0.9 0.0 copy-start.6
  0.9 0.0 copy-start.7
  1.0 0.0 copy-start.8
  1.0 0.0 copy-start.9
  1.0 0.2 pack.1
  1.2 3.1 %collective-permute-start = (bf16[464,128]{1,0:T(8,128)(2,1)S(1)}, bf16[464,128]{1,0:T(8,128)(2,1)S(1)}, u32[]{:S(2)}, u32[]{:S(2)}) collective-permute-start(bf16[464,128]{1,0:T(8,128)(2,1)S(1)} %get-tuple-element.23), channel_id=1, source_target_pairs={{0,4},{4,0},{8,12},{12,8},{16,20},{20,16},{24,28},{28,24},{32,36},... | collective-permute-start | bytes 356360 | tf_op jit(solution)/shard_map/ppermute | solution.py:497
  4.3 0.1 collective-permute-start.1
  4.4 0.0 copy-done.2
  4.4 0.0 copy-done.3
  4.4 0.0 copy-done.6
  4.4 0.0 copy-done.7
  4.4 0.0 copy-done.8
  4.4 0.0 copy-done.9
  4.4 1.2 %prepare.1 = (bf16[1,2,64,512]{3,2,1,0:T(8,128)(2,1)S(1)}, bf16[2,64,128]{2,1,0:T(8,128)(2,1)S(1)}, f32[16,512]{1,0:T(8,128)S(1)}, bf16[7,128,128]{2,1,0:T(8,128...) custom-call(bf16[1,2,64,512]{3,2,1,0:T(8,128)(2,1)S(1)} %copy-done, ...), custom_call_target="tpu_custom_call" | custom-call | flops 2000000000 | bytes 20000000 | tf_op jit(solution)/shard_map/prepare/pallas_call | solution.py:475
  5.6 0.1 collective-permute-start.2
  5.7 1.6 %collective-permute-start.3 = (bf16[2,64,128]{2,1,0:T(8,128)(2,1)S(1)}, bf16[2,64,128]{2,1,0:T(8,128)(2,1)S(1)}, u32[]{:S(2)}, u32[]{:S(2)}) collective-permute-start(bf16[2,64,128]{2,1,0:T(8,128)(2,1)S(1)} %get-tuple-element.27.own), channel_id=1, source_target_pairs={{0,128},{64,192},{128,0},{192,64},{1,129},{65,193},{129,1},{193,65... | collective-permute-start | bytes 98312 | tf_op jit(solution)/shard_map/ppermute | solution.py:503
  7.3 0.3 %collective-permute-start.4 = (bf16[2,64,128]{2,1,0:T(8,128)(2,1)S(1)}, bf16[2,64,128]{2,1,0:T(8,128)(2,1)S(1)}, u32[]{:S(2)}, u32[]{:S(2)}) collective-permute-start(bf16[2,64,128]{2,1,0:T(8,128)(2,1)S(1)} %get-tuple-element.27.own), channel_id=1, source_target_pairs={{0,192},{64,128},{128,64},{192,0},{1,193},{65,129},{129,65},{193,1... | collective-permute-start | bytes 98312 | tf_op jit(solution)/shard_map/ppermute | solution.py:503
  7.6 5.3 %collective-permute-done.1.second = bf16[464,128]{1,0:T(8,128)(2,1)S(1)} collective-permute-done((bf16[464,128]{1,0:T(8,128)(2,1)S(1)}, bf16[464,128]{1,0:T(8,128)(2,1)S(1)}, u32[]{:S(2)}, u32[]{:S(2)}) %collective-permute-start.1) | collective-permute-done | bytes 118816 | tf_op jit(solution)/shard_map/ppermute | solution.py:498
  12.9 0.0 collective-permute-done.first
  12.9 0.1 collective-permute-start.5
  13.0 0.7 %collective-permute-start.6 = (bf16[128,128]{1,0:T(8,128)(2,1)S(1)}, bf16[128,128]{1,0:T(8,128)(2,1)S(1)}, u32[]{:S(2)}, u32[]{:S(2)}) collective-permute-start(bf16[128,128]{1,0:T(8,128)(2,1)S(1)} %pad_maximum_fusion.halo), channel_id=1, source_target_pairs={{0,128},{64,192},{128,0},{192,64},{1,129},{65,193},{129,1},{193,65... | collective-permute-start | bytes 98312 | tf_op jit(solution)/shard_map/ppermute | solution.py:503
  13.7 0.0 collective-permute-done.2.peer1
  13.7 1.2 %collective-permute-start.7 = (bf16[128,128]{1,0:T(8,128)(2,1)S(1)}, bf16[128,128]{1,0:T(8,128)(2,1)S(1)}, u32[]{:S(2)}, u32[]{:S(2)}) collective-permute-start(bf16[128,128]{1,0:T(8,128)(2,1)S(1)} %pad_maximum_fusion.halo), channel_id=1, source_target_pairs={{0,192},{64,128},{128,64},{192,0},{1,193},{65,129},{129,65},{193,1... | collective-permute-start | bytes 98312 | tf_op jit(solution)/shard_map/ppermute | solution.py:503
  14.9 0.7 %lines.1 = (bf16[256,256]{1,0:T(8,128)(2,1)S(1)}, f32[7,256,128]{2,1,0:T(8,128)S(1)}) custom-call(bf16[1,2,64,512]{3,2,1,0:T(8,128)(2,1)S(1)} %get-tuple-element.21.secondary, f32[16,128]{1,0:T(8,128)S(1)} %get-tuple-element.22.line_rows, bf16[464,128]{1,0:T(8,128)(2,1)S(1)} %collective-permute-done.first, ...), custom_call_target="tpu_custom_call" | custom-call | flops 1000000000 | bytes 10000000 | tf_op jit(solution)/shard_map/lines/pallas_call | solution.py:475
  15.6 0.0 collective-permute-done.3.peer2
  15.6 0.0 collective-permute-done.4.peer3
  15.6 0.0 collective-permute-done.5.halo1
  15.6 1.7 %collective-permute-done.6.halo2 = bf16[128,128]{1,0:T(8,128)(2,1)S(1)} collective-permute-done((bf16[128,128]{1,0:T(8,128)(2,1)S(1)}, bf16[128,128]{1,0:T(8,128)(2,1)S(1)}, u32[]{:S(2)}, u32[]{:S(2)}) %collective-permute-start.6) | collective-permute-done | bytes 32800 | tf_op jit(solution)/shard_map/ppermute | solution.py:503
  17.3 0.1 collective-permute-done.7.halo3
  17.4 0.2 reference.1
  17.6 0.5 %collective-permute-start.8 = (bf16[272,128]{1,0:T(8,128)(2,1)S(1)}, bf16[272,128]{1,0:T(8,128)(2,1)S(1)}, u32[]{:S(2)}, u32[]{:S(2)}) collective-permute-start(bf16[272,128]{1,0:T(8,128)(2,1)S(1)} %get-tuple-element.35), channel_id=1, source_target_pairs={{0,1},{1,0},{2,3},{3,2},{4,5},{5,4},{6,7},{7,6},{8,9},{9,8},{10,11... | collective-permute-start | bytes 208904 | tf_op jit(solution)/shard_map/ppermute | solution.py:497
  18.1 2.4 %collective-permute-start.9 = (bf16[272,128]{1,0:T(8,128)(2,1)S(1)}, bf16[272,128]{1,0:T(8,128)(2,1)S(1)}, u32[]{:S(2)}, u32[]{:S(2)}) collective-permute-start(bf16[272,128]{1,0:T(8,128)(2,1)S(1)} %get-tuple-element.36), channel_id=1, source_target_pairs={{0,64},{1,2},{2,1},{3,67},{64,0},{65,66},{66,65},{67,3},{128,192},... | collective-permute-start | bytes 208904 | tf_op jit(solution)/shard_map/ppermute | solution.py:498
  20.6 3.0 %interior.1.part = f32[1,2,64,512]{3,2,1,0:T(8,128)S(1)} custom-call(f32[7,256,128]{2,1,0:T(8,128)S(1)} %get-tuple-element.26.resampled, bf16[256,512]{1,0:T(8,128)(2,1)S(1)} %get-tuple-element.30.master, bf16[768,256]{1,0:T(8,128)(2,1)S(1)} %get-tuple-element.31.forward, bf16[384,768]{1,0:T(8,128)(2,1)S(1)} %get-tuple-element.32.lines, ...), custom_call_target="tpu_custom_call" | custom-call | flops 4000000000 | bytes 40000000 | tf_op jit(solution)/shard_map/interior/pallas_call | solution.py:475
  23.6 0.0 collective-permute-done.8.first
  23.6 0.0 collective-permute-done.9.second
  23.6 2.8 %edge.1 = f32[1,2,64,512]{3,2,1,0:T(8,128)} custom-call(f32[1,2,64,512]{3,2,1,0:T(8,128)S(1)} %interior.1.part, bf16[256,256]{1,0:T(8,128)(2,1)S(1)} %get-tuple-element.28.edges, bf16[256,512]{1,0:T(8,128)(2,1)S(1)} %get-tuple-element.30.master, f32[16,512]{1,0:T(8,128)S(1)} %get-tuple-element.29.sample_rows, ...), custom_call_target="tpu_custom_call" | custom-call | flops 1000000000 | bytes 10000000 | tf_op jit(solution)/shard_map/edge/pallas_call | solution.py:475
  (4 shorter events, 0.0 us)
Async XLA Ops:
  0.0 0.9 %copy-start = (bf16[1,2,64,512]{3,2,1,0:T(8,128)(2,1)S(1)}, bf16[1,2,64,512]{3,2,1,0:T(8,128)(2,1)}, u32[]{:S(2)}) copy-start(bf16[1,2,64,512]{3,2,1,0:T(8,128)(2,1)} %secondary.3) | copy-start | bytes 393220
  0.0 0.9 %copy-start.1 = (bf16[2,64,1,128]{3,1,2,0:T(8,128)(2,1)S(1)}, bf16[2,64,1,128]{3,1,2,0:T(8,128)(2,1)}, u32[]{:S(2)}) copy-start(bf16[2,64,1,128]{3,1,2,0:T(8,128)(2,1)} %param.10) | copy-start | bytes 98308
  0.0 0.9 %copy-start.4 = (s32[1,64]{1,0:T(1,128)S(1)}, s32[1,64]{1,0:T(1,128)}, u32[]{:S(2)}) copy-start(s32[1,64]{1,0:T(1,128)} %shift.3) | copy-start | bytes 772
  0.0 0.9 %copy-start.5 = (f32[1,64]{1,0:T(1,128)S(1)}, f32[1,64]{1,0:T(1,128)}, u32[]{:S(2)}) copy-start(f32[1,64]{1,0:T(1,128)} %fraction.3) | copy-start | bytes 772
  0.9 3.5 %copy-start.2 = (s32[1,512]{1,0:T(1,128)S(1)}, s32[1,512]{1,0:T(1,128)}, u32[]{:S(2)}) copy-start(s32[1,512]{1,0:T(1,128)} %shift.2) | copy-start | bytes 6148
  0.9 3.5 %copy-start.3 = (f32[1,512]{1,0:T(1,128)S(1)}, f32[1,512]{1,0:T(1,128)}, u32[]{:S(2)}) copy-start(f32[1,512]{1,0:T(1,128)} %fraction.2) | copy-start | bytes 6148
  0.9 3.5 %copy-start.6 = (bf16[3072,256]{1,0:T(8,128)(2,1)S(1)}, bf16[3072,256]{1,0:T(8,128)(2,1)}, u32[]{:S(2)}) copy-start(bf16[3072,256]{1,0:T(8,128)(2,1)} %constant.11.clone.refs_3_) | copy-start | bytes 4718596
  0.9 3.5 %copy-start.7 = (bf16[384,768]{1,0:T(8,128)(2,1)S(1)}, bf16[384,768]{1,0:T(8,128)(2,1)}, u32[]{:S(2)}) copy-start(bf16[384,768]{1,0:T(8,128)(2,1)} %constant.9.clone.refs_1_) | copy-start | bytes 1769476
  1.0 3.4 %copy-start.8 = (bf16[768,256]{1,0:T(8,128)(2,1)S(1)}, bf16[768,256]{1,0:T(8,128)(2,1)}, u32[]{:S(2)}) copy-start(bf16[768,256]{1,0:T(8,128)(2,1)} %constant.8.clone.refs_0_) | copy-start | bytes 1179652
  1.0 3.4 %copy-start.9 = (bf16[128,1152]{1,0:T(8,128)(2,1)S(1)}, bf16[128,1152]{1,0:T(8,128)(2,1)}, u32[]{:S(2)}) copy-start(bf16[128,1152]{1,0:T(8,128)(2,1)} %constant.10.clone.refs_2_) | copy-start | bytes 884740
  1.2 11.7 %collective-permute-start = (bf16[464,128]{1,0:T(8,128)(2,1)S(1)}, bf16[464,128]{1,0:T(8,128)(2,1)S(1)}, u32[]{:S(2)}, u32[]{:S(2)}) collective-permute-start(bf16[464,128]{1,0:T(8,128)(2,1)S(1)} %get-tuple-element.23), channel_id=1, source_target_pairs={{0,4},{4,0},{8,12},{12,8},{16,20},{20,16},{24,28},{28,24},{32,36},... | collective-permute-start | bytes 356360 | tf_op jit(solution)/shard_map/ppermute | solution.py:497
  4.3 8.5 %collective-permute-start.1 = (bf16[464,128]{1,0:T(8,128)(2,1)S(1)}, bf16[464,128]{1,0:T(8,128)(2,1)S(1)}, u32[]{:S(2)}, u32[]{:S(2)}) collective-permute-start(bf16[464,128]{1,0:T(8,128)(2,1)S(1)} %get-tuple-element.24), channel_id=1, source_target_pairs={{0,64},{4,8},{8,4},{12,16},{16,12},{20,24},{24,20},{28,32},{32,28}... | collective-permute-start | bytes 356360 | tf_op jit(solution)/shard_map/ppermute | solution.py:498
  5.6 8.1 %collective-permute-start.2 = (bf16[2,64,128]{2,1,0:T(8,128)(2,1)S(1)}, bf16[2,64,128]{2,1,0:T(8,128)(2,1)S(1)}, u32[]{:S(2)}, u32[]{:S(2)}) collective-permute-start(bf16[2,64,128]{2,1,0:T(8,128)(2,1)S(1)} %get-tuple-element.27.own), channel_id=1, source_target_pairs={{0,64},{64,0},{128,192},{192,128},{1,65},{65,1},{129,193},{193,129... | collective-permute-start | bytes 98312 | tf_op jit(solution)/shard_map/ppermute | solution.py:503
  5.7 9.8 %collective-permute-start.3 = (bf16[2,64,128]{2,1,0:T(8,128)(2,1)S(1)}, bf16[2,64,128]{2,1,0:T(8,128)(2,1)S(1)}, u32[]{:S(2)}, u32[]{:S(2)}) collective-permute-start(bf16[2,64,128]{2,1,0:T(8,128)(2,1)S(1)} %get-tuple-element.27.own), channel_id=1, source_target_pairs={{0,128},{64,192},{128,0},{192,64},{1,129},{65,193},{129,1},{193,65... | collective-permute-start | bytes 98312 | tf_op jit(solution)/shard_map/ppermute | solution.py:503
  7.3 8.3 %collective-permute-start.4 = (bf16[2,64,128]{2,1,0:T(8,128)(2,1)S(1)}, bf16[2,64,128]{2,1,0:T(8,128)(2,1)S(1)}, u32[]{:S(2)}, u32[]{:S(2)}) collective-permute-start(bf16[2,64,128]{2,1,0:T(8,128)(2,1)S(1)} %get-tuple-element.27.own), channel_id=1, source_target_pairs={{0,192},{64,128},{128,64},{192,0},{1,193},{65,129},{129,65},{193,1... | collective-permute-start | bytes 98312 | tf_op jit(solution)/shard_map/ppermute | solution.py:503
  12.9 2.7 %collective-permute-start.5 = (bf16[128,128]{1,0:T(8,128)(2,1)S(1)}, bf16[128,128]{1,0:T(8,128)(2,1)S(1)}, u32[]{:S(2)}, u32[]{:S(2)}) collective-permute-start(bf16[128,128]{1,0:T(8,128)(2,1)S(1)} %pad_maximum_fusion.halo), channel_id=1, source_target_pairs={{0,64},{64,0},{128,192},{192,128},{1,65},{65,1},{129,193},{193,129... | collective-permute-start | bytes 98312 | tf_op jit(solution)/shard_map/ppermute | solution.py:503
  13.0 4.3 %collective-permute-start.6 = (bf16[128,128]{1,0:T(8,128)(2,1)S(1)}, bf16[128,128]{1,0:T(8,128)(2,1)S(1)}, u32[]{:S(2)}, u32[]{:S(2)}) collective-permute-start(bf16[128,128]{1,0:T(8,128)(2,1)S(1)} %pad_maximum_fusion.halo), channel_id=1, source_target_pairs={{0,128},{64,192},{128,0},{192,64},{1,129},{65,193},{129,1},{193,65... | collective-permute-start | bytes 98312 | tf_op jit(solution)/shard_map/ppermute | solution.py:503
  13.7 3.7 %collective-permute-start.7 = (bf16[128,128]{1,0:T(8,128)(2,1)S(1)}, bf16[128,128]{1,0:T(8,128)(2,1)S(1)}, u32[]{:S(2)}, u32[]{:S(2)}) collective-permute-start(bf16[128,128]{1,0:T(8,128)(2,1)S(1)} %pad_maximum_fusion.halo), channel_id=1, source_target_pairs={{0,192},{64,128},{128,64},{192,0},{1,193},{65,129},{129,65},{193,1... | collective-permute-start | bytes 98312 | tf_op jit(solution)/shard_map/ppermute | solution.py:503
  17.6 6.0 %collective-permute-start.8 = (bf16[272,128]{1,0:T(8,128)(2,1)S(1)}, bf16[272,128]{1,0:T(8,128)(2,1)S(1)}, u32[]{:S(2)}, u32[]{:S(2)}) collective-permute-start(bf16[272,128]{1,0:T(8,128)(2,1)S(1)} %get-tuple-element.35), channel_id=1, source_target_pairs={{0,1},{1,0},{2,3},{3,2},{4,5},{5,4},{6,7},{7,6},{8,9},{9,8},{10,11... | collective-permute-start | bytes 208904 | tf_op jit(solution)/shard_map/ppermute | solution.py:497
  18.1 5.5 %collective-permute-start.9 = (bf16[272,128]{1,0:T(8,128)(2,1)S(1)}, bf16[272,128]{1,0:T(8,128)(2,1)S(1)}, u32[]{:S(2)}, u32[]{:S(2)}) collective-permute-start(bf16[272,128]{1,0:T(8,128)(2,1)S(1)} %get-tuple-element.36), channel_id=1, source_target_pairs={{0,64},{1,2},{2,1},{3,67},{64,0},{65,66},{66,65},{67,3},{128,192},... | collective-permute-start | bytes 208904 | tf_op jit(solution)/shard_map/ppermute | solution.py:498

commit v4 on v3

v4 whole, which is shorter than its diff:
```python
import functools

import jax
import jax.numpy as jnp
import ml_dtypes
import numpy as np
from jax import lax
from jax.experimental import pallas as pl
from jax.experimental.pallas import tpu as pltpu
from jax.sharding import PartitionSpec as P

PATCH = 64
HALF = 32
TAPS = 8
MARGIN = 48
LINES_DEV = 64
SAMPLES_DEV = 512
BF = jnp.bfloat16
F32 = jnp.float32
VMEM_LIMIT = 32 * 1024 * 1024


def split_table(table):
    high = table.astype(ml_dtypes.bfloat16)
    low = (table - high.astype(np.float64)).astype(ml_dtypes.bfloat16)
    return high, low


def hann(position):
    return np.minimum(position + 0.5, PATCH - 0.5 - position) / HALF


def sample_forward():
    table = np.zeros((2, 128, 2, 64, 2))
    v = np.arange(64)
    for p in range(2):
        for m in range(64):
            angle = 2 * np.pi * ((v * m) % 64) / 64
            n = m + 32 * p
            table[0, n, 0, :, p] = np.cos(angle)
            table[1, n, 0, :, p] = np.sin(angle)
            table[0, n, 1, :, p] = -np.sin(angle)
            table[1, n, 1, :, p] = np.cos(angle)
    return table.reshape(256, 256)


def line_forward():
    table = np.zeros((2, 64, 2, 64))
    u = np.arange(64)
    for m in range(64):
        angle = 2 * np.pi * ((u * m) % 64) / 64
        table[0, :, 0, m] = np.cos(angle)
        table[0, :, 1, m] = np.sin(angle)
        table[1, :, 0, m] = -np.sin(angle)
        table[1, :, 1, m] = np.cos(angle)
    return table.reshape(128, 128)


def line_inverse():
    table = np.zeros((2, 2, 32, 2, 64))
    u = np.arange(64)
    for m in range(64):
        angle = 2 * np.pi * ((u * m) % 64) / 64
        weight = hann(m) / 64
        table[m // 32, 0, m % 32, 0, :] = weight * np.cos(angle)
        table[m // 32, 0, m % 32, 1, :] = -weight * np.sin(angle)
        table[m // 32, 1, m % 32, 0, :] = weight * np.sin(angle)
        table[m // 32, 1, m % 32, 1, :] = weight * np.cos(angle)
    return table.reshape(128, 128)


def sample_inverse(start):
    table = np.zeros((2, 64, 2, 2, 128))
    v = np.arange(64)
    for p in range(2):
        for y in range(128):
            n = 32 + y - start - 32 * p
            if 0 <= n < 64:
                angle = 2 * np.pi * ((v * n) % 64) / 64
                weight = hann(n) / 64
                table[0, :, p, 0, y] = weight * np.cos(angle)
                table[1, :, p, 0, y] = -weight * np.sin(angle)
                table[0, :, p, 1, y] = weight * np.sin(angle)
                table[1, :, p, 1, y] = weight * np.cos(angle)
    return table.reshape(256, 256)


def triple(table, axis):
    high, low = split_table(table)
    return np.concatenate([high, high, low], axis=axis)


def filter_tables():
    inverse = [sample_inverse(start) for start in (0, 64, 128, 96)]
    return [
        triple(sample_forward(), 0),
        triple(line_forward(), 1),
        triple(line_inverse(), 1),
        np.concatenate([triple(table, 0) for table in inverse], axis=0),
    ]


def sinc_rows(fraction):
    tap = lax.broadcasted_iota(jnp.int32, (TAPS, fraction.shape[1]), 0)
    distance = fraction - (tap - (TAPS // 2 - 1)).astype(F32)
    centre = distance == 0.0
    sign = jnp.where(tap % 2 == 1, 1.0, -1.0)
    wave = sign * jnp.sin(np.float32(np.pi) * fraction)
    sinc = wave / jnp.where(centre, 1.0, np.float32(np.pi) * distance)
    sinc = jnp.where(centre, 1.0, sinc)
    taper = 0.5 + 0.5 * jnp.cos(np.float32(np.pi) * distance / (TAPS // 2))
    return (sinc * taper).astype(BF).astype(F32)


def kernel_rows(shift, fraction):
    weights = sinc_rows(fraction)
    row = lax.broadcasted_iota(jnp.int32, weights.shape, 0)
    shifts = jnp.where(row == 0, shift.astype(F32), 0.0)
    return jnp.concatenate([weights, shifts], axis=0)


def band_matrix(rows, depth):
    width = rows.shape[1]
    shift = rows[TAPS : TAPS + 1].astype(jnp.int32)
    source = lax.broadcasted_iota(jnp.int32, (depth, width), 0)
    target = lax.broadcasted_iota(jnp.int32, (depth, width), 1)
    step = source - (target + 13 + shift)
    matrix = jnp.zeros((depth, width), F32)
    for k in range(TAPS):
        matrix = jnp.where(step == k, rows[k : k + 1], matrix)
    return matrix


def split(values):
    high = values.astype(BF)
    return high, (values - high.astype(F32)).astype(BF)


def dot(left, right):
    return jnp.dot(left, right, preferred_element_type=F32)


def columns_triple(values):
    high, low = split(values)
    return jnp.concatenate([high, low, high], axis=1)


def rows_triple(values):
    high, low = split(values)
    return jnp.concatenate([high, low, high], axis=0)


def shifted(tiles, start):
    index, offset = start // 128, start % 128
    here = pltpu.roll(tiles[index], 128 - offset, 1)
    after = pltpu.roll(tiles[min(index + 1, 3)], 128 - offset, 1)
    lane = lax.broadcasted_iota(jnp.int32, here.shape, 1)
    return jnp.where(lane < 128 - offset, here, after)


def tiles_of(values):
    return [values[:, t * 128 : t * 128 + 128].astype(F32) for t in range(4)]


def lead_body(out):
    out[...] = jnp.zeros_like(out)


def pack_body(secondary, own, shift, fraction, lead, first, second, line_rows):
    odd = lax.axis_index("az") % 2 == 1

    def fill(message, line, half):
        for part in range(2):
            for tile in range(4):
                rows = slice((2 * tile + part) * 48, (2 * tile + part) * 48 + 48)
                message[rows] = secondary[0, part, line : line + 48, tile * 128 : tile * 128 + 128]
            message[384 + part * 32 : 416 + part * 32] = own[part, half : half + 32]

    @pl.when(odd)
    def _():
        fill(first, 0, 0)
        fill(second, 16, 32)

    @pl.when(jnp.logical_not(odd))
    def _():
        fill(first, 16, 32)
        fill(second, 0, 0)

    row_shift = jnp.concatenate([shift[...], shift[...]], axis=1)
    row_fraction = jnp.concatenate([fraction[...], fraction[...]], axis=1)
    rows = kernel_rows(pltpu.roll(row_shift, 32, 1), pltpu.roll(row_fraction, 32, 1)) + lead[...]
    line_rows[...] = rows
    first[448:464] = rows.astype(BF)
    second[448:464] = rows.astype(BF)


def prepare_body(secondary, own, shift, fraction, *refs):
    tables, outs = refs[0:4], refs[4:13]
    secondary_v, own_v, sample_rows, bands = outs[0:4]
    tables_v = outs[4:8]
    shift_v, fraction_v, sems = outs[8], refs[13], refs[14]
    pairs = [(shift, shift_v), (fraction, fraction_v), (own, own_v), (secondary, secondary_v)]
    pairs.extend(zip(tables, tables_v))
    copies = [
        pltpu.make_async_copy(source, target, sems.at[at]) for at, (source, target) in enumerate(pairs)
    ]
    for copy in copies:
        copy.start()
    for copy in copies[:2]:
        copy.wait()
    samples = kernel_rows(shift_v[...], fraction_v[...])
    sample_rows[...] = samples
    tiles = tiles_of(samples)
    for j in range(1, 8):
        bands[j - 1] = band_matrix(shifted(tiles, 64 * j - 32), 128).astype(BF)
    for copy in copies[2:]:
        copy.wait()


def lines_body(secondary, line_rows, first, second, bands, edges, resampled, late, extended, halo_rows):
    odd = lax.axis_index("az") % 2 == 1
    has_top = lax.axis_index("az") > 0
    has_bottom = lax.axis_index("az") < lax.axis_size("az") - 1

    def place(top, bottom):
        for part in range(2):
            for tile in range(4):
                rows = slice((2 * tile + part) * 48, (2 * tile + part) * 48 + 48)
                lanes = slice(tile * 128, tile * 128 + 128)
                extended[part, 0:48, lanes] = top[rows]
                extended[part, 112:160, lanes] = bottom[rows]
        halo_rows[0] = top[448:464].astype(F32)
        halo_rows[1] = bottom[448:464].astype(F32)

    @pl.when(odd)
    def _():
        place(first, second)

    @pl.when(jnp.logical_not(odd))
    def _():
        place(second, first)

    late[0:64] = first[384:448]
    late[64:128] = second[384:448]
    for part in range(2):
        extended[part, 48:112] = secondary[0, part]

    lane = lax.broadcasted_iota(jnp.int32, (16, 128), 1)
    rows = jnp.where(
        lane < 32,
        pltpu.roll(halo_rows[0], 64, 1),
        jnp.where(lane < 96, line_rows[...], pltpu.roll(halo_rows[1], 64, 1)),
    )
    matrix = band_matrix(rows, 160)
    line = lax.broadcasted_iota(jnp.int32, matrix.shape, 0)
    low = jnp.where(has_top, 0, 48)
    high = jnp.where(has_bottom, 160, 112)
    matrix = jnp.where((line >= low) & (line < high), matrix, 0.0).astype(BF)
    values = [
        lax.dot_general(
            matrix, extended[part], (((0,), (0,)), ((), ())), preferred_element_type=F32
        )
        for part in range(2)
    ]
    values = jnp.concatenate(values, axis=0).astype(BF)
    edges[:, 0:128] = values[:, 0:128]
    edges[:, 128:256] = values[:, 384:512]
    tiles = tiles_of(values)
    for j in range(1, 8):
        resampled[j - 1] = dot(shifted(tiles, 64 * j - 48).astype(BF), bands[j - 1])


def by_date(pieces, store):
    date = lax.axis_index("date")
    for value in range(4):

        @pl.when(date == value)
        def _():
            for offset in range(4):
                place = (value ^ offset) * 128
                store(pieces[offset], slice(place, place + 128))


def root(values):
    return values * lax.rsqrt(jnp.maximum(values, np.float32(1e-36)))


def sample_columns(real, imag, master_real, master_imag, forward):
    product = jnp.concatenate(
        [master_real * real + master_imag * imag, master_imag * real - master_real * imag], axis=1
    )
    columns = dot(columns_triple(product), forward)
    return columns[:, :128], columns[:, 128:]


def response_of(spectrum):
    real, imag = spectrum[:64], spectrum[64:]
    smooth = root(real * real + imag * imag)
    smooth = smooth + pltpu.roll(smooth, 2, 1) + pltpu.roll(smooth, 126, 1)
    smooth = smooth + pltpu.roll(smooth, 1, 0) + pltpu.roll(smooth, 63, 0)
    return root(smooth)


def window_scales(responses):
    sums = jnp.concatenate(
        [jnp.sum(values.reshape(8, 8, 128), axis=0) for values in responses], axis=0
    )
    high, low = split(sums)
    row = lax.broadcasted_iota(jnp.int32, (256, 128), 0)
    lane = lax.broadcasted_iota(jnp.int32, (256, 128), 1)
    same = jnp.where((row - lane) % 2 == 0, 1.0, 0.0).astype(BF)
    totals = dot(jnp.concatenate([high, low], axis=1), same)
    scales = []
    for at in range(len(responses)):
        total = jnp.sum(totals[8 * at : 8 * at + 8], axis=0, keepdims=True)
        scales.append(1.0 / (total * np.float32(1 / 4096) + np.float32(3e-06)))
    return scales


def filter_band(highs, lows, lines, inverse):
    stacked = [jnp.concatenate([high, low, high], axis=0) for high, low in zip(highs, lows)]
    spectrum = dot(lines, jnp.concatenate(stacked, axis=1))
    spectra = [spectrum[:, at * 128 : at * 128 + 128] for at in range(len(highs))]
    responses = [response_of(values) for values in spectra]
    gained = [
        rows_triple(values * jnp.concatenate([response, response], axis=0))
        for values, response in zip(spectra, responses)
    ]
    back = dot(inverse, jnp.concatenate(gained, axis=1))
    scales = window_scales(responses)
    return [
        back[:, at * 128 : at * 128 + 128] * scales[at] for at in range(len(highs))
    ]


def pair_rows(top, bottom):
    real = jnp.concatenate([top[:32], bottom[:32]], axis=0)
    imag = jnp.concatenate([top[32:], bottom[32:]], axis=0)
    return columns_triple(jnp.concatenate([real, imag], axis=1))


def early_body(own, peer1, peer2, peer3, resampled, forward, lines, inverse,
               master, column_high, column_low, back):
    def store(piece, lanes):
        master[0:64, lanes] = piece[0]
        master[64:128, lanes] = piece[1]

    by_date((own, peer1, peer2, peer3), store)
    tiles = tiles_of(master)
    highs, lows = [], []
    for j in range(1, 8):
        around = shifted(tiles, 64 * j - 32)
        real, imag = sample_columns(
            resampled[j - 1, 32:96], resampled[j - 1, 160:224], around[:64], around[64:], forward[...]
        )
        high, low = split(jnp.concatenate([real, imag], axis=0))
        column_high[j - 1] = high
        column_low[j - 1] = low
        highs.append(high)
        lows.append(low)
    middle = filter_band(highs, lows, lines[...], inverse[...])
    for j in range(1, 8):
        back[j - 1] = middle[j - 1]


def reference_body(halo, halo1, halo2, halo3, master, edges, sample_rows,
                   around, send_first, send_second):
    az = lax.axis_index("az")
    odd = az % 2 == 1

    def store(piece, lanes):
        @pl.when(odd)
        def _():
            for part in range(2):
                around[part * 64 : part * 64 + 32, lanes] = piece[part * 32 : part * 32 + 32]
                around[part * 64 + 32 : part * 64 + 64, lanes] = piece[64 + part * 32 : 96 + part * 32]

        @pl.when(jnp.logical_not(odd))
        def _():
            for part in range(2):
                around[part * 64 : part * 64 + 32, lanes] = piece[64 + part * 32 : 96 + part * 32]
                around[part * 64 + 32 : part * 64 + 64, lanes] = piece[part * 32 : part * 32 + 32]

    by_date((halo, halo1, halo2, halo3), store)

    @pl.when(az == 0)
    def _():
        for part in range(2):
            around[part * 64 : part * 64 + 32] = jnp.zeros((32, 512), BF)

    @pl.when(az == lax.axis_size("az") - 1)
    def _():
        for part in range(2):
            around[part * 64 + 32 : part * 64 + 64] = jnp.zeros((32, 512), BF)

    lane = lax.broadcasted_iota(jnp.int32, (128, 128), 1)
    narrow = lax.broadcasted_iota(jnp.int32, (32, 128), 1)

    def message(tile, edge, turn):
        lanes = slice(tile * 128, tile * 128 + 128)
        rows = edges[:, edge * 128 : edge * 128 + 128].astype(F32)
        own, far = master[:, lanes].astype(F32), around[:, lanes].astype(F32)
        real = jnp.concatenate([far[:32], own[:64], far[32:64]], axis=0)
        imag = jnp.concatenate([far[64:96], own[64:], far[96:]], axis=0)
        wide = jnp.where(
            lane < 48,
            pltpu.roll(rows[:128], turn[0], 1) if turn[0] else rows[:128],
            jnp.where(
                lane < 96,
                pltpu.roll(rows[128:], turn[1], 1),
                pltpu.roll(real, turn[2], 1) if turn[2] else real,
            ),
        )
        tail = pltpu.roll(imag[:32], (turn[2] + 32) % 128, 1)
        for group in range(1, 4):
            step = (turn[2] + 32 + 32 * group) % 128
            part = imag[32 * group : 32 * group + 32]
            tail = jnp.where(
                narrow < 32 * group, tail, pltpu.roll(part, step, 1) if step else part
            )
        return wide.astype(BF), tail.astype(BF), sample_rows[:, lanes].astype(BF)

    to_right = message(3, 1, (48, 96, 0))
    to_left = message(0, 0, (0, 48, 96))
    rg_odd = lax.axis_index("rg") % 2 == 1

    def send(target, parts):
        target[0:128], target[128:160], target[160:176] = parts

    @pl.when(rg_odd)
    def _():
        send(send_first, to_left)
        send(send_second, to_right)

    @pl.when(jnp.logical_not(rg_odd))
    def _():
        send(send_first, to_right)
        send(send_second, to_left)


def interior_body(resampled, master, column_high, column_low, middle, forward, lines, inverse,
                  samples, out):
    tiles = tiles_of(master)
    upper_high, upper_low, lower_high, lower_low = [], [], [], []
    for j in range(1, 8):
        around = shifted(tiles, 64 * j - 32)
        values = resampled.at[j - 1]
        real, imag = sample_columns(
            jnp.concatenate([values[0:32], values[96:128]], axis=0),
            jnp.concatenate([values[128:160], values[224:256]], axis=0),
            around[:64], around[64:], forward[...],
        )
        real, imag = split(real), split(imag)
        for which, own, upper, lower in (
            (0, column_high, upper_high, lower_high), (1, column_low, upper_low, lower_low)
        ):
            held = own.at[j - 1]
            upper.append(jnp.concatenate(
                [real[which][:32], held[0:32], imag[which][:32], held[64:96]], axis=0))
            lower.append(jnp.concatenate(
                [held[32:64], real[which][32:], held[96:128], imag[which][32:]], axis=0))
    upper = filter_band(upper_high, upper_low, lines[...], inverse[64:128])
    lower = filter_band(lower_high, lower_low, lines[...], inverse[0:64])
    parts = []
    for j in range(1, 8):
        tops = middle[j - 1, 0:64] + upper[j - 1]
        bottoms = middle[j - 1, 64:128] + lower[j - 1]
        if j == 7:
            lane = lax.broadcasted_iota(jnp.int32, tops.shape, 1)
            tops = jnp.where(lane % 2 == 0, tops, 0.0)
            bottoms = jnp.where(lane % 2 == 0, bottoms, 0.0)
        parts.append(pair_rows(tops, bottoms))
    for block in range(4):
        used = [j for j in (2 * block, 2 * block + 1, 2 * block + 2) if 1 <= j <= 7]
        start = (used[0] - 2 * block) * 768
        values = dot(
            jnp.concatenate([parts[j - 1] for j in used], axis=1),
            samples[start : start + 768 * len(used)],
        )
        out[0, 0, :, block * 128 : block * 128 + 128] = values[:, :128]
        out[0, 1, :, block * 128 : block * 128 + 128] = values[:, 128:]


def edge_body(part, edges, master, around, sample_rows, first, second, forward, lines, inverse,
              samples, out, sides, sems):
    centre = pltpu.make_async_copy(
        part.at[:, :, :, 128:384], out.at[:, :, :, 128:384], sems.at[0]
    )
    centre.start()
    rg = lax.axis_index("rg")
    odd = rg % 2 == 1
    first_f = first[...].astype(F32)
    second_f = second[...].astype(F32)
    has_left = jnp.where(rg > 0, 1.0, 0.0).astype(F32)
    has_right = jnp.where(rg < lax.axis_size("rg") - 1, 1.0, 0.0).astype(F32)
    from_left = jnp.where(odd, first_f, second_f) * has_left
    from_right = jnp.where(odd, second_f, first_f) * has_right

    def turned(values, step):
        return pltpu.roll(values, step % 128, 1) if step % 128 else values

    def block(message, tile, edge, cuts, reverse):
        lanes = slice(tile * 128, tile * 128 + 128)

        def mixed(cut, halo, own):
            lane = lax.broadcasted_iota(jnp.int32, own.shape, 1)
            return jnp.where(lane >= cut if reverse else lane < cut, halo, own)

        row_turn, cell_turn = (80, 64) if reverse else (0, 0)
        own_row, own_cell = (80, 64) if reverse else (48, 32)
        rows = edges[:, edge * 128 : edge * 128 + 128].astype(F32)
        window = [
            mixed(cuts[0], turned(message[:128], row_turn - 48 * which),
                  turned(rows[which * 128 : which * 128 + 128], own_row))
            for which in range(2)
        ]
        own, far = master[:, lanes].astype(F32), around[:, lanes].astype(F32)
        real = jnp.concatenate([far[:32], own[:64], far[32:64]], axis=0)
        imag = jnp.concatenate([far[64:96], own[64:], far[96:]], axis=0)
        real = mixed(cuts[1], turned(message[:128], cell_turn - 96), turned(real, own_cell))
        tail = [turned(message[128:160], cell_turn - 32 * group) for group in range(4)]
        imag = mixed(cuts[1], jnp.concatenate(tail, axis=0), turned(imag, own_cell))
        sample = mixed(
            cuts[1], turned(message[160:176], 64 if reverse else 32),
            turned(sample_rows[:, lanes], own_cell),
        )
        matrix = band_matrix(sample, 128).astype(BF)
        values = dot(jnp.concatenate(window, axis=0).astype(BF), matrix)
        return sample_columns(values[:128], values[128:], real, imag, forward[...])

    columns = [
        block(from_left, 0, 0, (48, 32), False), block(from_right, 3, 1, (80, 64), True)
    ]
    bands = []
    for band, rows in ((0, slice(64, 128)), (1, slice(0, 128)), (2, slice(0, 64))):
        highs, lows = [], []
        for real, imag in columns:
            picked = slice(band * 32, band * 32 + 64)
            high, low = split(jnp.concatenate([real[picked], imag[picked]], axis=0))
            highs.append(high)
            lows.append(low)
        bands.append(filter_band(highs, lows, lines[...], inverse[rows]))
    for at, target in ((0, 0), (1, 3)):
        tops = bands[1][at][:64] + bands[0][at]
        bottoms = bands[1][at][64:] + bands[2][at]
        values = dot(pair_rows(tops, bottoms), samples[target * 768 : target * 768 + 768])
        lanes = slice(target * 128, target * 128 + 128)
        side = slice(at * 128, at * 128 + 128)
        sides[0, 0, :, side] = part[0, 0, :, lanes] + values[:, :128]
        sides[0, 1, :, side] = part[0, 1, :, lanes] + values[:, 128:]
    copies = [
        pltpu.make_async_copy(
            sides.at[:, :, :, at * 128 : at * 128 + 128],
            out.at[:, :, :, target * 128 : target * 128 + 128],
            sems.at[at + 1],
        )
        for at, target in ((0, 0), (1, 3))
    ]
    for copy in copies:
        copy.start()
    centre.wait()
    for copy in copies:
        copy.wait()


def call(name, body, outputs, scratch=(), hbm=0, cost=0, far_out=False):
    vmem = pl.BlockSpec(memory_space=pltpu.VMEM)
    far = pl.BlockSpec(memory_space=pltpu.HBM)
    return lambda *args: pl.pallas_call(
        body,
        name=name,
        out_shape=[jax.ShapeDtypeStruct(shape, kind) for shape, kind in outputs],
        in_specs=[far] * hbm + [vmem] * (len(args) - hbm),
        out_specs=[far if far_out else vmem] * len(outputs),
        scratch_shapes=list(scratch),
        compiler_params=pltpu.CompilerParams(vmem_limit_bytes=VMEM_LIMIT),
        cost_estimate=pl.CostEstimate(flops=cost, bytes_accessed=cost // 100, transcendentals=0),
    )(*args)


def exchange(first, second, axis):
    size = lax.axis_size(axis)
    dates = lax.axis_size("date")
    pairs = []
    for date in range(dates):
        for i in range(size):
            partner = (date, i + 1 if i % 2 == 1 else i - 1)
            if i in (0, size - 1):
                partner = (date ^ 1, i)
            pairs.append((date * size + i, partner[0] * size + partner[1]))
    received_first = lax.ppermute(first, axis, [(i, i ^ 1) for i in range(size)])
    received_second = lax.ppermute(second, ("date", axis), pairs)
    return received_first, received_second


def date_swap(values, k):
    return lax.ppermute(values, "date", [(i, i ^ k) for i in range(4)])


def on_device(reference_slab, secondary, az_shift, az_fraction, rg_shift, rg_fraction):
    own = reference_slab.reshape(2, LINES_DEV, 128)
    message = ((464, 128), BF)
    lead = call("lead", lead_body, [((16, 128), F32)], cost=2 * 10**9)()[0]
    first, second, line_rows = call(
        "pack", pack_body, [message, message, ((16, 128), F32)],
        cost=10**9,
    )(secondary, own, az_shift, az_fraction, lead)
    tables = [jnp.asarray(table) for table in filter_tables()]
    prepared = call(
        "prepare", prepare_body,
        [((1, 2, LINES_DEV, 512), BF), ((2, LINES_DEV, 128), BF), ((16, 512), F32), ((7, 128, 128), BF)]
        + [(table.shape, BF) for table in tables],
        [pltpu.VMEM((1, 512), jnp.int32), pltpu.VMEM((1, 512), F32), pltpu.SemaphoreType.DMA((8,))],
        hbm=8, cost=2 * 10**9,
    )(secondary, own, rg_shift, rg_fraction, *tables)
    secondary_v, own_v, sample_rows, bands = prepared[:4]
    tables_v = prepared[4:]
    first, second = exchange(first, second, "az")
    peers = [date_swap(own_v, k) for k in (1, 2, 3)]
    halo = jnp.concatenate([first[384:448], second[384:448]], axis=0)
    halo2, halo3 = [date_swap(halo, k) for k in (2, 3)]
    edges, resampled, late = call(
        "lines", lines_body, [((256, 256), BF), ((7, 256, 128), F32), ((128, 128), BF)],
        [pltpu.VMEM((2, 160, 512), BF), pltpu.VMEM((2, 16, 128), F32)],
        cost=10**9,
    )(secondary_v, line_rows, first, second, bands)
    halo1 = date_swap(late, 1)
    columns = ((7, 128, 128), BF)
    master, column_high, column_low, middle = call(
        "early", early_body, [((128, 512), BF), columns, columns, ((7, 128, 128), F32)],
        cost=2 * 10**9,
    )(own_v, *peers, resampled, *tables_v[:3])
    message = ((176, 128), BF)
    around, first, second = call(
        "reference", reference_body, [((128, 512), BF), message, message], cost=10**8
    )(halo, halo1, halo2, halo3, master, edges, sample_rows)
    first, second = exchange(first, second, "rg")
    whole = ((1, 2, LINES_DEV, SAMPLES_DEV), F32)
    part = call("interior", interior_body, [whole], cost=4 * 10**9)(
        resampled, around, column_high, column_low, middle, *tables_v
    )[0]
    return call(
        "edge", edge_body, [whole],
        [pltpu.VMEM((1, 2, LINES_DEV, 256), F32), pltpu.SemaphoreType.DMA((3,))],
        cost=10**9, far_out=True,
    )(part, edges, master, around, sample_rows, first, second, *tables_v)[0]


def solution(mesh):
    in_specs = (
        P(None, "az", "rg", "date"),
        P("date", None, "az", "rg"),
        P("date", "az"),
        P("date", "az"),
        P("date", "rg"),
        P("date", "rg"),
    )
    out_specs = P("date", None, "az", "rg")
    return jax.shard_map(
        on_device, mesh=mesh, in_specs=in_specs, out_specs=out_specs, check_vma=False
    )
```

time: 26.5 us -> 25.3 us (0.955)
  the two profiles are of different devices: /device:TPU:136 before, /device:TPU:144 now
where the time goes in v4:
time: 25.3 us; the launch traced here: 25.2 us
  Pallas kernels  8.82 us (35%)
  starting transfers between devices  8.43 us (33%)
  waiting for transfers between devices  6.89 us (27%)
  local copies, waits for them, and re-layouts  0.93 us (4%)
    pallas_call x8, Pallas kernels, call(): pl.pallas_call(body, name=name, out_shape=[jax.ShapeDtypeStruct(shape, ki...  8.82 us
    ppermute x2, starting transfers between devices, exchange(): lax.ppermute(first, axis, [(i, i ^ 1) for i in range(size)])  4.48 us
    ppermute x2, waiting for transfers between devices, exchange(): received_second = lax.ppermute(second, ('date', axis), pairs)  4.05 us
    ppermute x6, starting transfers between devices, date_swap(): return lax.ppermute(values, 'date', [(i, i ^ k) for i in range(4)])  3.89 us
    ppermute x2, waiting for transfers between devices, exchange(): lax.ppermute(first, axis, [(i, i ^ 1) for i in range(size)])  2.74 us
    unnamed x20, local copies, waits for them, and re-layouts  0.93 us
  transfers between devices with their start and end apart: 10, of which 5 were waited for; matrix products, arithmetic and copies ran while one was open for 0% of the time, Pallas kernels for 22%

profile of v4, /device:TPU:144, one launch (start us, length us, event | category | flops | bytes accessed | tf_op | source)
XLA Modules:
  0.0 25.2 jit_solution(14720689825282045138)
XLA Ops:
  0.0 0.0 copy-start
  0.0 0.0 copy-start.5
  0.0 0.0 copy-start.4
  0.0 0.0 copy-start.1
  0.0 0.9 %copy-done = bf16[1,2,64,512]{3,2,1,0:T(8,128)(2,1)S(1)} copy-done((bf16[1,2,64,512]{3,2,1,0:T(8,128)(2,1)S(1)}, bf16[1,2,64,512]{3,2,1,0:T(8,128)(2,1)}, u32[]{:S(2)}) %copy-start) | copy-done | bytes 131096
  0.9 0.0 copy-done.5
  0.9 0.0 copy-done.4
  0.9 0.0 copy-done.1
  0.9 0.0 copy-start.2
  0.9 0.0 copy-start.3
  0.9 0.0 copy-start.6
  0.9 0.0 copy-start.7
  1.0 0.0 copy-start.8
  1.0 0.0 copy-start.9
  1.0 0.2 pack.1
  1.2 3.1 %collective-permute-start = (bf16[464,128]{1,0:T(8,128)(2,1)S(1)}, bf16[464,128]{1,0:T(8,128)(2,1)S(1)}, u32[]{:S(2)}, u32[]{:S(2)}) collective-permute-start(bf16[464,128]{1,0:T(8,128)(2,1)S(1)} %get-tuple-element.28), channel_id=1, source_target_pairs={{0,4},{4,0},{8,12},{12,8},{16,20},{20,16},{24,28},{28,24},{32,36},... | collective-permute-start | bytes 356360 | tf_op jit(solution)/shard_map/ppermute | solution.py:591
  4.3 0.1 collective-permute-start.1
  4.4 0.0 copy-done.2
  4.4 0.0 copy-done.3
  4.4 0.0 copy-done.6
  4.4 0.0 copy-done.7
  4.4 0.0 copy-done.8
  4.4 0.0 copy-done.9
  4.4 1.3 %prepare.1 = (bf16[1,2,64,512]{3,2,1,0:T(8,128)(2,1)S(1)}, bf16[2,64,128]{2,1,0:T(8,128)(2,1)S(1)}, f32[16,512]{1,0:T(8,128)S(1)}, bf16[7,128,128]{2,1,0:T(8,128...) custom-call(bf16[1,2,64,512]{3,2,1,0:T(8,128)(2,1)S(1)} %copy-done, ...), custom_call_target="tpu_custom_call" | custom-call | flops 2000000000 | bytes 20000000 | tf_op jit(solution)/shard_map/prepare/pallas_call | solution.py:569
  5.7 0.5 %collective-permute-start.7 = (bf16[2,64,128]{2,1,0:T(8,128)(2,1)S(1)}, bf16[2,64,128]{2,1,0:T(8,128)(2,1)S(1)}, u32[]{:S(2)}, u32[]{:S(2)}) collective-permute-start(bf16[2,64,128]{2,1,0:T(8,128)(2,1)S(1)} %get-tuple-element.33.own), channel_id=1, source_target_pairs={{0,192},{64,128},{128,64},{192,0},{1,193},{65,129},{129,65},{193,1... | collective-permute-start | bytes 98312 | tf_op jit(solution)/shard_map/ppermute | solution.py:597
  6.2 1.2 %collective-permute-start.6 = (bf16[2,64,128]{2,1,0:T(8,128)(2,1)S(1)}, bf16[2,64,128]{2,1,0:T(8,128)(2,1)S(1)}, u32[]{:S(2)}, u32[]{:S(2)}) collective-permute-start(bf16[2,64,128]{2,1,0:T(8,128)(2,1)S(1)} %get-tuple-element.33.own), channel_id=1, source_target_pairs={{0,128},{64,192},{128,0},{192,64},{1,129},{65,193},{129,1},{193,65... | collective-permute-start | bytes 98312 | tf_op jit(solution)/shard_map/ppermute | solution.py:597
  7.4 0.3 %collective-permute-start.5 = (bf16[2,64,128]{2,1,0:T(8,128)(2,1)S(1)}, bf16[2,64,128]{2,1,0:T(8,128)(2,1)S(1)}, u32[]{:S(2)}, u32[]{:S(2)}) collective-permute-start(bf16[2,64,128]{2,1,0:T(8,128)(2,1)S(1)} %get-tuple-element.33.own), channel_id=1, source_target_pairs={{0,64},{64,0},{128,192},{192,128},{1,65},{65,1},{129,193},{193,129... | collective-permute-start | bytes 98312 | tf_op jit(solution)/shard_map/ppermute | solution.py:597
  7.7 2.4 %collective-permute-done.first = bf16[464,128]{1,0:T(8,128)(2,1)S(1)} collective-permute-done((bf16[464,128]{1,0:T(8,128)(2,1)S(1)}, bf16[464,128]{1,0:T(8,128)(2,1)S(1)}, u32[]{:S(2)}, u32[]{:S(2)}) %collective-permute-start) | collective-permute-done | bytes 118816 | tf_op jit(solution)/shard_map/ppermute | solution.py:591
  10.1 2.8 %collective-permute-done.1.second = bf16[464,128]{1,0:T(8,128)(2,1)S(1)} collective-permute-done((bf16[464,128]{1,0:T(8,128)(2,1)S(1)}, bf16[464,128]{1,0:T(8,128)(2,1)S(1)}, u32[]{:S(2)}, u32[]{:S(2)}) %collective-permute-start.1) | collective-permute-done | bytes 118816 | tf_op jit(solution)/shard_map/ppermute | solution.py:592
  12.9 0.0 collective-permute-start.4
  12.9 0.7 %collective-permute-start.3 = (bf16[128,128]{1,0:T(8,128)(2,1)S(1)}, bf16[128,128]{1,0:T(8,128)(2,1)S(1)}, u32[]{:S(2)}, u32[]{:S(2)}) collective-permute-start(bf16[128,128]{1,0:T(8,128)(2,1)S(1)} %pad_maximum_fusion.halo), channel_id=1, source_target_pairs={{0,128},{64,192},{128,0},{192,64},{1,129},{65,193},{129,1},{193,65... | collective-permute-start | bytes 98312 | tf_op jit(solution)/shard_map/ppermute | solution.py:597
  13.5 0.7 %lines.1 = (bf16[256,256]{1,0:T(8,128)(2,1)S(1)}, f32[7,256,128]{2,1,0:T(8,128)S(1)}, bf16[128,128]{1,0:T(8,128)(2,1)S(1)}) custom-call(bf16[1,2,64,512]{3,2,1,0:T(8,128)(2,1)S(1)} %get-tuple-element.26.secondary, f32[16,128]{1,0:T(8,128)S(1)} %get-tuple-element.27.line_rows, bf16[464,128]{1,0:T(8,128)(2,1)S(1)} %collective-permute-done.first, ...), custom_call_target="tpu_custom_call" | custom-call | flops 1000000000 | bytes 10000000 | tf_op jit(solution)/shard_map/lines/pallas_call | solution.py:569
  14.3 0.0 collective-permute-done.7.peer3
  14.3 1.3 %collective-permute-start.2 = (bf16[128,128]{1,0:T(8,128)(2,1)S(1)}, bf16[128,128]{1,0:T(8,128)(2,1)S(1)}, u32[]{:S(2)}, u32[]{:S(2)}) collective-permute-start(bf16[128,128]{1,0:T(8,128)(2,1)S(1)} %get-tuple-element.32), channel_id=1, source_target_pairs={{0,64},{64,0},{128,192},{192,128},{1,65},{65,1},{129,193},{193,129... | collective-permute-start | bytes 98312 | tf_op jit(solution)/shard_map/ppermute | solution.py:597
  15.5 0.0 collective-permute-done.6.peer2
  15.5 0.0 collective-permute-done.5.peer1
  15.5 1.2 %early.1 = (bf16[128,512]{1,0:T(8,128)(2,1)S(1)}, bf16[7,128,128]{2,1,0:T(8,128)(2,1)S(1)}, bf16[7,128,128]{2,1,0:T(8,128)(2,1)S(1)}, f32[7,128,128]{2,1,0:T(8,128)S(1)}) custom-call(bf16[2,64,128]{2,1,0:T(8,128)(2,1)S(1)} %get-tuple-element.33.own, bf16[2,64,128]{2,1,0:T(8,128)(2,1)S(1)} %collective-permute-done.5.peer1, ...), custom_call_target="tpu_custom_call" | custom-call | flops 2000000000 | bytes 20000000 | tf_op jit(solution)/shard_map/early/pallas_call | solution.py:569
  16.8 0.0 collective-permute-done.4.halo3
  16.8 0.1 collective-permute-done.3.halo2
  16.9 0.0 collective-permute-done.2.halo1
  16.9 0.2 reference.1
  17.1 1.4 %collective-permute-start.8 = (bf16[176,128]{1,0:T(8,128)(2,1)S(1)}, bf16[176,128]{1,0:T(8,128)(2,1)S(1)}, u32[]{:S(2)}, u32[]{:S(2)}) collective-permute-start(bf16[176,128]{1,0:T(8,128)(2,1)S(1)} %get-tuple-element.45), channel_id=1, source_target_pairs={{0,1},{1,0},{2,3},{3,2},{4,5},{5,4},{6,7},{7,6},{8,9},{9,8},{10,11... | collective-permute-start | bytes 135176 | tf_op jit(solution)/shard_map/ppermute | solution.py:591
  18.5 0.0 collective-permute-start.9
  18.5 2.4 %interior.1.part = f32[1,2,64,512]{3,2,1,0:T(8,128)S(1)} custom-call(f32[7,256,128]{2,1,0:T(8,128)S(1)} %get-tuple-element.31.resampled, bf16[128,512]{1,0:T(8,128)(2,1)S(1)} %get-tuple-element.40.master.around, bf16[7,128,128]{2,1,0:T(8,128)(2,1)S(1)} %get-tuple-element.41.column_high, bf16[7,128,128]{2,1,0:T(8,128)(2,1)S(1)} %get-tuple-element.42.column_low, ...), custom_call_target="tpu_custom_call" | custom-call | flops 4000000000 | bytes 40000000 | tf_op jit(solution)/shard_map/interior/pallas_call | solution.py:569
  20.9 0.3 %collective-permute-done.8.first = bf16[176,128]{1,0:T(8,128)(2,1)S(1)} collective-permute-done((bf16[176,128]{1,0:T(8,128)(2,1)S(1)}, bf16[176,128]{1,0:T(8,128)(2,1)S(1)}, u32[]{:S(2)}, u32[]{:S(2)}) %collective-permute-start.8) | collective-permute-done | bytes 45088 | tf_op jit(solution)/shard_map/ppermute | solution.py:591
  21.2 1.3 %collective-permute-done.9.second = bf16[176,128]{1,0:T(8,128)(2,1)S(1)} collective-permute-done((bf16[176,128]{1,0:T(8,128)(2,1)S(1)}, bf16[176,128]{1,0:T(8,128)(2,1)S(1)}, u32[]{:S(2)}, u32[]{:S(2)}) %collective-permute-start.9) | collective-permute-done | bytes 45088 | tf_op jit(solution)/shard_map/ppermute | solution.py:592
  22.5 2.7 %edge.1 = f32[1,2,64,512]{3,2,1,0:T(8,128)} custom-call(f32[1,2,64,512]{3,2,1,0:T(8,128)S(1)} %interior.1.part, bf16[256,256]{1,0:T(8,128)(2,1)S(1)} %get-tuple-element.38.edges, bf16[128,512]{1,0:T(8,128)(2,1)S(1)} %get-tuple-element.37.master, bf16[128,512]{1,0:T(8,128)(2,1)S(1)} %get-tuple-element.40.master.around, ...), custom_call_target="tpu_custom_call" | custom-call | flops 1000000000 | bytes 10000000 | tf_op jit(solution)/shard_map/edge/pallas_call | solution.py:569
  (4 shorter events, 0.0 us)
Async XLA Ops:
  0.0 0.9 %copy-start = (bf16[1,2,64,512]{3,2,1,0:T(8,128)(2,1)S(1)}, bf16[1,2,64,512]{3,2,1,0:T(8,128)(2,1)}, u32[]{:S(2)}) copy-start(bf16[1,2,64,512]{3,2,1,0:T(8,128)(2,1)} %secondary.3) | copy-start | bytes 393220
  0.0 0.9 %copy-start.5 = (f32[1,64]{1,0:T(1,128)S(1)}, f32[1,64]{1,0:T(1,128)}, u32[]{:S(2)}) copy-start(f32[1,64]{1,0:T(1,128)} %fraction.3) | copy-start | bytes 772
  0.0 0.9 %copy-start.4 = (s32[1,64]{1,0:T(1,128)S(1)}, s32[1,64]{1,0:T(1,128)}, u32[]{:S(2)}) copy-start(s32[1,64]{1,0:T(1,128)} %shift.3) | copy-start | bytes 772
  0.0 0.9 %copy-start.1 = (bf16[2,64,1,128]{3,1,2,0:T(8,128)(2,1)S(1)}, bf16[2,64,1,128]{3,1,2,0:T(8,128)(2,1)}, u32[]{:S(2)}) copy-start(bf16[2,64,1,128]{3,1,2,0:T(8,128)(2,1)} %param.10) | copy-start | bytes 98308
  0.9 3.5 %copy-start.2 = (s32[1,512]{1,0:T(1,128)S(1)}, s32[1,512]{1,0:T(1,128)}, u32[]{:S(2)}) copy-start(s32[1,512]{1,0:T(1,128)} %shift.2) | copy-start | bytes 6148
  0.9 3.5 %copy-start.3 = (f32[1,512]{1,0:T(1,128)S(1)}, f32[1,512]{1,0:T(1,128)}, u32[]{:S(2)}) copy-start(f32[1,512]{1,0:T(1,128)} %fraction.2) | copy-start | bytes 6148
  0.9 3.5 %copy-start.6 = (bf16[3072,256]{1,0:T(8,128)(2,1)S(1)}, bf16[3072,256]{1,0:T(8,128)(2,1)}, u32[]{:S(2)}) copy-start(bf16[3072,256]{1,0:T(8,128)(2,1)} %constant.11.clone.refs_3_) | copy-start | bytes 4718596
  0.9 3.5 %copy-start.7 = (bf16[768,256]{1,0:T(8,128)(2,1)S(1)}, bf16[768,256]{1,0:T(8,128)(2,1)}, u32[]{:S(2)}) copy-start(bf16[768,256]{1,0:T(8,128)(2,1)} %constant.8.clone.refs_0_) | copy-start | bytes 1179652
  1.0 3.4 %copy-start.8 = (bf16[128,384]{1,0:T(8,128)(2,1)S(1)}, bf16[128,384]{1,0:T(8,128)(2,1)}, u32[]{:S(2)}) copy-start(bf16[128,384]{1,0:T(8,128)(2,1)} %constant.10.clone.refs_2_) | copy-start | bytes 294916
  1.0 3.4 %copy-start.9 = (bf16[128,384]{1,0:T(8,128)(2,1)S(1)}, bf16[128,384]{1,0:T(8,128)(2,1)}, u32[]{:S(2)}) copy-start(bf16[128,384]{1,0:T(8,128)(2,1)} %constant.9.clone.refs_1_) | copy-start | bytes 294916
  1.2 8.8 %collective-permute-start = (bf16[464,128]{1,0:T(8,128)(2,1)S(1)}, bf16[464,128]{1,0:T(8,128)(2,1)S(1)}, u32[]{:S(2)}, u32[]{:S(2)}) collective-permute-start(bf16[464,128]{1,0:T(8,128)(2,1)S(1)} %get-tuple-element.28), channel_id=1, source_target_pairs={{0,4},{4,0},{8,12},{12,8},{16,20},{20,16},{24,28},{28,24},{32,36},... | collective-permute-start | bytes 356360 | tf_op jit(solution)/shard_map/ppermute | solution.py:591
  4.3 8.5 %collective-permute-start.1 = (bf16[464,128]{1,0:T(8,128)(2,1)S(1)}, bf16[464,128]{1,0:T(8,128)(2,1)S(1)}, u32[]{:S(2)}, u32[]{:S(2)}) collective-permute-start(bf16[464,128]{1,0:T(8,128)(2,1)S(1)} %get-tuple-element.29), channel_id=1, source_target_pairs={{0,64},{4,8},{8,4},{12,16},{16,12},{20,24},{24,20},{28,32},{32,28}... | collective-permute-start | bytes 356360 | tf_op jit(solution)/shard_map/ppermute | solution.py:592
  5.7 8.5 %collective-permute-start.7 = (bf16[2,64,128]{2,1,0:T(8,128)(2,1)S(1)}, bf16[2,64,128]{2,1,0:T(8,128)(2,1)S(1)}, u32[]{:S(2)}, u32[]{:S(2)}) collective-permute-start(bf16[2,64,128]{2,1,0:T(8,128)(2,1)S(1)} %get-tuple-element.33.own), channel_id=1, source_target_pairs={{0,192},{64,128},{128,64},{192,0},{1,193},{65,129},{129,65},{193,1... | collective-permute-start | bytes 98312 | tf_op jit(solution)/shard_map/ppermute | solution.py:597
  6.2 9.4 %collective-permute-start.6 = (bf16[2,64,128]{2,1,0:T(8,128)(2,1)S(1)}, bf16[2,64,128]{2,1,0:T(8,128)(2,1)S(1)}, u32[]{:S(2)}, u32[]{:S(2)}) collective-permute-start(bf16[2,64,128]{2,1,0:T(8,128)(2,1)S(1)} %get-tuple-element.33.own), channel_id=1, source_target_pairs={{0,128},{64,192},{128,0},{192,64},{1,129},{65,193},{129,1},{193,65... | collective-permute-start | bytes 98312 | tf_op jit(solution)/shard_map/ppermute | solution.py:597
  7.4 8.1 %collective-permute-start.5 = (bf16[2,64,128]{2,1,0:T(8,128)(2,1)S(1)}, bf16[2,64,128]{2,1,0:T(8,128)(2,1)S(1)}, u32[]{:S(2)}, u32[]{:S(2)}) collective-permute-start(bf16[2,64,128]{2,1,0:T(8,128)(2,1)S(1)} %get-tuple-element.33.own), channel_id=1, source_target_pairs={{0,64},{64,0},{128,192},{192,128},{1,65},{65,1},{129,193},{193,129... | collective-permute-start | bytes 98312 | tf_op jit(solution)/shard_map/ppermute | solution.py:597
  12.9 3.9 %collective-permute-start.4 = (bf16[128,128]{1,0:T(8,128)(2,1)S(1)}, bf16[128,128]{1,0:T(8,128)(2,1)S(1)}, u32[]{:S(2)}, u32[]{:S(2)}) collective-permute-start(bf16[128,128]{1,0:T(8,128)(2,1)S(1)} %pad_maximum_fusion.halo), channel_id=1, source_target_pairs={{0,192},{64,128},{128,64},{192,0},{1,193},{65,129},{129,65},{193,1... | collective-permute-start | bytes 98312 | tf_op jit(solution)/shard_map/ppermute | solution.py:597
  12.9 4.0 %collective-permute-start.3 = (bf16[128,128]{1,0:T(8,128)(2,1)S(1)}, bf16[128,128]{1,0:T(8,128)(2,1)S(1)}, u32[]{:S(2)}, u32[]{:S(2)}) collective-permute-start(bf16[128,128]{1,0:T(8,128)(2,1)S(1)} %pad_maximum_fusion.halo), channel_id=1, source_target_pairs={{0,128},{64,192},{128,0},{192,64},{1,129},{65,193},{129,1},{193,65... | collective-permute-start | bytes 98312 | tf_op jit(solution)/shard_map/ppermute | solution.py:597
  14.3 2.6 %collective-permute-start.2 = (bf16[128,128]{1,0:T(8,128)(2,1)S(1)}, bf16[128,128]{1,0:T(8,128)(2,1)S(1)}, u32[]{:S(2)}, u32[]{:S(2)}) collective-permute-start(bf16[128,128]{1,0:T(8,128)(2,1)S(1)} %get-tuple-element.32), channel_id=1, source_target_pairs={{0,64},{64,0},{128,192},{192,128},{1,65},{65,1},{129,193},{193,129... | collective-permute-start | bytes 98312 | tf_op jit(solution)/shard_map/ppermute | solution.py:597
  17.1 4.1 %collective-permute-start.8 = (bf16[176,128]{1,0:T(8,128)(2,1)S(1)}, bf16[176,128]{1,0:T(8,128)(2,1)S(1)}, u32[]{:S(2)}, u32[]{:S(2)}) collective-permute-start(bf16[176,128]{1,0:T(8,128)(2,1)S(1)} %get-tuple-element.45), channel_id=1, source_target_pairs={{0,1},{1,0},{2,3},{3,2},{4,5},{5,4},{6,7},{7,6},{8,9},{9,8},{10,11... | collective-permute-start | bytes 135176 | tf_op jit(solution)/shard_map/ppermute | solution.py:591
  18.5 4.0 %collective-permute-start.9 = (bf16[176,128]{1,0:T(8,128)(2,1)S(1)}, bf16[176,128]{1,0:T(8,128)(2,1)S(1)}, u32[]{:S(2)}, u32[]{:S(2)}) collective-permute-start(bf16[176,128]{1,0:T(8,128)(2,1)S(1)} %get-tuple-element.46), channel_id=1, source_target_pairs={{0,64},{1,2},{2,1},{3,67},{64,0},{65,66},{66,65},{67,3},{128,192},... | collective-permute-start | bytes 135176 | tf_op jit(solution)/shard_map/ppermute | solution.py:592

commit v5 on v4

--- a/solution.py
+++ b/solution.py
@@ -54,6 +54,14 @@
         table[1, :, 0, m] = -np.sin(angle)
         table[1, :, 1, m] = np.cos(angle)
     return table.reshape(128, 128)
+
+
+def line_bands():
+    small = line_forward().reshape(2, 64, 2, 64)
+    table = np.zeros((3, 2, 64, 2, 128))
+    for band in range(3):
+        table[band, :, :, :, 32 * band : 32 * band + 64] = small
+    return table.reshape(384, 256)
 
 
 def line_inverse():
@@ -91,10 +99,11 @@
 
 
 def filter_tables():
-    inverse = [sample_inverse(start) for start in (0, 64, 128, 96)]
+    inverse = [sample_inverse(start) for start in (0, 64, 128)]
+    inverse.append(inverse[0] + sample_inverse(96))
     return [
         triple(sample_forward(), 0),
-        triple(line_forward(), 1),
+        triple(line_bands(), 1),
         triple(line_inverse(), 1),
         np.concatenate([triple(table, 0) for table in inverse], axis=0),
     ]
@@ -194,13 +203,27 @@
     second[448:464] = rows.astype(BF)
 
 
-def prepare_body(secondary, own, shift, fraction, *refs):
-    tables, outs = refs[0:4], refs[4:13]
-    secondary_v, own_v, sample_rows, bands = outs[0:4]
-    tables_v = outs[4:8]
-    shift_v, fraction_v, sems = outs[8], refs[13], refs[14]
-    pairs = [(shift, shift_v), (fraction, fraction_v), (own, own_v), (secondary, secondary_v)]
-    pairs.extend(zip(tables, tables_v))
+def cross_pack_body(first, second, own, cross_first, cross_second, own_v):
+    own_v[...] = own[...]
+    cross_first[...] = first[384:448]
+    cross_second[...] = second[384:448]
+
+
+def core_pack_body(own, piece, first, second, cross_first, cross_second, after, message):
+    del after
+    for part in range(2):
+        message[part * 64 : part * 64 + 64] = own[part]
+        message[256 + part * 64 : 320 + part * 64] = piece[part]
+    message[128:192] = first[384:448]
+    message[192:256] = second[384:448]
+    message[384:448] = cross_first[...]
+    message[448:512] = cross_second[...]
+
+
+def prepare_body(secondary, shift, fraction, after, secondary_v, sample_rows, bands,
+                 shift_v, fraction_v, sems):
+    del after
+    pairs = [(shift, shift_v), (fraction, fraction_v), (secondary, secondary_v)]
     copies = [
         pltpu.make_async_copy(source, target, sems.at[at]) for at, (source, target) in enumerate(pairs)
     ]
@@ -217,7 +240,7 @@
         copy.wait()
 
 
-def lines_body(secondary, line_rows, first, second, bands, edges, resampled, late, extended, halo_rows):
+def lines_body(secondary, line_rows, first, second, bands, edges, resampled, extended, halo_rows):
     odd = lax.axis_index("az") % 2 == 1
     has_top = lax.axis_index("az") > 0
     has_bottom = lax.axis_index("az") < lax.axis_size("az") - 1
@@ -240,8 +263,6 @@
     def _():
         place(second, first)
 
-    late[0:64] = first[384:448]
-    late[64:128] = second[384:448]
     for part in range(2):
         extended[part, 48:112] = secondary[0, part]
 
@@ -285,12 +306,18 @@
     return values * lax.rsqrt(jnp.maximum(values, np.float32(1e-36)))
 
 
-def sample_columns(real, imag, master_real, master_imag, forward):
-    product = jnp.concatenate(
+def cross_product(real, imag, master_real, master_imag):
+    return jnp.concatenate(
         [master_real * real + master_imag * imag, master_imag * real - master_real * imag], axis=1
     )
-    columns = dot(columns_triple(product), forward)
-    return columns[:, :128], columns[:, 128:]
+
+
+def sample_columns(products, forward):
+    result = []
+    for product in products:
+        columns = dot(columns_triple(product), forward)
+        result.append((split(columns[:, :128]), split(columns[:, 128:])))
+    return result
 
 
 def response_of(spectrum):
@@ -317,10 +344,7 @@
     return scales
 
 
-def filter_band(highs, lows, lines, inverse):
-    stacked = [jnp.concatenate([high, low, high], axis=0) for high, low in zip(highs, lows)]
-    spectrum = dot(lines, jnp.concatenate(stacked, axis=1))
-    spectra = [spectrum[:, at * 128 : at * 128 + 128] for at in range(len(highs))]
+def filter_band(spectra, inverse):
     responses = [response_of(values) for values in spectra]
     gained = [
         rows_triple(values * jnp.concatenate([response, response], axis=0))
@@ -329,7 +353,7 @@
     back = dot(inverse, jnp.concatenate(gained, axis=1))
     scales = window_scales(responses)
     return [
-        back[:, at * 128 : at * 128 + 128] * scales[at] for at in range(len(highs))
+        back[:, at * 128 : at * 128 + 128] * scales[at] for at in range(len(spectra))
     ]
 
 
@@ -339,59 +363,51 @@
     return columns_triple(jnp.concatenate([real, imag], axis=1))
 
 
-def early_body(own, peer1, peer2, peer3, resampled, forward, lines, inverse,
-               master, column_high, column_low, back):
-    def store(piece, lanes):
-        master[0:64, lanes] = piece[0]
-        master[64:128, lanes] = piece[1]
-
-    by_date((own, peer1, peer2, peer3), store)
-    tiles = tiles_of(master)
-    highs, lows = [], []
-    for j in range(1, 8):
-        around = shifted(tiles, 64 * j - 32)
-        real, imag = sample_columns(
-            resampled[j - 1, 32:96], resampled[j - 1, 160:224], around[:64], around[64:], forward[...]
-        )
-        high, low = split(jnp.concatenate([real, imag], axis=0))
-        column_high[j - 1] = high
-        column_low[j - 1] = low
-        highs.append(high)
-        lows.append(low)
-    middle = filter_band(highs, lows, lines[...], inverse[...])
-    for j in range(1, 8):
-        back[j - 1] = middle[j - 1]
-
-
-def reference_body(halo, halo1, halo2, halo3, master, edges, sample_rows,
-                   around, send_first, send_second):
+def reference_body(own, peer2, core, first, second, cross_first, cross_second, edges,
+                   sample_rows, master, send_first, send_second):
     az = lax.axis_index("az")
     odd = az % 2 == 1
+    pieces = (
+        (own.at[0], own.at[1]), (core.at[0:64], core.at[64:128]),
+        (peer2.at[0], peer2.at[1]), (core.at[256:320], core.at[320:384]),
+    )
+    halos = (
+        (first.at[384:448], second.at[384:448]),
+        (core.at[128:192], core.at[192:256]),
+        (cross_first, cross_second),
+        (core.at[384:448], core.at[448:512]),
+    )
 
     def store(piece, lanes):
+        middle, halo = piece
+        for part in range(2):
+            master[part * 128 + 32 : part * 128 + 96, lanes] = middle[part][...]
+
+        def place(top, bottom):
+            for part in range(2):
+                rows = slice(part * 32, part * 32 + 32)
+                master[part * 128 : part * 128 + 32, lanes] = top[rows]
+                master[part * 128 + 96 : part * 128 + 128, lanes] = bottom[rows]
+
         @pl.when(odd)
         def _():
-            for part in range(2):
-                around[part * 64 : part * 64 + 32, lanes] = piece[part * 32 : part * 32 + 32]
-                around[part * 64 + 32 : part * 64 + 64, lanes] = piece[64 + part * 32 : 96 + part * 32]
+            place(*halo)
 
         @pl.when(jnp.logical_not(odd))
         def _():
-            for part in range(2):
-                around[part * 64 : part * 64 + 32, lanes] = piece[64 + part * 32 : 96 + part * 32]
-                around[part * 64 + 32 : part * 64 + 64, lanes] = piece[part * 32 : part * 32 + 32]
-
-    by_date((halo, halo1, halo2, halo3), store)
+            place(*halo[::-1])
+
+    by_date(list(zip(pieces, halos)), store)
 
     @pl.when(az == 0)
     def _():
         for part in range(2):
-            around[part * 64 : part * 64 + 32] = jnp.zeros((32, 512), BF)
+            master[part * 128 : part * 128 + 32] = jnp.zeros((32, 512), BF)
 
     @pl.when(az == lax.axis_size("az") - 1)
     def _():
         for part in range(2):
-            around[part * 64 + 32 : part * 64 + 64] = jnp.zeros((32, 512), BF)
+            master[part * 128 + 96 : part * 128 + 128] = jnp.zeros((32, 512), BF)
 
     lane = lax.broadcasted_iota(jnp.int32, (128, 128), 1)
     narrow = lax.broadcasted_iota(jnp.int32, (32, 128), 1)
@@ -399,9 +415,8 @@
     def message(tile, edge, turn):
         lanes = slice(tile * 128, tile * 128 + 128)
         rows = edges[:, edge * 128 : edge * 128 + 128].astype(F32)
-        own, far = master[:, lanes].astype(F32), around[:, lanes].astype(F32)
-        real = jnp.concatenate([far[:32], own[:64], far[32:64]], axis=0)
-        imag = jnp.concatenate([far[64:96], own[64:], far[96:]], axis=0)
+        cells = master[:, lanes].astype(F32)
+        real, imag = cells[:128], cells[128:]
         wide = jnp.where(
             lane < 48,
             pltpu.roll(rows[:128], turn[0], 1) if turn[0] else rows[:128],
@@ -438,33 +453,35 @@
         send(send_second, to_left)
 
 
-def interior_body(resampled, master, column_high, column_low, middle, forward, lines, inverse,
-                  samples, out):
+def filter_columns(columns, lines, inverse):
+    stacked = [
+        jnp.concatenate([real[0], imag[0], real[1], imag[1], real[0], imag[0]], axis=0)
+        for real, imag in columns
+    ]
+    spectrum = dot(lines[...], jnp.concatenate(stacked, axis=1))
+    bands = []
+    for band, rows in ((0, slice(64, 128)), (1, slice(0, 128)), (2, slice(0, 64))):
+        spectra = [
+            spectrum[band * 128 : band * 128 + 128, at * 128 : at * 128 + 128]
+            for at in range(len(columns))
+        ]
+        bands.append(filter_band(spectra, inverse[rows]))
+    return [
+        (middle[:64] + upper, middle[64:] + lower)
+        for upper, middle, lower in zip(*bands)
+    ]
+
+
+def interior_body(resampled, master, forward, lines, inverse, samples, out):
     tiles = tiles_of(master)
-    upper_high, upper_low, lower_high, lower_low = [], [], [], []
+    products = []
     for j in range(1, 8):
         around = shifted(tiles, 64 * j - 32)
         values = resampled.at[j - 1]
-        real, imag = sample_columns(
-            jnp.concatenate([values[0:32], values[96:128]], axis=0),
-            jnp.concatenate([values[128:160], values[224:256]], axis=0),
-            around[:64], around[64:], forward[...],
-        )
-        real, imag = split(real), split(imag)
-        for which, own, upper, lower in (
-            (0, column_high, upper_high, lower_high), (1, column_low, upper_low, lower_low)
-        ):
-            held = own.at[j - 1]
-            upper.append(jnp.concatenate(
-                [real[which][:32], held[0:32], imag[which][:32], held[64:96]], axis=0))
-            lower.append(jnp.concatenate(
-                [held[32:64], real[which][32:], held[96:128], imag[which][32:]], axis=0))
-    upper = filter_band(upper_high, upper_low, lines[...], inverse[64:128])
-    lower = filter_band(lower_high, lower_low, lines[...], inverse[0:64])
+        products.append(cross_product(values[:128], values[128:], around[:128], around[128:]))
+    columns = sample_columns(products, forward[...])
     parts = []
-    for j in range(1, 8):
-        tops = middle[j - 1, 0:64] + upper[j - 1]
-        bottoms = middle[j - 1, 64:128] + lower[j - 1]
+    for j, (tops, bottoms) in enumerate(filter_columns(columns, lines, inverse), 1):
         if j == 7:
             lane = lax.broadcasted_iota(jnp.int32, tops.shape, 1)
             tops = jnp.where(lane % 2 == 0, tops, 0.0)
@@ -481,7 +498,7 @@
         out[0, 1, :, block * 128 : block * 128 + 128] = values[:, 128:]
 
 
-def edge_body(part, edges, master, around, sample_rows, first, second, forward, lines, inverse,
+def edge_body(part, edges, master, sample_rows, first, second, forward, lines, inverse,
               samples, out, sides, sems):
     centre = pltpu.make_async_copy(
         part.at[:, :, :, 128:384], out.at[:, :, :, 128:384], sems.at[0]
@@ -514,9 +531,8 @@
                   turned(rows[which * 128 : which * 128 + 128], own_row))
             for which in range(2)
         ]
-        own, far = master[:, lanes].astype(F32), around[:, lanes].astype(F32)
-        real = jnp.concatenate([far[:32], own[:64], far[32:64]], axis=0)
-        imag = jnp.concatenate([far[64:96], own[64:], far[96:]], axis=0)
+        cells = master[:, lanes].astype(F32)
+        real, imag = cells[:128], cells[128:]
         real = mixed(cuts[1], turned(message[:128], cell_turn - 96), turned(real, own_cell))
         tail = [turned(message[128:160], cell_turn - 32 * group) for group in range(4)]
         imag = mixed(cuts[1], jnp.concatenate(tail, axis=0), turned(imag, own_cell))
@@ -526,28 +542,22 @@
         )
         matrix = band_matrix(sample, 128).astype(BF)
         values = dot(jnp.concatenate(window, axis=0).astype(BF), matrix)
-        return sample_columns(values[:128], values[128:], real, imag, forward[...])
-
-    columns = [
+        return cross_product(values[:128], values[128:], real, imag)
+
+    products = [
         block(from_left, 0, 0, (48, 32), False), block(from_right, 3, 1, (80, 64), True)
     ]
-    bands = []
-    for band, rows in ((0, slice(64, 128)), (1, slice(0, 128)), (2, slice(0, 64))):
-        highs, lows = [], []
-        for real, imag in columns:
-            picked = slice(band * 32, band * 32 + 64)
-            high, low = split(jnp.concatenate([real[picked], imag[picked]], axis=0))
-            highs.append(high)
-            lows.append(low)
-        bands.append(filter_band(highs, lows, lines[...], inverse[rows]))
+    results = filter_columns(sample_columns(products, forward[...]), lines, inverse)
+    rows = jnp.concatenate([pair_rows(tops, bottoms) for tops, bottoms in results], axis=0)
+    values = dot(rows, samples[2304:3072])
+    lane = lax.broadcasted_iota(jnp.int32, (64, 128), 1)
     for at, target in ((0, 0), (1, 3)):
-        tops = bands[1][at][:64] + bands[0][at]
-        bottoms = bands[1][at][64:] + bands[2][at]
-        values = dot(pair_rows(tops, bottoms), samples[target * 768 : target * 768 + 768])
         lanes = slice(target * 128, target * 128 + 128)
         side = slice(at * 128, at * 128 + 128)
-        sides[0, 0, :, side] = part[0, 0, :, lanes] + values[:, :128]
-        sides[0, 1, :, side] = part[0, 1, :, lanes] + values[:, 128:]
+        kept = (lane < 64) if at == 0 else (lane >= 64)
+        for which in range(2):
+            found = values[at * 64 : at * 64 + 64, which * 128 : which * 128 + 128]
+            sides[0, which, :, side] = part[0, which, :, lanes] + jnp.where(kept, found, 0.0)
     copies = [
         pltpu.make_async_copy(
             sides.at[:, :, :, at * 128 : at * 128 + 128],
@@ -578,17 +588,20 @@
     )(*args)
 
 
-def exchange(first, second, axis):
+def exchange(first, second, axis, turn=0):
     size = lax.axis_size(axis)
     dates = lax.axis_size("date")
     pairs = []
     for date in range(dates):
         for i in range(size):
-            partner = (date, i + 1 if i % 2 == 1 else i - 1)
+            partner = (date ^ turn, i + 1 if i % 2 == 1 else i - 1)
             if i in (0, size - 1):
                 partner = (date ^ 1, i)
             pairs.append((date * size + i, partner[0] * size + partner[1]))
-    received_first = lax.ppermute(first, axis, [(i, i ^ 1) for i in range(size)])
+    near = [
+        (date * size + i, (date ^ turn) * size + (i ^ 1)) for date in range(dates) for i in range(size)
+    ]
+    received_first = lax.ppermute(first, ("date", axis), near)
     received_second = lax.ppermute(second, ("date", axis), pairs)
     return received_first, received_second
 
@@ -605,45 +618,44 @@
         "pack", pack_body, [message, message, ((16, 128), F32)],
         cost=10**9,
     )(secondary, own, az_shift, az_fraction, lead)
+    half = ((64, 128), BF)
+    cross_first, cross_second, own_v = call(
+        "cross_pack", cross_pack_body, [half, half, ((2, LINES_DEV, 128), BF)], cost=2 * 10**9
+    )(first, second, own)
+    first, second = exchange(first, second, "az")
     tables = [jnp.asarray(table) for table in filter_tables()]
     prepared = call(
         "prepare", prepare_body,
-        [((1, 2, LINES_DEV, 512), BF), ((2, LINES_DEV, 128), BF), ((16, 512), F32), ((7, 128, 128), BF)]
-        + [(table.shape, BF) for table in tables],
-        [pltpu.VMEM((1, 512), jnp.int32), pltpu.VMEM((1, 512), F32), pltpu.SemaphoreType.DMA((8,))],
-        hbm=8, cost=2 * 10**9,
-    )(secondary, own, rg_shift, rg_fraction, *tables)
-    secondary_v, own_v, sample_rows, bands = prepared[:4]
-    tables_v = prepared[4:]
-    first, second = exchange(first, second, "az")
-    peers = [date_swap(own_v, k) for k in (1, 2, 3)]
-    halo = jnp.concatenate([first[384:448], second[384:448]], axis=0)
-    halo2, halo3 = [date_swap(halo, k) for k in (2, 3)]
-    edges, resampled, late = call(
-        "lines", lines_body, [((256, 256), BF), ((7, 256, 128), F32), ((128, 128), BF)],
+        [((1, 2, LINES_DEV, 512), BF), ((16, 512), F32), ((7, 128, 128), BF)],
+        [pltpu.VMEM((1, 512), jnp.int32), pltpu.VMEM((1, 512), F32), pltpu.SemaphoreType.DMA((3,))],
+        hbm=3, cost=2 * 10**9,
+    )(secondary, rg_shift, rg_fraction, cross_first)
+    secondary_v, sample_rows, bands = prepared
+    cross_first, cross_second = exchange(cross_first, cross_second, "az", 2)
+    peer2 = date_swap(own_v, 2)
+    edges, resampled = call(
+        "lines", lines_body, [((256, 256), BF), ((7, 256, 128), F32)],
         [pltpu.VMEM((2, 160, 512), BF), pltpu.VMEM((2, 16, 128), F32)],
         cost=10**9,
     )(secondary_v, line_rows, first, second, bands)
-    halo1 = date_swap(late, 1)
-    columns = ((7, 128, 128), BF)
-    master, column_high, column_low, middle = call(
-        "early", early_body, [((128, 512), BF), columns, columns, ((7, 128, 128), F32)],
-        cost=2 * 10**9,
-    )(own_v, *peers, resampled, *tables_v[:3])
+    core = call("core_pack", core_pack_body, [((512, 128), BF)], cost=10**7)(
+        own_v, peer2, first, second, cross_first, cross_second, edges
+    )[0]
+    core = date_swap(core, 1)
     message = ((176, 128), BF)
-    around, first, second = call(
-        "reference", reference_body, [((128, 512), BF), message, message], cost=10**8
-    )(halo, halo1, halo2, halo3, master, edges, sample_rows)
+    master, first, second = call(
+        "reference", reference_body, [((256, 512), BF), message, message], cost=10**8
+    )(own_v, peer2, core, first, second, cross_first, cross_second, edges, sample_rows)
     first, second = exchange(first, second, "rg")
     whole = ((1, 2, LINES_DEV, SAMPLES_DEV), F32)
     part = call("interior", interior_body, [whole], cost=4 * 10**9)(
-        resampled, around, column_high, column_low, middle, *tables_v
+        resampled, master, *tables
     )[0]
     return call(
         "edge", edge_body, [whole],
         [pltpu.VMEM((1, 2, LINES_DEV, 256), F32), pltpu.SemaphoreType.DMA((3,))],
         cost=10**9, far_out=True,
-    )(part, edges, master, around, sample_rows, first, second, *tables_v)[0]
+    )(part, edges, master, sample_rows, first, second, *tables)[0]
 
 
 def solution(mesh):

time: 25.3 us -> 24.5 us (0.968)
  the two profiles are of different devices: /device:TPU:144 before, /device:TPU:110 now
where the time goes in v5:
time: 24.5 us; the launch traced here: 24.2 us
  starting transfers between devices  10.8 us (44%)
  Pallas kernels  6.96 us (28%)
  waiting for transfers between devices  5.4 us (22%)
  local copies, waits for them, and re-layouts  0.91 us (4%)
    ppermute x3, starting transfers between devices, exchange(): received_second = lax.ppermute(second, ('date', axis), pairs)  7.17 us
    pallas_call x9, Pallas kernels, call(): pl.pallas_call(body, name=name, out_shape=[jax.ShapeDtypeStruct(shape, ki...  6.96 us
    ppermute x3, waiting for transfers between devices, exchange(): received_second = lax.ppermute(second, ('date', axis), pairs)  4.06 us
    ppermute x3, starting transfers between devices, exchange(): received_first = lax.ppermute(first, ('date', axis), near)  3.53 us
    ppermute x2, waiting for transfers between devices, date_swap(): return lax.ppermute(values, 'date', [(i, i ^ k) for i in range(4)])  1.34 us
    unnamed x20, local copies, waits for them, and re-layouts  0.91 us
  transfers between devices with their start and end apart: 8, of which 3 were waited for; matrix products, arithmetic and copies ran while one was open for 0% of the time, Pallas kernels for 17%

profile of v5, /device:TPU:110, one launch (start us, length us, event | category | flops | bytes accessed | tf_op | source)
XLA Modules:
  0.0 24.2 jit_solution(1515091451690686307)
XLA Ops:
  0.0 0.0 copy-start
  0.0 0.0 copy-start.5
  0.0 0.0 copy-start.4
  0.0 0.0 copy-start.1
  0.0 0.9 %copy-done = bf16[1,2,64,512]{3,2,1,0:T(8,128)(2,1)S(1)} copy-done((bf16[1,2,64,512]{3,2,1,0:T(8,128)(2,1)S(1)}, bf16[1,2,64,512]{3,2,1,0:T(8,128)(2,1)}, u32[]{:S(2)}) %copy-start) | copy-done | bytes 131096
  0.9 0.0 copy-done.5
  0.9 0.0 copy-done.4
  0.9 0.0 copy-done.1
  0.9 0.2 pack.1
  1.2 1.5 %collective-permute-start = (bf16[464,128]{1,0:T(8,128)(2,1)S(1)}, bf16[464,128]{1,0:T(8,128)(2,1)S(1)}, u32[]{:S(2)}, u32[]{:S(2)}) collective-permute-start(bf16[464,128]{1,0:T(8,128)(2,1)S(1)} %get-tuple-element.19.first), channel_id=1, source_target_pairs={{0,4},{4,0},{8,12},{12,8},{16,20},{20,16},{24,28},{28,24},{32,36},... | collective-permute-start | bytes 356360 | tf_op jit(solution)/shard_map/ppermute | solution.py:604
  2.6 0.0 copy-start.2
  2.6 0.0 copy-start.3
  2.6 4.7 %collective-permute-start.1 = (bf16[464,128]{1,0:T(8,128)(2,1)S(1)}, bf16[464,128]{1,0:T(8,128)(2,1)S(1)}, u32[]{:S(2)}, u32[]{:S(2)}) collective-permute-start(bf16[464,128]{1,0:T(8,128)(2,1)S(1)} %get-tuple-element.20.second), channel_id=1, source_target_pairs={{0,64},{4,8},{8,4},{12,16},{16,12},{20,24},{24,20},{28,32},{32,28}... | collective-permute-start | bytes 356360 | tf_op jit(solution)/shard_map/ppermute | solution.py:605
  7.3 0.1 collective-permute-start.4
  7.4 1.5 %collective-permute-start.3 = (bf16[64,128]{1,0:T(8,128)(2,1)S(1)}, bf16[64,128]{1,0:T(8,128)(2,1)S(1)}, u32[]{:S(2)}, u32[]{:S(2)}) collective-permute-start(bf16[64,128]{1,0:T(8,128)(2,1)S(1)} %get-tuple-element.21.after), channel_id=1, source_target_pairs={{0,132},{4,128},{8,140},{12,136},{16,148},{20,144},{24,156},{28,15... | collective-permute-start | bytes 49160 | tf_op jit(solution)/shard_map/ppermute | solution.py:604
  8.9 0.0 collective-permute-start.2
  8.9 0.0 copy-done.2
  8.9 0.0 copy-done.3
  8.9 0.6 %prepare.1 = (bf16[1,2,64,512]{3,2,1,0:T(8,128)(2,1)S(1)}, f32[16,512]{1,0:T(8,128)S(1)}, bf16[7,128,128]{2,1,0:T(8,128)(2,1)S(1)}) custom-call(bf16[1,2,64,512]{3,2,1,0:T(8,128)(2,1)S(1)} %copy-done, s32[1,512]{1,0:T(1,128)S(1)} %copy-done.2, f32[1,512]{1,0:T(1,128)S(1)} %copy-done.3, bf16[64,128]{1,0:T(8,128)(2,1)S(1)} %get-tuple-element.21.after), custom_call_target="tpu_custom_call" | custom-call | flops 2000000000 | bytes 20000000 | tf_op jit(solution)/shard_map/prepare/pallas_call | solution.py:579
  9.6 0.0 collective-permute-done.first
  9.6 1.6 %collective-permute-done.1.second = bf16[464,128]{1,0:T(8,128)(2,1)S(1)} collective-permute-done((bf16[464,128]{1,0:T(8,128)(2,1)S(1)}, bf16[464,128]{1,0:T(8,128)(2,1)S(1)}, u32[]{:S(2)}, u32[]{:S(2)}) %collective-permute-start.1) | collective-permute-done | bytes 118816 | tf_op jit(solution)/shard_map/ppermute | solution.py:605
  11.2 0.0 copy-start.6
  11.2 0.0 copy-start.7
  11.2 0.0 copy-start.8
  11.2 0.0 copy-start.9
  11.2 0.7 %lines.3 = (bf16[256,256]{1,0:T(8,128)(2,1)S(1)}, f32[7,256,128]{2,1,0:T(8,128)S(1)}) custom-call(bf16[1,2,64,512]{3,2,1,0:T(8,128)(2,1)S(1)} %get-tuple-element.22.secondary, f32[16,128]{1,0:T(8,128)S(1)} %get-tuple-element.23.line_rows, bf16[464,128]{1,0:T(8,128)(2,1)S(1)} %collective-permute-done.first, ...), custom_call_target="tpu_custom_call" | custom-call | flops 1000000000 | bytes 10000000 | tf_op jit(solution)/shard_map/lines/pallas_call | solution.py:579
  11.9 2.5 %collective-permute-done.4.cross_second = bf16[64,128]{1,0:T(8,128)(2,1)S(1)} collective-permute-done((bf16[64,128]{1,0:T(8,128)(2,1)S(1)}, bf16[64,128]{1,0:T(8,128)(2,1)S(1)}, u32[]{:S(2)}, u32[]{:S(2)}) %collective-permute-start.4) | collective-permute-done | bytes 16416 | tf_op jit(solution)/shard_map/ppermute | solution.py:605
  14.4 0.0 collective-permute-done.3.cross_first
  14.4 0.0 collective-permute-done.2.piece.peer2
  14.4 0.1 collective-permute-start.5
  14.5 1.3 %collective-permute-done.5.core = bf16[512,128]{1,0:T(8,128)(2,1)S(1)} collective-permute-done((bf16[512,128]{1,0:T(8,128)(2,1)S(1)}, bf16[512,128]{1,0:T(8,128)(2,1)S(1)}, u32[]{:S(2)}, u32[]{:S(2)}) %collective-permute-start.5) | collective-permute-done | bytes 131104 | tf_op jit(solution)/shard_map/ppermute | solution.py:610
  15.9 0.2 reference.1
  16.1 0.5 %collective-permute-start.6 = (bf16[176,128]{1,0:T(8,128)(2,1)S(1)}, bf16[176,128]{1,0:T(8,128)(2,1)S(1)}, u32[]{:S(2)}, u32[]{:S(2)}) collective-permute-start(bf16[176,128]{1,0:T(8,128)(2,1)S(1)} %get-tuple-element.31), channel_id=1, source_target_pairs={{0,1},{1,0},{2,3},{3,2},{64,65},{65,64},{66,67},{67,66},{128,129},... | collective-permute-start | bytes 135176 | tf_op jit(solution)/shard_map/ppermute | solution.py:604
  16.6 2.4 %collective-permute-start.7 = (bf16[176,128]{1,0:T(8,128)(2,1)S(1)}, bf16[176,128]{1,0:T(8,128)(2,1)S(1)}, u32[]{:S(2)}, u32[]{:S(2)}) collective-permute-start(bf16[176,128]{1,0:T(8,128)(2,1)S(1)} %get-tuple-element.32), channel_id=1, source_target_pairs={{0,64},{1,2},{2,1},{3,67},{64,0},{65,66},{66,65},{67,3},{128,192},... | collective-permute-start | bytes 135176 | tf_op jit(solution)/shard_map/ppermute | solution.py:605
  19.0 0.0 copy-done.6
  19.0 0.0 copy-done.7
  19.0 0.0 copy-done.8
  19.0 0.0 copy-done.9
  19.0 2.8 %interior.1.part = f32[1,2,64,512]{3,2,1,0:T(8,128)S(1)} custom-call(f32[7,256,128]{2,1,0:T(8,128)S(1)} %get-tuple-element.25.resampled, bf16[256,512]{1,0:T(8,128)(2,1)S(1)} %get-tuple-element.30.master, bf16[768,256]{1,0:T(8,128)(2,1)S(1)} %copy-done.8, bf16[384,768]{1,0:T(8,128)(2,1)S(1)} %copy-done.7, bf16[128,384]{1,0:T(8,128)(2,1)S(1)} %copy-done.9, ...), custom_call_target="tpu_custom_call" | custom-call | flops 4000000000 | bytes 40000000 | tf_op jit(solution)/shard_map/interior/pallas_call | solution.py:579
  21.8 0.0 collective-permute-done.6.first
  21.8 0.0 collective-permute-done.7.second
  21.8 2.3 %edge.1 = f32[1,2,64,512]{3,2,1,0:T(8,128)} custom-call(f32[1,2,64,512]{3,2,1,0:T(8,128)S(1)} %interior.1.part, bf16[256,256]{1,0:T(8,128)(2,1)S(1)} %get-tuple-element.28.after.edges, bf16[256,512]{1,0:T(8,128)(2,1)S(1)} %get-tuple-element.30.master, f32[16,512]{1,0:T(8,128)S(1)} %get-tuple-element.29.sample_rows, ...), custom_call_target="tpu_custom_call" | custom-call | flops 1000000000 | bytes 10000000 | tf_op jit(solution)/shard_map/edge/pallas_call | solution.py:579
  (3 shorter events, 0.0 us)
Async XLA Ops:
  0.0 0.9 %copy-start = (bf16[1,2,64,512]{3,2,1,0:T(8,128)(2,1)S(1)}, bf16[1,2,64,512]{3,2,1,0:T(8,128)(2,1)}, u32[]{:S(2)}) copy-start(bf16[1,2,64,512]{3,2,1,0:T(8,128)(2,1)} %secondary.3) | copy-start | bytes 393220
  0.0 0.9 %copy-start.5 = (f32[1,64]{1,0:T(1,128)S(1)}, f32[1,64]{1,0:T(1,128)}, u32[]{:S(2)}) copy-start(f32[1,64]{1,0:T(1,128)} %fraction.2) | copy-start | bytes 772
  0.0 0.9 %copy-start.4 = (s32[1,64]{1,0:T(1,128)S(1)}, s32[1,64]{1,0:T(1,128)}, u32[]{:S(2)}) copy-start(s32[1,64]{1,0:T(1,128)} %shift.2) | copy-start | bytes 772
  0.0 0.9 %copy-start.1 = (bf16[2,64,1,128]{3,1,2,0:T(8,128)(2,1)S(1)}, bf16[2,64,1,128]{3,1,2,0:T(8,128)(2,1)}, u32[]{:S(2)}) copy-start(bf16[2,64,1,128]{3,1,2,0:T(8,128)(2,1)} %param.10) | copy-start | bytes 98308
  1.2 8.4 %collective-permute-start = (bf16[464,128]{1,0:T(8,128)(2,1)S(1)}, bf16[464,128]{1,0:T(8,128)(2,1)S(1)}, u32[]{:S(2)}, u32[]{:S(2)}) collective-permute-start(bf16[464,128]{1,0:T(8,128)(2,1)S(1)} %get-tuple-element.19.first), channel_id=1, source_target_pairs={{0,4},{4,0},{8,12},{12,8},{16,20},{20,16},{24,28},{28,24},{32,36},... | collective-permute-start | bytes 356360 | tf_op jit(solution)/shard_map/ppermute | solution.py:604
  2.6 6.3 %copy-start.2 = (s32[1,512]{1,0:T(1,128)S(1)}, s32[1,512]{1,0:T(1,128)}, u32[]{:S(2)}) copy-start(s32[1,512]{1,0:T(1,128)} %shift.3) | copy-start | bytes 6148
  2.6 6.3 %copy-start.3 = (f32[1,512]{1,0:T(1,128)S(1)}, f32[1,512]{1,0:T(1,128)}, u32[]{:S(2)}) copy-start(f32[1,512]{1,0:T(1,128)} %fraction.3) | copy-start | bytes 6148
  2.6 8.5 %collective-permute-start.1 = (bf16[464,128]{1,0:T(8,128)(2,1)S(1)}, bf16[464,128]{1,0:T(8,128)(2,1)S(1)}, u32[]{:S(2)}, u32[]{:S(2)}) collective-permute-start(bf16[464,128]{1,0:T(8,128)(2,1)S(1)} %get-tuple-element.20.second), channel_id=1, source_target_pairs={{0,64},{4,8},{8,4},{12,16},{16,12},{20,24},{24,20},{28,32},{32,28}... | collective-permute-start | bytes 356360 | tf_op jit(solution)/shard_map/ppermute | solution.py:605
  7.3 7.1 %collective-permute-start.4 = (bf16[64,128]{1,0:T(8,128)(2,1)S(1)}, bf16[64,128]{1,0:T(8,128)(2,1)S(1)}, u32[]{:S(2)}, u32[]{:S(2)}) collective-permute-start(bf16[64,128]{1,0:T(8,128)(2,1)S(1)} %get-tuple-element.27), channel_id=1, source_target_pairs={{0,64},{4,136},{8,132},{12,144},{16,140},{20,152},{24,148},{28,160... | collective-permute-start | bytes 49160 | tf_op jit(solution)/shard_map/ppermute | solution.py:605
  7.4 7.0 %collective-permute-start.3 = (bf16[64,128]{1,0:T(8,128)(2,1)S(1)}, bf16[64,128]{1,0:T(8,128)(2,1)S(1)}, u32[]{:S(2)}, u32[]{:S(2)}) collective-permute-start(bf16[64,128]{1,0:T(8,128)(2,1)S(1)} %get-tuple-element.21.after), channel_id=1, source_target_pairs={{0,132},{4,128},{8,140},{12,136},{16,148},{20,144},{24,156},{28,15... | collective-permute-start | bytes 49160 | tf_op jit(solution)/shard_map/ppermute | solution.py:604
  8.9 5.5 %collective-permute-start.2 = (bf16[2,64,128]{2,1,0:T(8,128)(2,1)S(1)}, bf16[2,64,128]{2,1,0:T(8,128)(2,1)S(1)}, u32[]{:S(2)}, u32[]{:S(2)}) collective-permute-start(bf16[2,64,128]{2,1,0:T(8,128)(2,1)S(1)} %get-tuple-element.26.own), channel_id=1, source_target_pairs={{0,128},{64,192},{128,0},{192,64},{1,129},{65,193},{129,1},{193,65... | collective-permute-start | bytes 98312 | tf_op jit(solution)/shard_map/ppermute | solution.py:610
  11.2 7.9 %copy-start.6 = (bf16[3072,256]{1,0:T(8,128)(2,1)S(1)}, bf16[3072,256]{1,0:T(8,128)(2,1)}, u32[]{:S(2)}) copy-start(bf16[3072,256]{1,0:T(8,128)(2,1)} %constant.11.clone.samples) | copy-start | bytes 4718596
  11.2 7.9 %copy-start.7 = (bf16[384,768]{1,0:T(8,128)(2,1)S(1)}, bf16[384,768]{1,0:T(8,128)(2,1)}, u32[]{:S(2)}) copy-start(bf16[384,768]{1,0:T(8,128)(2,1)} %constant.9.clone.lines) | copy-start | bytes 1769476
  11.2 7.9 %copy-start.8 = (bf16[768,256]{1,0:T(8,128)(2,1)S(1)}, bf16[768,256]{1,0:T(8,128)(2,1)}, u32[]{:S(2)}) copy-start(bf16[768,256]{1,0:T(8,128)(2,1)} %constant.8.clone.forward) | copy-start | bytes 1179652
  11.2 7.9 %copy-start.9 = (bf16[128,384]{1,0:T(8,128)(2,1)S(1)}, bf16[128,384]{1,0:T(8,128)(2,1)}, u32[]{:S(2)}) copy-start(bf16[128,384]{1,0:T(8,128)(2,1)} %constant.10.clone.inverse) | copy-start | bytes 294916
  14.4 1.4 %collective-permute-start.5 = (bf16[512,128]{1,0:T(8,128)(2,1)S(1)}, bf16[512,128]{1,0:T(8,128)(2,1)S(1)}, u32[]{:S(2)}, u32[]{:S(2)}) collective-permute-start(bf16[512,128]{1,0:T(8,128)(2,1)S(1)} %core_pack.1), channel_id=1, source_target_pairs={{0,64},{64,0},{128,192},{192,128},{1,65},{65,1},{129,193},{193,129... | collective-permute-start | bytes 393224 | tf_op jit(solution)/shard_map/ppermute | solution.py:610
  16.1 5.7 %collective-permute-start.6 = (bf16[176,128]{1,0:T(8,128)(2,1)S(1)}, bf16[176,128]{1,0:T(8,128)(2,1)S(1)}, u32[]{:S(2)}, u32[]{:S(2)}) collective-permute-start(bf16[176,128]{1,0:T(8,128)(2,1)S(1)} %get-tuple-element.31), channel_id=1, source_target_pairs={{0,1},{1,0},{2,3},{3,2},{64,65},{65,64},{66,67},{67,66},{128,129},... | collective-permute-start | bytes 135176 | tf_op jit(solution)/shard_map/ppermute | solution.py:604
  16.6 5.2 %collective-permute-start.7 = (bf16[176,128]{1,0:T(8,128)(2,1)S(1)}, bf16[176,128]{1,0:T(8,128)(2,1)S(1)}, u32[]{:S(2)}, u32[]{:S(2)}) collective-permute-start(bf16[176,128]{1,0:T(8,128)(2,1)S(1)} %get-tuple-element.32), channel_id=1, source_target_pairs={{0,64},{1,2},{2,1},{3,67},{64,0},{65,66},{66,65},{67,3},{128,192},... | collective-permute-start | bytes 135176 | tf_op jit(solution)/shard_map/ppermute | solution.py:605

commit v6 on v5

--- a/solution.py
+++ b/solution.py
@@ -203,21 +203,36 @@
     second[448:464] = rows.astype(BF)
 
 
-def cross_pack_body(first, second, own, cross_first, cross_second, own_v):
+def cross_pack_body(first, second, own, mate, message, own_v):
     own_v[...] = own[...]
-    cross_first[...] = first[384:448]
-    cross_second[...] = second[384:448]
-
-
-def core_pack_body(own, piece, first, second, cross_first, cross_second, after, message):
-    del after
+    odd = lax.axis_index("az") % 2
+    side = lax.axis_index("date") % 2
+
+    @pl.when(side == 0)
+    def _():
+        message[0:64] = first[384:448]
+
+    @pl.when(side == 1)
+    def _():
+        message[0:64] = second[384:448]
+
+    def fill(half):
+        for part in range(2):
+            message[64 + part * 32 : 96 + part * 32] = mate[part, half : half + 32]
+
+    @pl.when(odd != side)
+    def _():
+        fill(0)
+
+    @pl.when(odd == side)
+    def _():
+        fill(32)
+
+
+def core_pack_body(piece, cross, message):
     for part in range(2):
-        message[part * 64 : part * 64 + 64] = own[part]
-        message[256 + part * 64 : 320 + part * 64] = piece[part]
-    message[128:192] = first[384:448]
-    message[192:256] = second[384:448]
-    message[384:448] = cross_first[...]
-    message[448:512] = cross_second[...]
+        message[part * 64 : part * 64 + 64] = piece[part]
+    message[128:256] = cross[...]
 
 
 def prepare_body(secondary, shift, fraction, after, secondary_v, sample_rows, bands,
@@ -299,7 +314,7 @@
         def _():
             for offset in range(4):
                 place = (value ^ offset) * 128
-                store(pieces[offset], slice(place, place + 128))
+                store(pieces[offset], slice(place, place + 128), value)
 
 
 def root(values):
@@ -363,23 +378,24 @@
     return columns_triple(jnp.concatenate([real, imag], axis=1))
 
 
-def reference_body(own, peer2, core, first, second, cross_first, cross_second, edges,
-                   sample_rows, master, send_first, send_second):
+def reference_body(own, peer1, peer2, core, first, second, near, cross, edges, sample_rows,
+                   master, send_first, send_second):
     az = lax.axis_index("az")
     odd = az % 2 == 1
     pieces = (
-        (own.at[0], own.at[1]), (core.at[0:64], core.at[64:128]),
-        (peer2.at[0], peer2.at[1]), (core.at[256:320], core.at[320:384]),
-    )
+        (own.at[0], own.at[1]), (peer1.at[0], peer1.at[1]),
+        (peer2.at[0], peer2.at[1]), (core.at[0:64], core.at[64:128]),
+    )
+    held, lent = (cross.at[0:64], cross.at[64:128]), (core.at[192:256], core.at[128:192])
     halos = (
-        (first.at[384:448], second.at[384:448]),
-        (core.at[128:192], core.at[192:256]),
-        (cross_first, cross_second),
-        (core.at[384:448], core.at[448:512]),
-    )
-
-    def store(piece, lanes):
-        middle, halo = piece
+        (first.at[384:448], second.at[384:448]), (near.at[0:64], near.at[64:128]),
+        (held[0], lent[0]), (held[1], lent[1]),
+    )
+
+    def store(piece, lanes, date):
+        middle, halo, shared = piece
+        if shared and date % 2 == 1:
+            halo = halo[::-1]
         for part in range(2):
             master[part * 128 + 32 : part * 128 + 96, lanes] = middle[part][...]
 
@@ -397,7 +413,7 @@
         def _():
             place(*halo[::-1])
 
-    by_date(list(zip(pieces, halos)), store)
+    by_date(list(zip(pieces, halos, (False, False, True, True))), store)
 
     @pl.when(az == 0)
     def _():
@@ -588,22 +604,31 @@
     )(*args)
 
 
-def exchange(first, second, axis, turn=0):
+def exchange(first, second, axis):
     size = lax.axis_size(axis)
     dates = lax.axis_size("date")
     pairs = []
     for date in range(dates):
         for i in range(size):
-            partner = (date ^ turn, i + 1 if i % 2 == 1 else i - 1)
+            partner = (date, i + 1 if i % 2 == 1 else i - 1)
             if i in (0, size - 1):
                 partner = (date ^ 1, i)
             pairs.append((date * size + i, partner[0] * size + partner[1]))
-    near = [
-        (date * size + i, (date ^ turn) * size + (i ^ 1)) for date in range(dates) for i in range(size)
-    ]
-    received_first = lax.ppermute(first, ("date", axis), near)
+    received_first = lax.ppermute(first, axis, [(i, i ^ 1) for i in range(size)])
     received_second = lax.ppermute(second, ("date", axis), pairs)
     return received_first, received_second
+
+
+def cross_swap(values):
+    size = lax.axis_size("az")
+    pairs = []
+    for date in range(lax.axis_size("date")):
+        for i in range(size):
+            partner = i ^ 1
+            if date % 2 == 1:
+                partner = i if i in (0, size - 1) else i + 1 if i % 2 == 1 else i - 1
+            pairs.append((date * size + i, (date ^ 2) * size + partner))
+    return lax.ppermute(values, ("date", "az"), pairs)
 
 
 def date_swap(values, k):
@@ -613,15 +638,15 @@
 def on_device(reference_slab, secondary, az_shift, az_fraction, rg_shift, rg_fraction):
     own = reference_slab.reshape(2, LINES_DEV, 128)
     message = ((464, 128), BF)
+    peer1 = date_swap(own, 1)
     lead = call("lead", lead_body, [((16, 128), F32)], cost=2 * 10**9)()[0]
     first, second, line_rows = call(
         "pack", pack_body, [message, message, ((16, 128), F32)],
         cost=10**9,
     )(secondary, own, az_shift, az_fraction, lead)
-    half = ((64, 128), BF)
-    cross_first, cross_second, own_v = call(
-        "cross_pack", cross_pack_body, [half, half, ((2, LINES_DEV, 128), BF)], cost=2 * 10**9
-    )(first, second, own)
+    cross, own_v = call(
+        "cross_pack", cross_pack_body, [((128, 128), BF), ((2, LINES_DEV, 128), BF)], cost=2 * 10**9
+    )(first, second, own, peer1)
     first, second = exchange(first, second, "az")
     tables = [jnp.asarray(table) for table in filter_tables()]
     prepared = call(
@@ -629,23 +654,22 @@
         [((1, 2, LINES_DEV, 512), BF), ((16, 512), F32), ((7, 128, 128), BF)],
         [pltpu.VMEM((1, 512), jnp.int32), pltpu.VMEM((1, 512), F32), pltpu.SemaphoreType.DMA((3,))],
         hbm=3, cost=2 * 10**9,
-    )(secondary, rg_shift, rg_fraction, cross_first)
+    )(secondary, rg_shift, rg_fraction, cross)
     secondary_v, sample_rows, bands = prepared
-    cross_first, cross_second = exchange(cross_first, cross_second, "az", 2)
+    near = date_swap(jnp.concatenate([first[384:448], second[384:448]], axis=0), 1)
     peer2 = date_swap(own_v, 2)
+    cross = cross_swap(cross)
+    core = call("core_pack", core_pack_body, [((256, 128), BF)], cost=10**7)(peer2, cross)[0]
+    core = date_swap(core, 1)
     edges, resampled = call(
         "lines", lines_body, [((256, 256), BF), ((7, 256, 128), F32)],
         [pltpu.VMEM((2, 160, 512), BF), pltpu.VMEM((2, 16, 128), F32)],
         cost=10**9,
     )(secondary_v, line_rows, first, second, bands)
-    core = call("core_pack", core_pack_body, [((512, 128), BF)], cost=10**7)(
-        own_v, peer2, first, second, cross_first, cross_second, edges
-    )[0]
-    core = date_swap(core, 1)
     message = ((176, 128), BF)
     master, first, second = call(
         "reference", reference_body, [((256, 512), BF), message, message], cost=10**8
-    )(own_v, peer2, core, first, second, cross_first, cross_second, edges, sample_rows)
+    )(own_v, peer1, peer2, core, first, second, near, cross, edges, sample_rows)
     first, second = exchange(first, second, "rg")
     whole = ((1, 2, LINES_DEV, SAMPLES_DEV), F32)
     part = call("interior", interior_body, [whole], cost=4 * 10**9)(

time: 24.5 us -> 23.6 us (0.963); the launches traced: 24.2 us -> 23.6 us
  waiting for transfers between devices: 5.4 us -> 4.93 us
    ppermute x3 -> x2, waiting for transfers between devices: 4.06 us -> 0.01 us  [exchange(): received_second = lax.ppermute(second, ('date', axis), pairs)]
    ppermute x3, waiting for transfers between devices: 0.01 us -> 2.4 us  [the longest x1 2.39 us: cross_swap(): return lax.ppermute(values, ('date', 'az'), pairs)]
    ppermute x3, starting transfers between devices: 3.53 us -> 2.03 us  [the longest x2 2.02 us: exchange(): lax.ppermute(first, axis, [(i, i ^ 1) for i in range(size)])]
    ppermute x2 -> x4, starting transfers between devices: 0.09 us -> 1.58 us  [date_swap(): return lax.ppermute(values, 'date', [(i, i ^ k) for i in range(4)])]
    ppermute x2 -> x4, waiting for transfers between devices: 1.34 us -> 2.53 us  [date_swap(): return lax.ppermute(values, 'date', [(i, i ^ k) for i in range(4)])]
    ppermute x3 -> x2, starting transfers between devices: 7.17 us -> 7.1 us  [exchange(): received_second = lax.ppermute(second, ('date', axis), pairs)]
  transfers between devices with their start and end apart: 8 -> 9, of which waited for: 3 -> 3; matrix products, arithmetic and copies ran while one was open for 0% -> 0% of each run, Pallas kernels for 17% -> 19%
where the time goes in v6:
time: 23.6 us
  starting transfers between devices  10.7 us (45%)
  Pallas kernels  6.95 us (29%)
  waiting for transfers between devices  4.93 us (21%)
  local copies, waits for them, and re-layouts  0.82 us (3%)
    ppermute x2, starting transfers between devices, exchange(): received_second = lax.ppermute(second, ('date', axis), pairs)  7.1 us
    pallas_call x9, Pallas kernels, call(): pl.pallas_call(body, name=name, out_shape=[jax.ShapeDtypeStruct(shape, ki...  6.95 us
    ppermute x4, waiting for transfers between devices, date_swap(): return lax.ppermute(values, 'date', [(i, i ^ k) for i in range(4)])  2.53 us
    ppermute x1, waiting for transfers between devices, cross_swap(): return lax.ppermute(values, ('date', 'az'), pairs)  2.39 us
    ppermute x2, starting transfers between devices, exchange(): lax.ppermute(first, axis, [(i, i ^ 1) for i in range(size)])  2.02 us
    ppermute x4, starting transfers between devices, date_swap(): return lax.ppermute(values, 'date', [(i, i ^ k) for i in range(4)])  1.58 us
    unnamed x20, local copies, waits for them, and re-layouts  0.81 us
  transfers between devices with their start and end apart: 9, of which 3 were waited for; matrix products, arithmetic and copies ran while one was open for 0% of the time, Pallas kernels for 19%

profile of v6, /device:TPU:110, one launch (start us, length us, event | category | flops | bytes accessed | tf_op | source)
XLA Modules:
  0.0 23.6 jit_solution(2852292310914316656)
XLA Ops:
  0.0 0.0 copy-start
  0.0 0.0 copy-start.1
  0.0 0.0 copy-start.4
  0.0 0.0 copy-start.5
  0.0 0.1 collective-permute-start
  0.1 0.8 %copy-done = bf16[1,2,64,512]{3,2,1,0:T(8,128)(2,1)S(1)} copy-done((bf16[1,2,64,512]{3,2,1,0:T(8,128)(2,1)S(1)}, bf16[1,2,64,512]{3,2,1,0:T(8,128)(2,1)}, u32[]{:S(2)}) %copy-start) | copy-done | bytes 131096
  0.9 0.0 copy-done.1
  0.9 0.0 copy-done.4
  0.9 0.0 copy-done.5
  0.9 0.2 %pack.1 = (bf16[464,128]{1,0:T(8,128)(2,1)S(1)}, bf16[464,128]{1,0:T(8,128)(2,1)S(1)}, f32[16,128]{1,0:T(8,128)S(1)}) custom-call(bf16[1,2,64,512]{3,2,1,0:T(8,128)(2,1)S(1)} %copy-done, bf16[2,64,128]{2,1,0:T(8,128)(2,1)S(1)} %bitcast.2, s32[1,64]{1,0:T(1,128)S(1)} %copy-done.4, f32[1,64]{1,0:T(1,128)S(1)} %copy-done.5, f32[16,128]{1,0:T(8,128)S(1)} %lead.1), custom_call_target="tpu_custom_call" | custom-call | flops 1000000000 | bytes 10000000 | tf_op jit(solution)/shard_map/pack/pallas_call | solution.py:595
  1.2 1.5 %collective-permute-start.1 = (bf16[464,128]{1,0:T(8,128)(2,1)S(1)}, bf16[464,128]{1,0:T(8,128)(2,1)S(1)}, u32[]{:S(2)}, u32[]{:S(2)}) collective-permute-start(bf16[464,128]{1,0:T(8,128)(2,1)S(1)} %get-tuple-element.18.first), channel_id=1, source_target_pairs={{0,4},{4,0},{8,12},{12,8},{16,20},{20,16},{24,28},{28,24},{32,36},... | collective-permute-start | bytes 356360 | tf_op jit(solution)/shard_map/ppermute | solution.py:617
  2.6 0.0 copy-start.2
  2.6 0.0 copy-start.3
  2.6 4.7 %collective-permute-start.2 = (bf16[464,128]{1,0:T(8,128)(2,1)S(1)}, bf16[464,128]{1,0:T(8,128)(2,1)S(1)}, u32[]{:S(2)}, u32[]{:S(2)}) collective-permute-start(bf16[464,128]{1,0:T(8,128)(2,1)S(1)} %get-tuple-element.19.second), channel_id=1, source_target_pairs={{0,64},{4,8},{8,4},{12,16},{16,12},{20,24},{24,20},{28,32},{32,28}... | collective-permute-start | bytes 356360 | tf_op jit(solution)/shard_map/ppermute | solution.py:618
  7.3 0.0 collective-permute-done.mate.peer1
  7.4 0.9 %collective-permute-start.3 = (bf16[2,64,128]{2,1,0:T(8,128)(2,1)S(1)}, bf16[2,64,128]{2,1,0:T(8,128)(2,1)S(1)}, u32[]{:S(2)}, u32[]{:S(2)}) collective-permute-start(bf16[2,64,128]{2,1,0:T(8,128)(2,1)S(1)} %get-tuple-element.25.own), channel_id=1, source_target_pairs={{0,128},{64,192},{128,0},{192,64},{1,129},{65,193},{129,1},{193,65... | collective-permute-start | bytes 98312 | tf_op jit(solution)/shard_map/ppermute | solution.py:635
  8.3 0.0 collective-permute-start.4
  8.3 0.0 copy-done.2
  8.3 0.0 copy-done.3
  8.3 0.6 %prepare.1 = (bf16[1,2,64,512]{3,2,1,0:T(8,128)(2,1)S(1)}, f32[16,512]{1,0:T(8,128)S(1)}, bf16[7,128,128]{2,1,0:T(8,128)(2,1)S(1)}) custom-call(bf16[1,2,64,512]{3,2,1,0:T(8,128)(2,1)S(1)} %copy-done, s32[1,512]{1,0:T(1,128)S(1)} %copy-done.2, f32[1,512]{1,0:T(1,128)S(1)} %copy-done.3, bf16[128,128]{1,0:T(8,128)(2,1)S(1)} %get-tuple-element.20.after), custom_call_target="tpu_custom_call" | custom-call | flops 2000000000 | bytes 20000000 | tf_op jit(solution)/shard_map/prepare/pallas_call | solution.py:595
  8.9 2.4 %collective-permute-done.3.piece.peer2 = bf16[2,64,128]{2,1,0:T(8,128)(2,1)S(1)} collective-permute-done((bf16[2,64,128]{2,1,0:T(8,128)(2,1)S(1)}, bf16[2,64,128]{2,1,0:T(8,128)(2,1)S(1)}, u32[]{:S(2)}, u32[]{:S(2)}) %collective-permute-start.3) | collective-permute-done | bytes 32800 | tf_op jit(solution)/shard_map/ppermute | solution.py:635
  11.4 2.4 %collective-permute-done.4.cross = bf16[128,128]{1,0:T(8,128)(2,1)S(1)} collective-permute-done((bf16[128,128]{1,0:T(8,128)(2,1)S(1)}, bf16[128,128]{1,0:T(8,128)(2,1)S(1)}, u32[]{:S(2)}, u32[]{:S(2)}) %collective-permute-start.4) | collective-permute-done | bytes 32800 | tf_op jit(solution)/shard_map/ppermute | solution.py:631
  13.8 0.0 collective-permute-start.5
  13.8 0.0 collective-permute-done.2.second
  13.8 0.0 collective-permute-done.1.first
  13.8 0.6 %collective-permute-start.6 = (bf16[128,128]{1,0:T(8,128)(2,1)S(1)}, bf16[128,128]{1,0:T(8,128)(2,1)S(1)}, u32[]{:S(2)}, u32[]{:S(2)}) collective-permute-start(bf16[128,128]{1,0:T(8,128)(2,1)S(1)} %pad_maximum_fusion), channel_id=1, source_target_pairs={{0,64},{64,0},{128,192},{192,128},{1,65},{65,1},{129,193},{193,129... | collective-permute-start | bytes 98312 | tf_op jit(solution)/shard_map/ppermute | solution.py:635
  14.4 0.0 copy-start.6
  14.4 0.0 copy-start.7
  14.4 0.0 copy-start.8
  14.4 0.0 copy-start.9
  14.4 0.7 %lines.3 = (bf16[256,256]{1,0:T(8,128)(2,1)S(1)}, f32[7,256,128]{2,1,0:T(8,128)S(1)}) custom-call(bf16[1,2,64,512]{3,2,1,0:T(8,128)(2,1)S(1)} %get-tuple-element.21.secondary, f32[16,128]{1,0:T(8,128)S(1)} %get-tuple-element.22.line_rows, bf16[464,128]{1,0:T(8,128)(2,1)S(1)} %collective-permute-done.1.first, ...), custom_call_target="tpu_custom_call" | custom-call | flops 1000000000 | bytes 10000000 | tf_op jit(solution)/shard_map/lines/pallas_call | solution.py:595
  15.1 0.0 collective-permute-done.5.core
  15.1 0.1 collective-permute-done.6.near
  15.2 0.2 reference.1
  15.5 0.5 %collective-permute-start.7 = (bf16[176,128]{1,0:T(8,128)(2,1)S(1)}, bf16[176,128]{1,0:T(8,128)(2,1)S(1)}, u32[]{:S(2)}, u32[]{:S(2)}) collective-permute-start(bf16[176,128]{1,0:T(8,128)(2,1)S(1)} %get-tuple-element.29), channel_id=1, source_target_pairs={{0,1},{1,0},{2,3},{3,2},{4,5},{5,4},{6,7},{7,6},{8,9},{9,8},{10,11... | collective-permute-start | bytes 135176 | tf_op jit(solution)/shard_map/ppermute | solution.py:617
  16.0 2.4 %collective-permute-start.8 = (bf16[176,128]{1,0:T(8,128)(2,1)S(1)}, bf16[176,128]{1,0:T(8,128)(2,1)S(1)}, u32[]{:S(2)}, u32[]{:S(2)}) collective-permute-start(bf16[176,128]{1,0:T(8,128)(2,1)S(1)} %get-tuple-element.30), channel_id=1, source_target_pairs={{0,64},{1,2},{2,1},{3,67},{64,0},{65,66},{66,65},{67,3},{128,192},... | collective-permute-start | bytes 135176 | tf_op jit(solution)/shard_map/ppermute | solution.py:618
  18.4 0.0 copy-done.6
  18.4 0.0 copy-done.7
  18.4 0.0 copy-done.8
  18.4 0.0 copy-done.9
  18.4 2.8 %interior.1.part = f32[1,2,64,512]{3,2,1,0:T(8,128)S(1)} custom-call(f32[7,256,128]{2,1,0:T(8,128)S(1)} %get-tuple-element.24.resampled, bf16[256,512]{1,0:T(8,128)(2,1)S(1)} %get-tuple-element.28.master, bf16[768,256]{1,0:T(8,128)(2,1)S(1)} %copy-done.8, bf16[384,768]{1,0:T(8,128)(2,1)S(1)} %copy-done.7, bf16[128,384]{1,0:T(8,128)(2,1)S(1)} %copy-done.9, ...), custom_call_target="tpu_custom_call" | custom-call | flops 4000000000 | bytes 40000000 | tf_op jit(solution)/shard_map/interior/pallas_call | solution.py:595
  21.2 0.0 collective-permute-done.7.first
  21.2 0.0 collective-permute-done.8.second
  21.2 2.3 %edge.1 = f32[1,2,64,512]{3,2,1,0:T(8,128)} custom-call(f32[1,2,64,512]{3,2,1,0:T(8,128)S(1)} %interior.1.part, bf16[256,256]{1,0:T(8,128)(2,1)S(1)} %get-tuple-element.26.edges, bf16[256,512]{1,0:T(8,128)(2,1)S(1)} %get-tuple-element.28.master, f32[16,512]{1,0:T(8,128)S(1)} %get-tuple-element.27.sample_rows, ...), custom_call_target="tpu_custom_call" | custom-call | flops 1000000000 | bytes 10000000 | tf_op jit(solution)/shard_map/edge/pallas_call | solution.py:595
  (6 shorter events, 0.0 us)
Async XLA Ops:
  0.0 0.9 %copy-start = (bf16[1,2,64,512]{3,2,1,0:T(8,128)(2,1)S(1)}, bf16[1,2,64,512]{3,2,1,0:T(8,128)(2,1)}, u32[]{:S(2)}) copy-start(bf16[1,2,64,512]{3,2,1,0:T(8,128)(2,1)} %secondary.3) | copy-start | bytes 393220
  0.0 0.9 %copy-start.1 = (bf16[2,64,1,128]{3,1,2,0:T(8,128)(2,1)S(1)}, bf16[2,64,1,128]{3,1,2,0:T(8,128)(2,1)}, u32[]{:S(2)}) copy-start(bf16[2,64,1,128]{3,1,2,0:T(8,128)(2,1)} %param.10) | copy-start | bytes 98308
  0.0 0.9 %copy-start.4 = (s32[1,64]{1,0:T(1,128)S(1)}, s32[1,64]{1,0:T(1,128)}, u32[]{:S(2)}) copy-start(s32[1,64]{1,0:T(1,128)} %shift.2) | copy-start | bytes 772
  0.0 0.9 %copy-start.5 = (f32[1,64]{1,0:T(1,128)S(1)}, f32[1,64]{1,0:T(1,128)}, u32[]{:S(2)}) copy-start(f32[1,64]{1,0:T(1,128)} %fraction.2) | copy-start | bytes 772
  0.0 7.3 %collective-permute-start = (bf16[2,64,128]{2,1,0:T(8,128)(2,1)}, bf16[2,64,128]{2,1,0:T(8,128)(2,1)S(1)}, u32[]{:S(2)}, u32[]{:S(2)}) collective-permute-start(bf16[2,64,128]{2,1,0:T(8,128)(2,1)} %bitcast.1), channel_id=1, source_target_pairs={{0,64},{64,0},{128,192},{192,128},{1,65},{65,1},{129,193},{193,129... | collective-permute-start | bytes 98312 | tf_op jit(solution)/shard_map/ppermute | solution.py:635
  1.2 12.6 %collective-permute-start.1 = (bf16[464,128]{1,0:T(8,128)(2,1)S(1)}, bf16[464,128]{1,0:T(8,128)(2,1)S(1)}, u32[]{:S(2)}, u32[]{:S(2)}) collective-permute-start(bf16[464,128]{1,0:T(8,128)(2,1)S(1)} %get-tuple-element.18.first), channel_id=1, source_target_pairs={{0,4},{4,0},{8,12},{12,8},{16,20},{20,16},{24,28},{28,24},{32,36},... | collective-permute-start | bytes 356360 | tf_op jit(solution)/shard_map/ppermute | solution.py:617
  2.6 5.6 %copy-start.2 = (s32[1,512]{1,0:T(1,128)S(1)}, s32[1,512]{1,0:T(1,128)}, u32[]{:S(2)}) copy-start(s32[1,512]{1,0:T(1,128)} %shift.3) | copy-start | bytes 6148
  2.6 5.6 %copy-start.3 = (f32[1,512]{1,0:T(1,128)S(1)}, f32[1,512]{1,0:T(1,128)}, u32[]{:S(2)}) copy-start(f32[1,512]{1,0:T(1,128)} %fraction.3) | copy-start | bytes 6148
  2.6 11.1 %collective-permute-start.2 = (bf16[464,128]{1,0:T(8,128)(2,1)S(1)}, bf16[464,128]{1,0:T(8,128)(2,1)S(1)}, u32[]{:S(2)}, u32[]{:S(2)}) collective-permute-start(bf16[464,128]{1,0:T(8,128)(2,1)S(1)} %get-tuple-element.19.second), channel_id=1, source_target_pairs={{0,64},{4,8},{8,4},{12,16},{16,12},{20,24},{24,20},{28,32},{32,28}... | collective-permute-start | bytes 356360 | tf_op jit(solution)/shard_map/ppermute | solution.py:618
  7.4 4.0 %collective-permute-start.3 = (bf16[2,64,128]{2,1,0:T(8,128)(2,1)S(1)}, bf16[2,64,128]{2,1,0:T(8,128)(2,1)S(1)}, u32[]{:S(2)}, u32[]{:S(2)}) collective-permute-start(bf16[2,64,128]{2,1,0:T(8,128)(2,1)S(1)} %get-tuple-element.25.own), channel_id=1, source_target_pairs={{0,128},{64,192},{128,0},{192,64},{1,129},{65,193},{129,1},{193,65... | collective-permute-start | bytes 98312 | tf_op jit(solution)/shard_map/ppermute | solution.py:635
  8.3 5.5 %collective-permute-start.4 = (bf16[128,128]{1,0:T(8,128)(2,1)S(1)}, bf16[128,128]{1,0:T(8,128)(2,1)S(1)}, u32[]{:S(2)}, u32[]{:S(2)}) collective-permute-start(bf16[128,128]{1,0:T(8,128)(2,1)S(1)} %get-tuple-element.20.after), channel_id=1, source_target_pairs={{0,132},{4,128},{8,140},{12,136},{16,148},{20,144},{24,156},{28,15... | collective-permute-start | bytes 98312 | tf_op jit(solution)/shard_map/ppermute | solution.py:631
  13.8 1.4 %collective-permute-start.5 = (bf16[256,128]{1,0:T(8,128)(2,1)S(1)}, bf16[256,128]{1,0:T(8,128)(2,1)S(1)}, u32[]{:S(2)}, u32[]{:S(2)}) collective-permute-start(bf16[256,128]{1,0:T(8,128)(2,1)S(1)} %core_pack.1), channel_id=1, source_target_pairs={{0,64},{64,0},{128,192},{192,128},{1,65},{65,1},{129,193},{193,129... | collective-permute-start | bytes 196616 | tf_op jit(solution)/shard_map/ppermute | solution.py:635
  13.8 1.4 %collective-permute-start.6 = (bf16[128,128]{1,0:T(8,128)(2,1)S(1)}, bf16[128,128]{1,0:T(8,128)(2,1)S(1)}, u32[]{:S(2)}, u32[]{:S(2)}) collective-permute-start(bf16[128,128]{1,0:T(8,128)(2,1)S(1)} %pad_maximum_fusion), channel_id=1, source_target_pairs={{0,64},{64,0},{128,192},{192,128},{1,65},{65,1},{129,193},{193,129... | collective-permute-start | bytes 98312 | tf_op jit(solution)/shard_map/ppermute | solution.py:635
  14.4 4.0 %copy-start.6 = (bf16[3072,256]{1,0:T(8,128)(2,1)S(1)}, bf16[3072,256]{1,0:T(8,128)(2,1)}, u32[]{:S(2)}) copy-start(bf16[3072,256]{1,0:T(8,128)(2,1)} %constant.11.clone.samples) | copy-start | bytes 4718596
  14.4 4.0 %copy-start.7 = (bf16[384,768]{1,0:T(8,128)(2,1)S(1)}, bf16[384,768]{1,0:T(8,128)(2,1)}, u32[]{:S(2)}) copy-start(bf16[384,768]{1,0:T(8,128)(2,1)} %constant.9.clone.lines) | copy-start | bytes 1769476
  14.4 4.0 %copy-start.8 = (bf16[768,256]{1,0:T(8,128)(2,1)S(1)}, bf16[768,256]{1,0:T(8,128)(2,1)}, u32[]{:S(2)}) copy-start(bf16[768,256]{1,0:T(8,128)(2,1)} %constant.8.clone.forward) | copy-start | bytes 1179652
  14.4 4.0 %copy-start.9 = (bf16[128,384]{1,0:T(8,128)(2,1)S(1)}, bf16[128,384]{1,0:T(8,128)(2,1)}, u32[]{:S(2)}) copy-start(bf16[128,384]{1,0:T(8,128)(2,1)} %constant.10.clone.inverse) | copy-start | bytes 294916
  15.5 5.7 %collective-permute-start.7 = (bf16[176,128]{1,0:T(8,128)(2,1)S(1)}, bf16[176,128]{1,0:T(8,128)(2,1)S(1)}, u32[]{:S(2)}, u32[]{:S(2)}) collective-permute-start(bf16[176,128]{1,0:T(8,128)(2,1)S(1)} %get-tuple-element.29), channel_id=1, source_target_pairs={{0,1},{1,0},{2,3},{3,2},{4,5},{5,4},{6,7},{7,6},{8,9},{9,8},{10,11... | collective-permute-start | bytes 135176 | tf_op jit(solution)/shard_map/ppermute | solution.py:617
  16.0 5.2 %collective-permute-start.8 = (bf16[176,128]{1,0:T(8,128)(2,1)S(1)}, bf16[176,128]{1,0:T(8,128)(2,1)S(1)}, u32[]{:S(2)}, u32[]{:S(2)}) collective-permute-start(bf16[176,128]{1,0:T(8,128)(2,1)S(1)} %get-tuple-element.30), channel_id=1, source_target_pairs={{0,64},{1,2},{2,1},{3,67},{64,0},{65,66},{66,65},{67,3},{128,192},... | collective-permute-start | bytes 135176 | tf_op jit(solution)/shard_map/ppermute | solution.py:618

commit v7 on v6

--- a/solution.py
+++ b/solution.py
@@ -229,7 +229,10 @@
         fill(32)
 
 
-def core_pack_body(piece, cross, message):
+def core_pack_body(piece, cross, first, second, after, message):
+    del after
+    message[256:320] = first[384:448]
+    message[320:384] = second[384:448]
     for part in range(2):
         message[part * 64 : part * 64 + 64] = piece[part]
     message[128:256] = cross[...]
@@ -378,7 +381,7 @@
     return columns_triple(jnp.concatenate([real, imag], axis=1))
 
 
-def reference_body(own, peer1, peer2, core, first, second, near, cross, edges, sample_rows,
+def reference_body(own, peer1, peer2, core, first, second, cross, edges, sample_rows,
                    master, send_first, send_second):
     az = lax.axis_index("az")
     odd = az % 2 == 1
@@ -388,7 +391,7 @@
     )
     held, lent = (cross.at[0:64], cross.at[64:128]), (core.at[192:256], core.at[128:192])
     halos = (
-        (first.at[384:448], second.at[384:448]), (near.at[0:64], near.at[64:128]),
+        (first.at[384:448], second.at[384:448]), (core.at[256:320], core.at[320:384]),
         (held[0], lent[0]), (held[1], lent[1]),
     )
 
@@ -656,10 +659,11 @@
         hbm=3, cost=2 * 10**9,
     )(secondary, rg_shift, rg_fraction, cross)
     secondary_v, sample_rows, bands = prepared
-    near = date_swap(jnp.concatenate([first[384:448], second[384:448]], axis=0), 1)
     peer2 = date_swap(own_v, 2)
     cross = cross_swap(cross)
-    core = call("core_pack", core_pack_body, [((256, 128), BF)], cost=10**7)(peer2, cross)[0]
+    core = call("core_pack", core_pack_body, [((384, 128), BF)], cost=10**7)(
+        peer2, cross, first, second, sample_rows
+    )[0]
     core = date_swap(core, 1)
     edges, resampled = call(
         "lines", lines_body, [((256, 256), BF), ((7, 256, 128), F32)],
@@ -669,7 +673,7 @@
     message = ((176, 128), BF)
     master, first, second = call(
         "reference", reference_body, [((256, 512), BF), message, message], cost=10**8
-    )(own_v, peer1, peer2, core, first, second, near, cross, edges, sample_rows)
+    )(own_v, peer1, peer2, core, first, second, cross, edges, sample_rows)
     first, second = exchange(first, second, "rg")
     whole = ((1, 2, LINES_DEV, SAMPLES_DEV), F32)
     part = call("interior", interior_body, [whole], cost=4 * 10**9)(

time: 23.6 us -> 23.6 us (level)
  starting transfers between devices: 10.7 us -> 10.2 us
  waiting for transfers between devices: 4.93 us -> 5.32 us
    ppermute x4 -> x3, starting transfers between devices: 1.58 us -> 1.1 us  [date_swap(): return lax.ppermute(values, 'date', [(i, i ^ k) for i in range(4)])]
    ppermute x4 -> x3, waiting for transfers between devices: 2.53 us -> 2.92 us  [date_swap(): return lax.ppermute(values, 'date', [(i, i ^ k) for i in range(4)])]
  transfers between devices with their start and end apart: 9 -> 8, of which waited for: 3 -> 3; matrix products, arithmetic and copies ran while one was open for 0% -> 0% of each run, Pallas kernels for 19% -> 19%
where the time goes in v7:
time: 23.6 us; the launch traced here: 23.5 us
  starting transfers between devices  10.2 us (43%)
  Pallas kernels  6.95 us (29%)
  waiting for transfers between devices  5.32 us (23%)
  local copies, waits for them, and re-layouts  0.82 us (3%)
    ppermute x2, starting transfers between devices, exchange(): received_second = lax.ppermute(second, ('date', axis), pairs)  7.1 us
    pallas_call x9, Pallas kernels, call(): pl.pallas_call(body, name=name, out_shape=[jax.ShapeDtypeStruct(shape, ki...  6.95 us
    ppermute x3, waiting for transfers between devices, date_swap(): return lax.ppermute(values, 'date', [(i, i ^ k) for i in range(4)])  2.92 us
    ppermute x1, waiting for transfers between devices, cross_swap(): return lax.ppermute(values, ('date', 'az'), pairs)  2.39 us
    ppermute x2, starting transfers between devices, exchange(): lax.ppermute(first, axis, [(i, i ^ 1) for i in range(size)])  2.02 us
    ppermute x3, starting transfers between devices, date_swap(): return lax.ppermute(values, 'date', [(i, i ^ k) for i in range(4)])  1.1 us
    unnamed x20, local copies, waits for them, and re-layouts  0.82 us
  transfers between devices with their start and end apart: 8, of which 3 were waited for; matrix products, arithmetic and copies ran while one was open for 0% of the time, Pallas kernels for 19%

profile of v7, /device:TPU:110, one launch (start us, length us, event | category | flops | bytes accessed | tf_op | source)
XLA Modules:
  0.0 23.5 jit_solution(4411631433998376062)
XLA Ops:
  0.0 0.0 copy-start
  0.0 0.0 copy-start.1
  0.0 0.0 copy-start.4
  0.0 0.0 copy-start.5
  0.0 0.1 collective-permute-start
  0.1 0.8 %copy-done = bf16[1,2,64,512]{3,2,1,0:T(8,128)(2,1)S(1)} copy-done((bf16[1,2,64,512]{3,2,1,0:T(8,128)(2,1)S(1)}, bf16[1,2,64,512]{3,2,1,0:T(8,128)(2,1)}, u32[]{:S(2)}) %copy-start) | copy-done | bytes 131096
  0.9 0.0 copy-done.1
  0.9 0.0 copy-done.4
  0.9 0.0 copy-done.5
  0.9 0.2 %pack.1 = (bf16[464,128]{1,0:T(8,128)(2,1)S(1)}, bf16[464,128]{1,0:T(8,128)(2,1)S(1)}, f32[16,128]{1,0:T(8,128)S(1)}) custom-call(bf16[1,2,64,512]{3,2,1,0:T(8,128)(2,1)S(1)} %copy-done, bf16[2,64,128]{2,1,0:T(8,128)(2,1)S(1)} %bitcast.2, s32[1,64]{1,0:T(1,128)S(1)} %copy-done.4, f32[1,64]{1,0:T(1,128)S(1)} %copy-done.5, f32[16,128]{1,0:T(8,128)S(1)} %lead.1), custom_call_target="tpu_custom_call" | custom-call | flops 1000000000 | bytes 10000000 | tf_op jit(solution)/shard_map/pack/pallas_call | solution.py:598
  1.2 1.5 %collective-permute-start.1 = (bf16[464,128]{1,0:T(8,128)(2,1)S(1)}, bf16[464,128]{1,0:T(8,128)(2,1)S(1)}, u32[]{:S(2)}, u32[]{:S(2)}) collective-permute-start(bf16[464,128]{1,0:T(8,128)(2,1)S(1)} %get-tuple-element.18.first), channel_id=1, source_target_pairs={{0,4},{4,0},{8,12},{12,8},{16,20},{20,16},{24,28},{28,24},{32,36},... | collective-permute-start | bytes 356360 | tf_op jit(solution)/shard_map/ppermute | solution.py:620
  2.6 0.0 copy-start.2
  2.6 0.0 copy-start.3
  2.6 4.7 %collective-permute-start.2 = (bf16[464,128]{1,0:T(8,128)(2,1)S(1)}, bf16[464,128]{1,0:T(8,128)(2,1)S(1)}, u32[]{:S(2)}, u32[]{:S(2)}) collective-permute-start(bf16[464,128]{1,0:T(8,128)(2,1)S(1)} %get-tuple-element.19.second), channel_id=1, source_target_pairs={{0,64},{4,8},{8,4},{12,16},{16,12},{20,24},{24,20},{28,32},{32,28}... | collective-permute-start | bytes 356360 | tf_op jit(solution)/shard_map/ppermute | solution.py:621
  7.3 0.0 collective-permute-done.mate.peer1
  7.4 0.9 %collective-permute-start.3 = (bf16[2,64,128]{2,1,0:T(8,128)(2,1)S(1)}, bf16[2,64,128]{2,1,0:T(8,128)(2,1)S(1)}, u32[]{:S(2)}, u32[]{:S(2)}) collective-permute-start(bf16[2,64,128]{2,1,0:T(8,128)(2,1)S(1)} %get-tuple-element.25.own), channel_id=1, source_target_pairs={{0,128},{64,192},{128,0},{192,64},{1,129},{65,193},{129,1},{193,65... | collective-permute-start | bytes 98312 | tf_op jit(solution)/shard_map/ppermute | solution.py:638
  8.3 0.0 collective-permute-start.4
  8.3 0.0 copy-done.2
  8.3 0.0 copy-done.3
  8.3 0.6 %prepare.1 = (bf16[1,2,64,512]{3,2,1,0:T(8,128)(2,1)S(1)}, f32[16,512]{1,0:T(8,128)S(1)}, bf16[7,128,128]{2,1,0:T(8,128)(2,1)S(1)}) custom-call(bf16[1,2,64,512]{3,2,1,0:T(8,128)(2,1)S(1)} %copy-done, s32[1,512]{1,0:T(1,128)S(1)} %copy-done.2, f32[1,512]{1,0:T(1,128)S(1)} %copy-done.3, bf16[128,128]{1,0:T(8,128)(2,1)S(1)} %get-tuple-element.20.after), custom_call_target="tpu_custom_call" | custom-call | flops 2000000000 | bytes 20000000 | tf_op jit(solution)/shard_map/prepare/pallas_call | solution.py:598
  8.9 2.4 %collective-permute-done.3.piece.peer2 = bf16[2,64,128]{2,1,0:T(8,128)(2,1)S(1)} collective-permute-done((bf16[2,64,128]{2,1,0:T(8,128)(2,1)S(1)}, bf16[2,64,128]{2,1,0:T(8,128)(2,1)S(1)}, u32[]{:S(2)}, u32[]{:S(2)}) %collective-permute-start.3) | collective-permute-done | bytes 32800 | tf_op jit(solution)/shard_map/ppermute | solution.py:638
  11.4 2.4 %collective-permute-done.4.cross = bf16[128,128]{1,0:T(8,128)(2,1)S(1)} collective-permute-done((bf16[128,128]{1,0:T(8,128)(2,1)S(1)}, bf16[128,128]{1,0:T(8,128)(2,1)S(1)}, u32[]{:S(2)}, u32[]{:S(2)}) %collective-permute-start.4) | collective-permute-done | bytes 32800 | tf_op jit(solution)/shard_map/ppermute | solution.py:634
  13.8 0.0 collective-permute-done.1.first
  13.8 0.0 collective-permute-done.2.second
  13.8 0.1 collective-permute-start.5
  13.9 0.0 copy-start.6
  13.9 0.0 copy-start.7
  13.9 0.0 copy-start.8
  13.9 0.0 copy-start.9
  13.9 0.7 %lines.3 = (bf16[256,256]{1,0:T(8,128)(2,1)S(1)}, f32[7,256,128]{2,1,0:T(8,128)S(1)}) custom-call(bf16[1,2,64,512]{3,2,1,0:T(8,128)(2,1)S(1)} %get-tuple-element.21.secondary, f32[16,128]{1,0:T(8,128)S(1)} %get-tuple-element.22.line_rows, bf16[464,128]{1,0:T(8,128)(2,1)S(1)} %collective-permute-done.1.first, ...), custom_call_target="tpu_custom_call" | custom-call | flops 1000000000 | bytes 10000000 | tf_op jit(solution)/shard_map/lines/pallas_call | solution.py:598
  14.7 0.5 %collective-permute-done.5.core = bf16[384,128]{1,0:T(8,128)(2,1)S(1)} collective-permute-done((bf16[384,128]{1,0:T(8,128)(2,1)S(1)}, bf16[384,128]{1,0:T(8,128)(2,1)S(1)}, u32[]{:S(2)}, u32[]{:S(2)}) %collective-permute-start.5) | collective-permute-done | bytes 98336 | tf_op jit(solution)/shard_map/ppermute | solution.py:638
  15.2 0.2 reference.1
  15.4 0.5 %collective-permute-start.6 = (bf16[176,128]{1,0:T(8,128)(2,1)S(1)}, bf16[176,128]{1,0:T(8,128)(2,1)S(1)}, u32[]{:S(2)}, u32[]{:S(2)}) collective-permute-start(bf16[176,128]{1,0:T(8,128)(2,1)S(1)} %get-tuple-element.29), channel_id=1, source_target_pairs={{0,1},{1,0},{2,3},{3,2},{4,5},{5,4},{6,7},{7,6},{8,9},{9,8},{10,11... | collective-permute-start | bytes 135176 | tf_op jit(solution)/shard_map/ppermute | solution.py:620
  15.9 2.4 %collective-permute-start.7 = (bf16[176,128]{1,0:T(8,128)(2,1)S(1)}, bf16[176,128]{1,0:T(8,128)(2,1)S(1)}, u32[]{:S(2)}, u32[]{:S(2)}) collective-permute-start(bf16[176,128]{1,0:T(8,128)(2,1)S(1)} %get-tuple-element.30), channel_id=1, source_target_pairs={{0,64},{1,2},{2,1},{3,67},{64,0},{65,66},{66,65},{67,3},{128,192},... | collective-permute-start | bytes 135176 | tf_op jit(solution)/shard_map/ppermute | solution.py:621
  18.3 0.0 copy-done.6
  18.3 0.0 copy-done.7
  18.3 0.0 copy-done.8
  18.3 0.0 copy-done.9
  18.3 2.8 %interior.1.part = f32[1,2,64,512]{3,2,1,0:T(8,128)S(1)} custom-call(f32[7,256,128]{2,1,0:T(8,128)S(1)} %get-tuple-element.24.resampled, bf16[256,512]{1,0:T(8,128)(2,1)S(1)} %get-tuple-element.28.master, bf16[768,256]{1,0:T(8,128)(2,1)S(1)} %copy-done.8, bf16[384,768]{1,0:T(8,128)(2,1)S(1)} %copy-done.7, bf16[128,384]{1,0:T(8,128)(2,1)S(1)} %copy-done.9, ...), custom_call_target="tpu_custom_call" | custom-call | flops 4000000000 | bytes 40000000 | tf_op jit(solution)/shard_map/interior/pallas_call | solution.py:598
  21.1 0.0 collective-permute-done.6.first
  21.1 0.0 collective-permute-done.7.second
  21.1 2.3 %edge.1 = f32[1,2,64,512]{3,2,1,0:T(8,128)} custom-call(f32[1,2,64,512]{3,2,1,0:T(8,128)S(1)} %interior.1.part, bf16[256,256]{1,0:T(8,128)(2,1)S(1)} %get-tuple-element.27.edges, bf16[256,512]{1,0:T(8,128)(2,1)S(1)} %get-tuple-element.28.master, f32[16,512]{1,0:T(8,128)S(1)} %get-tuple-element.26.after.sample_rows, ...), custom_call_target="tpu_custom_call" | custom-call | flops 1000000000 | bytes 10000000 | tf_op jit(solution)/shard_map/edge/pallas_call | solution.py:598
  (3 shorter events, 0.0 us)
Async XLA Ops:
  0.0 0.9 %copy-start = (bf16[1,2,64,512]{3,2,1,0:T(8,128)(2,1)S(1)}, bf16[1,2,64,512]{3,2,1,0:T(8,128)(2,1)}, u32[]{:S(2)}) copy-start(bf16[1,2,64,512]{3,2,1,0:T(8,128)(2,1)} %secondary.3) | copy-start | bytes 393220
  0.0 0.9 %copy-start.1 = (bf16[2,64,1,128]{3,1,2,0:T(8,128)(2,1)S(1)}, bf16[2,64,1,128]{3,1,2,0:T(8,128)(2,1)}, u32[]{:S(2)}) copy-start(bf16[2,64,1,128]{3,1,2,0:T(8,128)(2,1)} %param.10) | copy-start | bytes 98308
  0.0 0.9 %copy-start.4 = (s32[1,64]{1,0:T(1,128)S(1)}, s32[1,64]{1,0:T(1,128)}, u32[]{:S(2)}) copy-start(s32[1,64]{1,0:T(1,128)} %shift.2) | copy-start | bytes 772
  0.0 0.9 %copy-start.5 = (f32[1,64]{1,0:T(1,128)S(1)}, f32[1,64]{1,0:T(1,128)}, u32[]{:S(2)}) copy-start(f32[1,64]{1,0:T(1,128)} %fraction.2) | copy-start | bytes 772
  0.0 7.3 %collective-permute-start = (bf16[2,64,128]{2,1,0:T(8,128)(2,1)}, bf16[2,64,128]{2,1,0:T(8,128)(2,1)S(1)}, u32[]{:S(2)}, u32[]{:S(2)}) collective-permute-start(bf16[2,64,128]{2,1,0:T(8,128)(2,1)} %bitcast.1), channel_id=1, source_target_pairs={{0,64},{64,0},{128,192},{192,128},{1,65},{65,1},{129,193},{193,129... | collective-permute-start | bytes 98312 | tf_op jit(solution)/shard_map/ppermute | solution.py:638
  1.2 12.6 %collective-permute-start.1 = (bf16[464,128]{1,0:T(8,128)(2,1)S(1)}, bf16[464,128]{1,0:T(8,128)(2,1)S(1)}, u32[]{:S(2)}, u32[]{:S(2)}) collective-permute-start(bf16[464,128]{1,0:T(8,128)(2,1)S(1)} %get-tuple-element.18.first), channel_id=1, source_target_pairs={{0,4},{4,0},{8,12},{12,8},{16,20},{20,16},{24,28},{28,24},{32,36},... | collective-permute-start | bytes 356360 | tf_op jit(solution)/shard_map/ppermute | solution.py:620
  2.6 5.6 %copy-start.2 = (s32[1,512]{1,0:T(1,128)S(1)}, s32[1,512]{1,0:T(1,128)}, u32[]{:S(2)}) copy-start(s32[1,512]{1,0:T(1,128)} %shift.3) | copy-start | bytes 6148
  2.6 5.6 %copy-start.3 = (f32[1,512]{1,0:T(1,128)S(1)}, f32[1,512]{1,0:T(1,128)}, u32[]{:S(2)}) copy-start(f32[1,512]{1,0:T(1,128)} %fraction.3) | copy-start | bytes 6148
  2.6 11.1 %collective-permute-start.2 = (bf16[464,128]{1,0:T(8,128)(2,1)S(1)}, bf16[464,128]{1,0:T(8,128)(2,1)S(1)}, u32[]{:S(2)}, u32[]{:S(2)}) collective-permute-start(bf16[464,128]{1,0:T(8,128)(2,1)S(1)} %get-tuple-element.19.second), channel_id=1, source_target_pairs={{0,64},{4,8},{8,4},{12,16},{16,12},{20,24},{24,20},{28,32},{32,28}... | collective-permute-start | bytes 356360 | tf_op jit(solution)/shard_map/ppermute | solution.py:621
  7.4 4.0 %collective-permute-start.3 = (bf16[2,64,128]{2,1,0:T(8,128)(2,1)S(1)}, bf16[2,64,128]{2,1,0:T(8,128)(2,1)S(1)}, u32[]{:S(2)}, u32[]{:S(2)}) collective-permute-start(bf16[2,64,128]{2,1,0:T(8,128)(2,1)S(1)} %get-tuple-element.25.own), channel_id=1, source_target_pairs={{0,128},{64,192},{128,0},{192,64},{1,129},{65,193},{129,1},{193,65... | collective-permute-start | bytes 98312 | tf_op jit(solution)/shard_map/ppermute | solution.py:638
  8.3 5.5 %collective-permute-start.4 = (bf16[128,128]{1,0:T(8,128)(2,1)S(1)}, bf16[128,128]{1,0:T(8,128)(2,1)S(1)}, u32[]{:S(2)}, u32[]{:S(2)}) collective-permute-start(bf16[128,128]{1,0:T(8,128)(2,1)S(1)} %get-tuple-element.20.after), channel_id=1, source_target_pairs={{0,132},{4,128},{8,140},{12,136},{16,148},{20,144},{24,156},{28,15... | collective-permute-start | bytes 98312 | tf_op jit(solution)/shard_map/ppermute | solution.py:634
  13.8 1.4 %collective-permute-start.5 = (bf16[384,128]{1,0:T(8,128)(2,1)S(1)}, bf16[384,128]{1,0:T(8,128)(2,1)S(1)}, u32[]{:S(2)}, u32[]{:S(2)}) collective-permute-start(bf16[384,128]{1,0:T(8,128)(2,1)S(1)} %core_pack.1), channel_id=1, source_target_pairs={{0,64},{64,0},{128,192},{192,128},{1,65},{65,1},{129,193},{193,129... | collective-permute-start | bytes 294920 | tf_op jit(solution)/shard_map/ppermute | solution.py:638
  13.9 4.4 %copy-start.6 = (bf16[3072,256]{1,0:T(8,128)(2,1)S(1)}, bf16[3072,256]{1,0:T(8,128)(2,1)}, u32[]{:S(2)}) copy-start(bf16[3072,256]{1,0:T(8,128)(2,1)} %constant.11.clone.samples) | copy-start | bytes 4718596
  13.9 4.4 %copy-start.7 = (bf16[384,768]{1,0:T(8,128)(2,1)S(1)}, bf16[384,768]{1,0:T(8,128)(2,1)}, u32[]{:S(2)}) copy-start(bf16[384,768]{1,0:T(8,128)(2,1)} %constant.9.clone.lines) | copy-start | bytes 1769476
  13.9 4.4 %copy-start.8 = (bf16[768,256]{1,0:T(8,128)(2,1)S(1)}, bf16[768,256]{1,0:T(8,128)(2,1)}, u32[]{:S(2)}) copy-start(bf16[768,256]{1,0:T(8,128)(2,1)} %constant.8.clone.forward) | copy-start | bytes 1179652
  13.9 4.4 %copy-start.9 = (bf16[128,384]{1,0:T(8,128)(2,1)S(1)}, bf16[128,384]{1,0:T(8,128)(2,1)}, u32[]{:S(2)}) copy-start(bf16[128,384]{1,0:T(8,128)(2,1)} %constant.10.clone.inverse) | copy-start | bytes 294916
  15.4 5.7 %collective-permute-start.6 = (bf16[176,128]{1,0:T(8,128)(2,1)S(1)}, bf16[176,128]{1,0:T(8,128)(2,1)S(1)}, u32[]{:S(2)}, u32[]{:S(2)}) collective-permute-start(bf16[176,128]{1,0:T(8,128)(2,1)S(1)} %get-tuple-element.29), channel_id=1, source_target_pairs={{0,1},{1,0},{2,3},{3,2},{4,5},{5,4},{6,7},{7,6},{8,9},{9,8},{10,11... | collective-permute-start | bytes 135176 | tf_op jit(solution)/shard_map/ppermute | solution.py:620
  15.9 5.2 %collective-permute-start.7 = (bf16[176,128]{1,0:T(8,128)(2,1)S(1)}, bf16[176,128]{1,0:T(8,128)(2,1)S(1)}, u32[]{:S(2)}, u32[]{:S(2)}) collective-permute-start(bf16[176,128]{1,0:T(8,128)(2,1)S(1)} %get-tuple-element.30), channel_id=1, source_target_pairs={{0,64},{1,2},{2,1},{3,67},{64,0},{65,66},{66,65},{67,3},{128,192},... | collective-permute-start | bytes 135176 | tf_op jit(solution)/shard_map/ppermute | solution.py:621

commit v8 on v7

--- a/solution.py
+++ b/solution.py
@@ -560,11 +560,26 @@
             turned(sample_rows[:, lanes], own_cell),
         )
         matrix = band_matrix(sample, 128).astype(BF)
-        values = dot(jnp.concatenate(window, axis=0).astype(BF), matrix)
-        return cross_product(values[:128], values[128:], real, imag)
-
+        return jnp.concatenate(window, axis=0).astype(BF), matrix, real, imag
+
+    sides_in = [
+        block(from_left, 0, 0, (48, 32), False), block(from_right, 3, 1, (80, 64), True)
+    ]
+    empty = jnp.zeros((128, 128), BF)
+    (left, left_matrix, *_), (right, right_matrix, *_) = sides_in
+    both = jnp.concatenate(
+        [
+            jnp.concatenate([left_matrix, empty], axis=1),
+            jnp.concatenate([empty, right_matrix], axis=1),
+        ],
+        axis=0,
+    )
+    values = dot(jnp.concatenate([left, right], axis=1), both)
     products = [
-        block(from_left, 0, 0, (48, 32), False), block(from_right, 3, 1, (80, 64), True)
+        cross_product(
+            values[:128, at * 128 : at * 128 + 128], values[128:, at * 128 : at * 128 + 128], *side[2:]
+        )
+        for at, side in enumerate(sides_in)
     ]
     results = filter_columns(sample_columns(products, forward[...]), lines, inverse)
     rows = jnp.concatenate([pair_rows(tops, bottoms) for tops, bottoms in results], axis=0)

time: 23.6 us -> 23.5 us (level)
  no operation moved by 1% of the time
where the time goes in v8:
time: 23.5 us; the launch traced here: 23.4 us
  starting transfers between devices  10.2 us (43%)
  Pallas kernels  6.91 us (29%)
  waiting for transfers between devices  5.32 us (23%)
  local copies, waits for them, and re-layouts  0.82 us (3%)
    ppermute x2, starting transfers between devices, exchange(): received_second = lax.ppermute(second, ('date', axis), pairs)  7.1 us
    pallas_call x9, Pallas kernels, call(): pl.pallas_call(body, name=name, out_shape=[jax.ShapeDtypeStruct(shape, ki...  6.91 us
    ppermute x3, waiting for transfers between devices, date_swap(): return lax.ppermute(values, 'date', [(i, i ^ k) for i in range(4)])  2.92 us
    ppermute x1, waiting for transfers between devices, cross_swap(): return lax.ppermute(values, ('date', 'az'), pairs)  2.39 us
    ppermute x2, starting transfers between devices, exchange(): lax.ppermute(first, axis, [(i, i ^ 1) for i in range(size)])  2.02 us
    ppermute x3, starting transfers between devices, date_swap(): return lax.ppermute(values, 'date', [(i, i ^ k) for i in range(4)])  1.1 us
    unnamed x20, local copies, waits for them, and re-layouts  0.82 us
  transfers between devices with their start and end apart: 8, of which 3 were waited for; matrix products, arithmetic and copies ran while one was open for 0% of the time, Pallas kernels for 19%

profile of v8, /device:TPU:110, one launch (start us, length us, event | category | flops | bytes accessed | tf_op | source)
XLA Modules:
  0.0 23.4 jit_solution(15203903704386530312)
XLA Ops:
  0.0 0.0 copy-start
  0.0 0.0 copy-start.1
  0.0 0.0 copy-start.4
  0.0 0.0 copy-start.5
  0.0 0.1 collective-permute-start
  0.1 0.8 %copy-done = bf16[1,2,64,512]{3,2,1,0:T(8,128)(2,1)S(1)} copy-done((bf16[1,2,64,512]{3,2,1,0:T(8,128)(2,1)S(1)}, bf16[1,2,64,512]{3,2,1,0:T(8,128)(2,1)}, u32[]{:S(2)}) %copy-start) | copy-done | bytes 131096
  0.9 0.0 copy-done.1
  0.9 0.0 copy-done.4
  0.9 0.0 copy-done.5
  0.9 0.2 %pack.1 = (bf16[464,128]{1,0:T(8,128)(2,1)S(1)}, bf16[464,128]{1,0:T(8,128)(2,1)S(1)}, f32[16,128]{1,0:T(8,128)S(1)}) custom-call(bf16[1,2,64,512]{3,2,1,0:T(8,128)(2,1)S(1)} %copy-done, bf16[2,64,128]{2,1,0:T(8,128)(2,1)S(1)} %bitcast.2, s32[1,64]{1,0:T(1,128)S(1)} %copy-done.4, f32[1,64]{1,0:T(1,128)S(1)} %copy-done.5, f32[16,128]{1,0:T(8,128)S(1)} %lead.1), custom_call_target="tpu_custom_call" | custom-call | flops 1000000000 | bytes 10000000 | tf_op jit(solution)/shard_map/pack/pallas_call | solution.py:613
  1.2 1.5 %collective-permute-start.1 = (bf16[464,128]{1,0:T(8,128)(2,1)S(1)}, bf16[464,128]{1,0:T(8,128)(2,1)S(1)}, u32[]{:S(2)}, u32[]{:S(2)}) collective-permute-start(bf16[464,128]{1,0:T(8,128)(2,1)S(1)} %get-tuple-element.18.first), channel_id=1, source_target_pairs={{0,4},{4,0},{8,12},{12,8},{16,20},{20,16},{24,28},{28,24},{32,36},... | collective-permute-start | bytes 356360 | tf_op jit(solution)/shard_map/ppermute | solution.py:635
  2.6 0.0 copy-start.2
  2.6 0.0 copy-start.3
  2.6 4.7 %collective-permute-start.2 = (bf16[464,128]{1,0:T(8,128)(2,1)S(1)}, bf16[464,128]{1,0:T(8,128)(2,1)S(1)}, u32[]{:S(2)}, u32[]{:S(2)}) collective-permute-start(bf16[464,128]{1,0:T(8,128)(2,1)S(1)} %get-tuple-element.19.second), channel_id=1, source_target_pairs={{0,64},{4,8},{8,4},{12,16},{16,12},{20,24},{24,20},{28,32},{32,28}... | collective-permute-start | bytes 356360 | tf_op jit(solution)/shard_map/ppermute | solution.py:636
  7.3 0.0 collective-permute-done.mate.peer1
  7.4 0.9 %collective-permute-start.3 = (bf16[2,64,128]{2,1,0:T(8,128)(2,1)S(1)}, bf16[2,64,128]{2,1,0:T(8,128)(2,1)S(1)}, u32[]{:S(2)}, u32[]{:S(2)}) collective-permute-start(bf16[2,64,128]{2,1,0:T(8,128)(2,1)S(1)} %get-tuple-element.25.own), channel_id=1, source_target_pairs={{0,128},{64,192},{128,0},{192,64},{1,129},{65,193},{129,1},{193,65... | collective-permute-start | bytes 98312 | tf_op jit(solution)/shard_map/ppermute | solution.py:653
  8.3 0.0 collective-permute-start.4
  8.3 0.0 copy-done.2
  8.3 0.0 copy-done.3
  8.3 0.6 %prepare.1 = (bf16[1,2,64,512]{3,2,1,0:T(8,128)(2,1)S(1)}, f32[16,512]{1,0:T(8,128)S(1)}, bf16[7,128,128]{2,1,0:T(8,128)(2,1)S(1)}) custom-call(bf16[1,2,64,512]{3,2,1,0:T(8,128)(2,1)S(1)} %copy-done, s32[1,512]{1,0:T(1,128)S(1)} %copy-done.2, f32[1,512]{1,0:T(1,128)S(1)} %copy-done.3, bf16[128,128]{1,0:T(8,128)(2,1)S(1)} %get-tuple-element.20.after), custom_call_target="tpu_custom_call" | custom-call | flops 2000000000 | bytes 20000000 | tf_op jit(solution)/shard_map/prepare/pallas_call | solution.py:613
  8.9 2.4 %collective-permute-done.3.piece.peer2 = bf16[2,64,128]{2,1,0:T(8,128)(2,1)S(1)} collective-permute-done((bf16[2,64,128]{2,1,0:T(8,128)(2,1)S(1)}, bf16[2,64,128]{2,1,0:T(8,128)(2,1)S(1)}, u32[]{:S(2)}, u32[]{:S(2)}) %collective-permute-start.3) | collective-permute-done | bytes 32800 | tf_op jit(solution)/shard_map/ppermute | solution.py:653
  11.4 2.4 %collective-permute-done.4.cross = bf16[128,128]{1,0:T(8,128)(2,1)S(1)} collective-permute-done((bf16[128,128]{1,0:T(8,128)(2,1)S(1)}, bf16[128,128]{1,0:T(8,128)(2,1)S(1)}, u32[]{:S(2)}, u32[]{:S(2)}) %collective-permute-start.4) | collective-permute-done | bytes 32800 | tf_op jit(solution)/shard_map/ppermute | solution.py:649
  13.8 0.0 collective-permute-done.1.first
  13.8 0.0 collective-permute-done.2.second
  13.8 0.1 collective-permute-start.5
  13.9 0.0 copy-start.6
  13.9 0.0 copy-start.7
  13.9 0.0 copy-start.8
  13.9 0.0 copy-start.9
  13.9 0.7 %lines.3 = (bf16[256,256]{1,0:T(8,128)(2,1)S(1)}, f32[7,256,128]{2,1,0:T(8,128)S(1)}) custom-call(bf16[1,2,64,512]{3,2,1,0:T(8,128)(2,1)S(1)} %get-tuple-element.21.secondary, f32[16,128]{1,0:T(8,128)S(1)} %get-tuple-element.22.line_rows, bf16[464,128]{1,0:T(8,128)(2,1)S(1)} %collective-permute-done.1.first, ...), custom_call_target="tpu_custom_call" | custom-call | flops 1000000000 | bytes 10000000 | tf_op jit(solution)/shard_map/lines/pallas_call | solution.py:613
  14.7 0.5 %collective-permute-done.5.core = bf16[384,128]{1,0:T(8,128)(2,1)S(1)} collective-permute-done((bf16[384,128]{1,0:T(8,128)(2,1)S(1)}, bf16[384,128]{1,0:T(8,128)(2,1)S(1)}, u32[]{:S(2)}, u32[]{:S(2)}) %collective-permute-start.5) | collective-permute-done | bytes 98336 | tf_op jit(solution)/shard_map/ppermute | solution.py:653
  15.2 0.2 reference.1
  15.4 0.5 %collective-permute-start.6 = (bf16[176,128]{1,0:T(8,128)(2,1)S(1)}, bf16[176,128]{1,0:T(8,128)(2,1)S(1)}, u32[]{:S(2)}, u32[]{:S(2)}) collective-permute-start(bf16[176,128]{1,0:T(8,128)(2,1)S(1)} %get-tuple-element.29), channel_id=1, source_target_pairs={{0,1},{1,0},{2,3},{3,2},{4,5},{5,4},{6,7},{7,6},{8,9},{9,8},{10,11... | collective-permute-start | bytes 135176 | tf_op jit(solution)/shard_map/ppermute | solution.py:635
  15.9 2.4 %collective-permute-start.7 = (bf16[176,128]{1,0:T(8,128)(2,1)S(1)}, bf16[176,128]{1,0:T(8,128)(2,1)S(1)}, u32[]{:S(2)}, u32[]{:S(2)}) collective-permute-start(bf16[176,128]{1,0:T(8,128)(2,1)S(1)} %get-tuple-element.30), channel_id=1, source_target_pairs={{0,64},{1,2},{2,1},{3,67},{64,0},{65,66},{66,65},{67,3},{128,192},... | collective-permute-start | bytes 135176 | tf_op jit(solution)/shard_map/ppermute | solution.py:636
  18.3 0.0 copy-done.6
  18.3 0.0 copy-done.7
  18.3 0.0 copy-done.8
  18.3 0.0 copy-done.9
  18.3 2.8 %interior.1.part = f32[1,2,64,512]{3,2,1,0:T(8,128)S(1)} custom-call(f32[7,256,128]{2,1,0:T(8,128)S(1)} %get-tuple-element.24.resampled, bf16[256,512]{1,0:T(8,128)(2,1)S(1)} %get-tuple-element.28.master, bf16[768,256]{1,0:T(8,128)(2,1)S(1)} %copy-done.8, bf16[384,768]{1,0:T(8,128)(2,1)S(1)} %copy-done.7, bf16[128,384]{1,0:T(8,128)(2,1)S(1)} %copy-done.9, ...), custom_call_target="tpu_custom_call" | custom-call | flops 4000000000 | bytes 40000000 | tf_op jit(solution)/shard_map/interior/pallas_call | solution.py:613
  21.1 0.0 collective-permute-done.6.first
  21.1 0.0 collective-permute-done.7.second
  21.1 2.3 %edge.1 = f32[1,2,64,512]{3,2,1,0:T(8,128)} custom-call(f32[1,2,64,512]{3,2,1,0:T(8,128)S(1)} %interior.1.part, bf16[256,256]{1,0:T(8,128)(2,1)S(1)} %get-tuple-element.27.edges, bf16[256,512]{1,0:T(8,128)(2,1)S(1)} %get-tuple-element.28.master, f32[16,512]{1,0:T(8,128)S(1)} %get-tuple-element.26.after.sample_rows, ...), custom_call_target="tpu_custom_call" | custom-call | flops 1000000000 | bytes 10000000 | tf_op jit(solution)/shard_map/edge/pallas_call | solution.py:613
  (3 shorter events, 0.0 us)
Async XLA Ops:
  0.0 0.9 %copy-start = (bf16[1,2,64,512]{3,2,1,0:T(8,128)(2,1)S(1)}, bf16[1,2,64,512]{3,2,1,0:T(8,128)(2,1)}, u32[]{:S(2)}) copy-start(bf16[1,2,64,512]{3,2,1,0:T(8,128)(2,1)} %secondary.3) | copy-start | bytes 393220
  0.0 0.9 %copy-start.1 = (bf16[2,64,1,128]{3,1,2,0:T(8,128)(2,1)S(1)}, bf16[2,64,1,128]{3,1,2,0:T(8,128)(2,1)}, u32[]{:S(2)}) copy-start(bf16[2,64,1,128]{3,1,2,0:T(8,128)(2,1)} %param.10) | copy-start | bytes 98308
  0.0 0.9 %copy-start.4 = (s32[1,64]{1,0:T(1,128)S(1)}, s32[1,64]{1,0:T(1,128)}, u32[]{:S(2)}) copy-start(s32[1,64]{1,0:T(1,128)} %shift.2) | copy-start | bytes 772
  0.0 0.9 %copy-start.5 = (f32[1,64]{1,0:T(1,128)S(1)}, f32[1,64]{1,0:T(1,128)}, u32[]{:S(2)}) copy-start(f32[1,64]{1,0:T(1,128)} %fraction.2) | copy-start | bytes 772
  0.0 7.3 %collective-permute-start = (bf16[2,64,128]{2,1,0:T(8,128)(2,1)}, bf16[2,64,128]{2,1,0:T(8,128)(2,1)S(1)}, u32[]{:S(2)}, u32[]{:S(2)}) collective-permute-start(bf16[2,64,128]{2,1,0:T(8,128)(2,1)} %bitcast.1), channel_id=1, source_target_pairs={{0,64},{64,0},{128,192},{192,128},{1,65},{65,1},{129,193},{193,129... | collective-permute-start | bytes 98312 | tf_op jit(solution)/shard_map/ppermute | solution.py:653
  1.2 12.6 %collective-permute-start.1 = (bf16[464,128]{1,0:T(8,128)(2,1)S(1)}, bf16[464,128]{1,0:T(8,128)(2,1)S(1)}, u32[]{:S(2)}, u32[]{:S(2)}) collective-permute-start(bf16[464,128]{1,0:T(8,128)(2,1)S(1)} %get-tuple-element.18.first), channel_id=1, source_target_pairs={{0,4},{4,0},{8,12},{12,8},{16,20},{20,16},{24,28},{28,24},{32,36},... | collective-permute-start | bytes 356360 | tf_op jit(solution)/shard_map/ppermute | solution.py:635
  2.6 5.6 %copy-start.2 = (s32[1,512]{1,0:T(1,128)S(1)}, s32[1,512]{1,0:T(1,128)}, u32[]{:S(2)}) copy-start(s32[1,512]{1,0:T(1,128)} %shift.3) | copy-start | bytes 6148
  2.6 5.6 %copy-start.3 = (f32[1,512]{1,0:T(1,128)S(1)}, f32[1,512]{1,0:T(1,128)}, u32[]{:S(2)}) copy-start(f32[1,512]{1,0:T(1,128)} %fraction.3) | copy-start | bytes 6148
  2.6 11.1 %collective-permute-start.2 = (bf16[464,128]{1,0:T(8,128)(2,1)S(1)}, bf16[464,128]{1,0:T(8,128)(2,1)S(1)}, u32[]{:S(2)}, u32[]{:S(2)}) collective-permute-start(bf16[464,128]{1,0:T(8,128)(2,1)S(1)} %get-tuple-element.19.second), channel_id=1, source_target_pairs={{0,64},{4,8},{8,4},{12,16},{16,12},{20,24},{24,20},{28,32},{32,28}... | collective-permute-start | bytes 356360 | tf_op jit(solution)/shard_map/ppermute | solution.py:636
  7.4 4.0 %collective-permute-start.3 = (bf16[2,64,128]{2,1,0:T(8,128)(2,1)S(1)}, bf16[2,64,128]{2,1,0:T(8,128)(2,1)S(1)}, u32[]{:S(2)}, u32[]{:S(2)}) collective-permute-start(bf16[2,64,128]{2,1,0:T(8,128)(2,1)S(1)} %get-tuple-element.25.own), channel_id=1, source_target_pairs={{0,128},{64,192},{128,0},{192,64},{1,129},{65,193},{129,1},{193,65... | collective-permute-start | bytes 98312 | tf_op jit(solution)/shard_map/ppermute | solution.py:653
  8.3 5.5 %collective-permute-start.4 = (bf16[128,128]{1,0:T(8,128)(2,1)S(1)}, bf16[128,128]{1,0:T(8,128)(2,1)S(1)}, u32[]{:S(2)}, u32[]{:S(2)}) collective-permute-start(bf16[128,128]{1,0:T(8,128)(2,1)S(1)} %get-tuple-element.20.after), channel_id=1, source_target_pairs={{0,132},{4,128},{8,140},{12,136},{16,148},{20,144},{24,156},{28,15... | collective-permute-start | bytes 98312 | tf_op jit(solution)/shard_map/ppermute | solution.py:649
  13.8 1.4 %collective-permute-start.5 = (bf16[384,128]{1,0:T(8,128)(2,1)S(1)}, bf16[384,128]{1,0:T(8,128)(2,1)S(1)}, u32[]{:S(2)}, u32[]{:S(2)}) collective-permute-start(bf16[384,128]{1,0:T(8,128)(2,1)S(1)} %core_pack.1), channel_id=1, source_target_pairs={{0,64},{64,0},{128,192},{192,128},{1,65},{65,1},{129,193},{193,129... | collective-permute-start | bytes 294920 | tf_op jit(solution)/shard_map/ppermute | solution.py:653
  13.9 4.4 %copy-start.6 = (bf16[3072,256]{1,0:T(8,128)(2,1)S(1)}, bf16[3072,256]{1,0:T(8,128)(2,1)}, u32[]{:S(2)}) copy-start(bf16[3072,256]{1,0:T(8,128)(2,1)} %constant.11.clone.samples) | copy-start | bytes 4718596
  13.9 4.4 %copy-start.7 = (bf16[384,768]{1,0:T(8,128)(2,1)S(1)}, bf16[384,768]{1,0:T(8,128)(2,1)}, u32[]{:S(2)}) copy-start(bf16[384,768]{1,0:T(8,128)(2,1)} %constant.9.clone.lines) | copy-start | bytes 1769476
  13.9 4.4 %copy-start.8 = (bf16[768,256]{1,0:T(8,128)(2,1)S(1)}, bf16[768,256]{1,0:T(8,128)(2,1)}, u32[]{:S(2)}) copy-start(bf16[768,256]{1,0:T(8,128)(2,1)} %constant.8.clone.forward) | copy-start | bytes 1179652
  13.9 4.4 %copy-start.9 = (bf16[128,384]{1,0:T(8,128)(2,1)S(1)}, bf16[128,384]{1,0:T(8,128)(2,1)}, u32[]{:S(2)}) copy-start(bf16[128,384]{1,0:T(8,128)(2,1)} %constant.10.clone.inverse) | copy-start | bytes 294916
  15.4 5.7 %collective-permute-start.6 = (bf16[176,128]{1,0:T(8,128)(2,1)S(1)}, bf16[176,128]{1,0:T(8,128)(2,1)S(1)}, u32[]{:S(2)}, u32[]{:S(2)}) collective-permute-start(bf16[176,128]{1,0:T(8,128)(2,1)S(1)} %get-tuple-element.29), channel_id=1, source_target_pairs={{0,1},{1,0},{2,3},{3,2},{4,5},{5,4},{6,7},{7,6},{8,9},{9,8},{10,11... | collective-permute-start | bytes 135176 | tf_op jit(solution)/shard_map/ppermute | solution.py:635
  15.9 5.2 %collective-permute-start.7 = (bf16[176,128]{1,0:T(8,128)(2,1)S(1)}, bf16[176,128]{1,0:T(8,128)(2,1)S(1)}, u32[]{:S(2)}, u32[]{:S(2)}) collective-permute-start(bf16[176,128]{1,0:T(8,128)(2,1)S(1)} %get-tuple-element.30), channel_id=1, source_target_pairs={{0,64},{1,2},{2,1},{3,67},{64,0},{65,66},{66,65},{67,3},{128,192},... | collective-permute-start | bytes 135176 | tf_op jit(solution)/shard_map/ppermute | solution.py:636
